TPU v7x, 32 devices: a whole 2x2x4 slice. The times are simulated.
32 devices in a mesh: rep: 4 (over y, x), fsdp: 8 (over z, core).
Axes of the slice: x: 2, y: 2, z: 4, core: 2. Of those that a mesh axis runs over, the one named last changes fastest.
Arguments:
- block_input: bfloat16 [4096, 4096], P(('rep', 'fsdp')), may hold values from -6 to 6
- ssd_input: bfloat16 [4096, 4096], P(('rep', 'fsdp')), may hold values from -6 to 6
- out_grad: bfloat16 [4096, 4096], P(('rep', 'fsdp')), may hold values from -0.29882812 to 0.29882812
- start_state: bfloat16 [32, 64, 4096], P(('rep', 'fsdp')), may hold values from -12 to 12
- step_bias: float32 [64], replicated, may hold values from -1 to 1
- decay_log: float32 [64], replicated, may hold values from -7 to -2.5
- local_params: float32 [4, 192, 4096], P('rep', 'fsdp'), may hold values from -0.09375 to 0.09375
- global_params: float32 [192, 4096], P('fsdp'), may hold values from -0.75 to 0.75
- momentum: float32 [192, 4096], P('fsdp'), may hold values from -3 to 3
Outputs:
- block_grad: bfloat16 [4096, 4096], P(('rep', 'fsdp'))
- new_params: float32 [192, 4096], P('fsdp')
- new_momentum: float32 [192, 4096], P('fsdp')
All inputs are finite; a program needn't handle non-finite values.
Results may differ from a plain program's by a relative error of at most 0.012.
Values may be sent and summed in bfloat16 or wider, within the bound.
No kernel may reach another device: no remote copies, remote signals or barrier semaphores. Data moves between devices by JAX's collectives and lax.ppermute only.
A program may use at most 64 MiB of HBM per device.

v0:
```python
import functools

import jax
import jax.numpy as jnp
from jax import lax
from jax.experimental import pallas as pl
from jax.experimental.pallas import tpu as pltpu
from jax.sharding import PartitionSpec as P

STATE = 64
LOG2E = 1.4426950408889634

inner_rate = 0.002
outer_rate = 0.7
momentum_decay = 0.9

VMEM_LIMIT = 48 * 1024 * 1024


def params(**more):
    return pltpu.CompilerParams(vmem_limit_bytes=VMEM_LIMIT, **more)


def whole_vmem(count):
    return [pl.BlockSpec(memory_space=pltpu.VMEM)] * count


def contract(left, right, dims):
    return lax.dot_general(left, right, (dims, ((), ())), preferred_element_type=jnp.float32)


def terms(value, count):
    out = []
    for _ in range(count):
        out.append(value.astype(jnp.bfloat16))
        value = value - out[-1].astype(jnp.float32)
    return out


def early_kernel(cot_ref, val_ref, state_ref, cross_ref, enter_ref):
    block = cot_ref.shape[0]
    lanes = lax.broadcasted_iota(jnp.int32, (block, 2 * STATE), 1)
    rows = lax.broadcasted_iota(jnp.int32, (block, block), 0)
    cols = lax.broadcasted_iota(jnp.int32, (block, block), 1)
    causal = rows >= cols
    low = lanes < STATE
    square = (2 * STATE, 2 * STATE)
    same_head = (lax.broadcasted_iota(jnp.int32, square, 0) < STATE) == (
        lax.broadcasted_iota(jnp.int32, square, 1) < STATE
    )
    for pair in range(cot_ref.shape[1] // (2 * STATE)):
        span = slice(pair * 2 * STATE, (pair + 1) * 2 * STATE)
        cot = cot_ref[:, span]
        val = val_ref[:, span]
        zero = jnp.zeros_like(cot)
        for odd in range(2):
            one = jnp.where(low, zero, cot) if odd else jnp.where(low, cot, zero)
            cross = contract(one, val, ((1,), (1,)))
            cross_ref[2 * pair + odd] = jnp.where(causal, cross, 0.0).astype(cross_ref.dtype)
        state = state_ref[span, :]
        wide = jnp.concatenate([state, state], axis=1)
        wide = jnp.where(same_head, wide, jnp.zeros_like(wide))
        enter_ref[:, span] = contract(cot, wide, ((1,), (0,)))


def early_products(out_grad, ssd_input, state, part, width):
    block = out_grad.shape[0]
    heads = width // STATE
    steps = 4
    piece = width // steps
    return pl.pallas_call(
        early_kernel,
        grid=(steps,),
        in_specs=[
            pl.BlockSpec((block, piece), lambda i: (0, part * steps + i)),
            pl.BlockSpec((block, piece), lambda i: (0, part * steps + i)),
            pl.BlockSpec((piece, STATE), lambda i: (part * steps + i, 0)),
        ],
        out_specs=[
            pl.BlockSpec((heads // steps, block, block), lambda i: (i, 0, 0)),
            pl.BlockSpec((block, piece), lambda i: (0, i)),
        ],
        out_shape=[
            jax.ShapeDtypeStruct((heads, block, block), jnp.bfloat16),
            jax.ShapeDtypeStruct((block, width), jnp.float32),
        ],
        compiler_params=params(),
        cost_estimate=pl.CostEstimate(
            flops=2 * block * width * 4 * block, bytes_accessed=8 * block * width, transcendentals=0
        ),
        name="early_products",
    )(out_grad, ssd_input, state)


def stacked(refs):
    if len(refs) == 1:
        return refs[0][...]
    return jnp.concatenate([r[...].astype(jnp.float32) for r in refs], axis=0).astype(jnp.bfloat16)


def shard_rows(index, k, rows):
    return pl.ds(pl.multiple_of((index ^ k) * rows, 8), rows)


def ssd_kernel(order, where_ref, rows_ref, bias_ref, decay_ref, *rest):
    shards = len(order)
    cross_refs, enter_refs, rest = rest[:2], rest[2:4], rest[4:]
    weight_refs = rest[:shards]
    grad_ref, mine_ref, other_ref, proj_ref, col_ref, out_ref = rest[shards:]
    block = rows_ref.shape[0]
    heads = bias_ref.shape[1]
    per = weight_refs[0].shape[0]
    arrived = contract(stacked(weight_refs), rows_ref[...], ((1,), (1,)))
    for at, k in enumerate(order):
        if shards > 1:
            proj_ref[shard_rows(where_ref[1], k, per), :] = arrived[at * per : (at + 1) * per]
        else:
            proj_ref[...] = arrived
    key_t = proj_ref[:STATE, :]
    query_t = proj_ref[STATE : 2 * STATE, :]
    bias_t = jnp.broadcast_to(bias_ref[...], (block, heads)).T
    rate = jnp.exp(jnp.broadcast_to(decay_ref[...], (block, heads)).T)
    raw = proj_ref[2 * STATE :, :] + bias_t
    step_t = jnp.maximum(raw, 0.0) + jnp.log1p(jnp.exp(-jnp.abs(raw)))
    up = lax.broadcasted_iota(jnp.int32, (block, block), 0)
    across = lax.broadcasted_iota(jnp.int32, (block, block), 1)
    before = jnp.where(up <= across, 1.0, 0.0).astype(jnp.bfloat16)
    after = jnp.where(up >= across, 1.0, 0.0).astype(jnp.bfloat16)
    cum_t = LOG2E * contract(
        jnp.concatenate(terms(-step_t * rate, 3), axis=1),
        jnp.concatenate([before] * 3, axis=0),
        ((1,), (0,)),
    )
    cum = cum_t.T
    step = step_t.T
    query = query_t.T
    query_high, query_low = terms(query, 2)
    key_high, key_low = terms(key_t, 2)
    scores = contract(
        jnp.concatenate([query_high, query_high, query_low], axis=1),
        jnp.concatenate([key_high, key_low, key_high], axis=0),
        ((1,), (0,)),
    )
    entered = jnp.exp2(cum)
    query_twice = jnp.concatenate([query, query], axis=1)
    low = lax.broadcasted_iota(jnp.int32, (block, 2 * STATE), 1) < STATE
    head_of = lax.broadcasted_iota(jnp.int32, (block, heads), 1)
    below = lax.broadcasted_iota(jnp.int32, (block, heads), 0) < STATE

    score_grad = jnp.zeros((block, block), jnp.float32)
    query_grad = jnp.zeros((block, 2 * STATE), jnp.float32)
    row_sums = jnp.zeros((block, heads), jnp.float32)
    for h0 in range(0, heads, 4):
        left, right = [], []
        for h in range(h0, h0 + 4):
            span = cum[:, h : h + 1] - cum_t[h : h + 1, :]
            cross = cross_refs[2 * h // heads][h % (heads // 2)]
            weight = cross.astype(jnp.float32) * jnp.exp2(jnp.minimum(span, 0.0))
            score_grad = score_grad + weight * step_t[h : h + 1, :]
            mixed = weight * scores
            col_ref[h : h + 1, :] = jnp.sum(mixed, axis=0, keepdims=True)
            left.append(mixed.astype(jnp.bfloat16))
            right.append(jnp.where(head_of == h, step, 0.0).astype(jnp.bfloat16))
        for h in range(h0, h0 + 4, 2):
            gain = jnp.where(low, entered[:, h : h + 1], entered[:, h + 1 : h + 2])
            at = h % (heads // 2) * STATE
            part = enter_refs[2 * h // heads][:, at : at + 2 * STATE] * gain
            query_grad = query_grad + part
            left.append((part * query_twice).astype(jnp.bfloat16))
            right.append(
                jnp.where(head_of == jnp.where(below, h, h + 1), 1.0, 0.0).astype(jnp.bfloat16)
            )
        row_sums = row_sums + contract(
            jnp.concatenate(left, axis=1), jnp.concatenate(right, axis=0), ((1,), (0,))
        )

    cols_t = col_ref[...]
    cum_grad = row_sums.T - step_t * cols_t
    later = contract(
        jnp.concatenate(terms(cum_grad, 2), axis=1),
        jnp.concatenate([after] * 2, axis=0),
        ((1,), (0,)),
    )
    step_grad = cols_t - rate * later
    raw_grad = step_grad / (1.0 + jnp.exp(-raw))
    score_grad = score_grad.astype(jnp.bfloat16)
    out_ref[:STATE, :] = contract(query_t.astype(jnp.bfloat16), score_grad, ((1,), (0,)))
    query_all = (query_grad[:, :STATE] + query_grad[:, STATE:]).T
    out_ref[STATE : 2 * STATE, :] = query_all + contract(key_high, score_grad, ((1,), (1,)))
    out_ref[2 * STATE :, :] = raw_grad
    if shards == 1:
        grad_ref[...] = out_ref[...].astype(jnp.bfloat16)
        mine_ref[...] = jnp.zeros_like(mine_ref)
        other_ref[...] = jnp.zeros_like(other_ref)
        return
    core = where_ref[1] % 2
    for part, ref in ((core, mine_ref), (1 - core, other_ref)):
        of_core = [out_ref[shard_rows(f + part, 0, per), :] for f in range(0, shards, 2)]
        ref[...] = jnp.concatenate(of_core, axis=0).astype(jnp.bfloat16)
    for at, k in enumerate(order):
        proj_ref[at * per : (at + 1) * per, :] = out_ref[shard_rows(where_ref[1], k, per), :]
    grad_ref[...] = proj_ref[...].astype(jnp.bfloat16)


def ssd_backward(where, rows_in, step_bias, decay_log, cross, enter, weights, order):
    block = rows_in.shape[0]
    heads = step_bias.shape[0]
    cols = sum(w.shape[0] for w in weights)
    half = (cols // 2, block)
    return pl.pallas_call(
        functools.partial(ssd_kernel, order),
        in_specs=[pl.BlockSpec(memory_space=pltpu.SMEM)] + whole_vmem(7 + len(order)),
        out_specs=whole_vmem(3),
        out_shape=[
            jax.ShapeDtypeStruct((cols, block), jnp.bfloat16),
            jax.ShapeDtypeStruct(half, jnp.bfloat16),
            jax.ShapeDtypeStruct(half, jnp.bfloat16),
        ],
        scratch_shapes=[
            pltpu.VMEM((cols, block), jnp.float32),
            pltpu.VMEM((heads, block), jnp.float32),
            pltpu.VMEM((cols, block), jnp.float32),
        ],
        compiler_params=params(),
        cost_estimate=pl.CostEstimate(
            flops=2 * block * cols * rows_in.shape[1],
            bytes_accessed=16 * rows_in.size,
            transcendentals=heads * block * block,
        ),
        name="ssd_backward",
    )(where, rows_in, step_bias.reshape(1, -1), decay_log.reshape(1, -1), *cross, *enter, *weights)


def block_grad_kernel(grad_ref, *refs):
    out_ref = refs[-1]
    weights = stacked(refs[:-1])
    out_ref[...] = contract(grad_ref[...].T, weights, ((1,), (0,))).astype(out_ref.dtype)


def block_gradient(grad, weights):
    depth = weights[0].shape[1]
    cols, block = grad.shape
    return pl.pallas_call(
        block_grad_kernel,
        in_specs=whole_vmem(1 + len(weights)),
        out_specs=pl.BlockSpec(memory_space=pltpu.VMEM),
        out_shape=jax.ShapeDtypeStruct((block, depth), jnp.bfloat16),
        compiler_params=params(),
        cost_estimate=pl.CostEstimate(
            flops=2 * block * cols * depth, bytes_accessed=4 * cols * depth, transcendentals=0
        ),
        name="block_gradient",
    )(grad, *weights)


def pieces_kernel(where_ref, rows_ref, own_ref, *outs):
    block = rows_ref.shape[0]
    width = outs[0].shape[1]
    for k, out in enumerate(outs):
        cols = pl.ds(pl.multiple_of((where_ref[0] ^ k) * width, 128), width)
        out[:block, :] = rows_ref[:, cols]
        out[block:, :] = own_ref[:, cols]


def column_pieces(where, rows_in, own, replicas):
    tokens, depth = rows_in.shape
    shape = (tokens + own.shape[0], depth // replicas)
    return pl.pallas_call(
        pieces_kernel,
        in_specs=[pl.BlockSpec(memory_space=pltpu.SMEM)] + whole_vmem(2),
        out_specs=whole_vmem(replicas),
        out_shape=[jax.ShapeDtypeStruct(shape, jnp.bfloat16)] * replicas,
        compiler_params=params(),
        name="column_pieces",
    )(where, rows_in, own)


def slice_kernel(replicas, where_ref, *refs):
    grads, pieces, refs = refs[:replicas], refs[replicas : 2 * replicas], refs[2 * replicas :]
    twin, outs, total = refs[0], refs[1:-1], refs[-1]
    tokens = twin.shape[0] // replicas
    rows = total.shape[0]
    left, right = [], []
    for other in range(2):
        for k in range(replicas):
            left.append(grads[k][other * rows : (other + 1) * rows, :])
            right.append(
                twin[k * tokens : (k + 1) * tokens, :] if other else pieces[k][:tokens, :]
            )
    total[...] = contract(
        jnp.concatenate(left, axis=1), jnp.concatenate(right, axis=0), ((1,), (0,))
    )
    per = outs[0].shape[0]
    chip = where_ref[1] // 2
    for k, out in enumerate(outs):
        out[...] = total[shard_rows(chip, k, per), :].astype(jnp.bfloat16)


def gradient_slice(where, grads, pieces, twin, chips):
    rows = grads[0].shape[0] // (2 * chips)
    width = twin.shape[1]
    return pl.pallas_call(
        functools.partial(slice_kernel, len(pieces)),
        in_specs=[pl.BlockSpec(memory_space=pltpu.SMEM)] + whole_vmem(1 + 2 * len(pieces)),
        out_specs=whole_vmem(chips),
        out_shape=[jax.ShapeDtypeStruct((rows, width), jnp.bfloat16)] * chips,
        scratch_shapes=[pltpu.VMEM((rows * chips, width), jnp.float32)],
        compiler_params=params(),
        name="gradient_slice",
    )(where, *grads, *pieces, twin)


def stepped_kernel(chips, *refs):
    sums, pieces, out_ref = refs[:chips], refs[chips:-1], refs[-1]
    rows = out_ref.shape[0]
    total = sums[0][...].astype(jnp.float32)
    for part in sums[1:]:
        total = total + part[...].astype(jnp.float32)
    level = pieces[0][-rows:, :].astype(jnp.float32)
    for piece in pieces[1:]:
        level = level + piece[-rows:, :].astype(jnp.float32)
    mean = (level - inner_rate * total) * (1.0 / len(pieces))
    out_ref[...] = mean.astype(jnp.bfloat16)


def stepped_slice(sums, pieces):
    return pl.pallas_call(
        functools.partial(stepped_kernel, len(sums)),
        in_specs=whole_vmem(len(sums) + len(pieces)),
        out_specs=pl.BlockSpec(memory_space=pltpu.VMEM),
        out_shape=jax.ShapeDtypeStruct(sums[0].shape, jnp.bfloat16),
        compiler_params=params(),
        name="stepped_slice",
    )(*sums, *pieces)


def outer_kernel(where_ref, par_ref, mom_ref, *refs):
    stepped, (new_par, new_mom) = refs[:-2], refs[-2:]
    width = stepped[0].shape[1]
    for k, part in enumerate(stepped):
        cols = pl.ds(pl.multiple_of((where_ref[0] ^ k) * width, 128), width)
        old = par_ref[:, cols]
        pseudo = old - part[...].astype(jnp.float32)
        fresh = momentum_decay * mom_ref[:, cols] + pseudo
        new_mom[:, cols] = fresh
        new_par[:, cols] = old - outer_rate * (pseudo + momentum_decay * fresh)


def outer_step(where, global_params, momentum, stepped):
    return pl.pallas_call(
        outer_kernel,
        in_specs=[pl.BlockSpec(memory_space=pltpu.SMEM)] + whole_vmem(2 + len(stepped)),
        out_specs=whole_vmem(2),
        out_shape=[jax.ShapeDtypeStruct(global_params.shape, jnp.float32)] * 2,
        compiler_params=params(),
        name="outer_step",
    )(where, global_params, momentum, *stepped)


def on_device(
    sizes,
    block_input,
    ssd_input,
    out_grad,
    start_state,
    step_bias,
    decay_log,
    local_params,
    global_params,
    momentum,
):
    replicas, chips, cores = sizes
    local_rows = local_params[0]
    rows, depth = local_rows.shape
    own = local_rows.astype(jnp.bfloat16)
    seq_width = ssd_input.shape[1]
    blocks = start_state.shape[0]
    block = block_input.shape[0] // blocks
    fast = (
        cores == 2
        and chips == 4
        and rows % 8 == 0
        and replicas & (replicas - 1) == 0
        and depth % (128 * replicas) == 0
    )
    rep = lax.axis_index("rep")
    spot = lax.axis_index("line") * cores + lax.axis_index("core")
    where = jnp.stack([rep, spot]).astype(jnp.int32)

    def send(value, axis, k):
        count = dict(rep=replicas, line=chips, core=cores)[axis]
        return lax.ppermute(value, axis, [(i, i ^ k) for i in range(count)])

    if fast:
        near = send(own, "line", 1)
        far = send(own, "line", 3)
        order = (0, 2, 6, 4, 1, 3, 7, 5)
    else:
        weights = [lax.all_gather(own, ("line", "core"), axis=0, tiled=True)]
        order = (0,)

    early = [[], []]
    states = [start_state[b].reshape(seq_width, STATE) for b in range(blocks)]
    states, own_late = lax.optimization_barrier((states, own))
    for b in range(blocks):
        seq = slice(b * block, (b + 1) * block)
        for half in range(2):
            early[half].append(
                early_products(out_grad[seq], ssd_input[seq], states[b], half, seq_width // 2)
            )
    if fast:
        pieces = column_pieces(where, block_input, own_late, replicas)
        far, _ = lax.optimization_barrier((far, pieces))
        pieces = [pieces[0]] + [send(pieces[k], "rep", k) for k in range(1, replicas)]
        middle = send(far, "line", 1)
        twins = [send(own, "core", 1), send(near, "core", 1)]
        middle, early, twins = lax.optimization_barrier((middle, early, twins))
        twins = twins + [send(far, "core", 1), send(middle, "core", 1)]
        weights = [own, near, far, middle] + twins

    grads, mine, other = [], [], []
    for b in range(blocks):
        seq = slice(b * block, (b + 1) * block)
        parts = ssd_backward(
            where,
            block_input[seq],
            step_bias,
            decay_log,
            [early[0][b][0], early[1][b][0]],
            [early[0][b][1], early[1][b][1]],
            weights,
            order,
        )
        for kept, part in zip((grads, mine, other), parts):
            kept.append(part)
    grad, mine, other = (
        kept[0] if blocks == 1 else jnp.concatenate(kept, axis=1) for kept in (grads, mine, other)
    )
    block_grad = block_gradient(grad, weights)

    if not fast:
        gradient = lax.psum_scatter(
            contract(grad, block_input, ((1,), (0,))),
            ("line", "core"),
            scatter_dimension=0,
            tiled=True,
        )
        pseudo = global_params - (local_rows - inner_rate * gradient)
        mean_pseudo = lax.psum(pseudo.astype(jnp.bfloat16), "rep").astype(jnp.float32) / replicas
        new_momentum = momentum_decay * momentum + mean_pseudo
        new_params = global_params - outer_rate * (mean_pseudo + momentum_decay * new_momentum)
        return (block_grad, new_params, new_momentum)

    tokens = blocks * block
    mine, pieces = lax.optimization_barrier((mine, pieces))
    twin = send(jnp.concatenate([p[:tokens] for p in pieces], axis=0), "core", 1)

    both = jnp.concatenate([mine, send(other, "core", 1)], axis=0)
    plane = [both] + [send(both, "rep", k) for k in range(1, replicas)]
    sums = gradient_slice(where, plane, pieces, twin, chips)
    sums = [sums[0]] + [send(sums[k], "line", k) for k in range(1, chips)]
    stepped = stepped_slice(sums, pieces)
    stepped = [stepped] + [send(stepped, "rep", k) for k in range(1, replicas)]
    new_params, new_momentum = outer_step(where, global_params, momentum, stepped)
    return (block_grad, new_params, new_momentum)


def solution(mesh):
    replicas, shards = mesh.shape["rep"], mesh.shape["fsdp"]
    cores = 2 if shards % 2 == 0 else 1
    sizes = (replicas, shards // cores, cores)
    apart = jax.sharding.Mesh(mesh.devices.reshape(sizes), ("rep", "line", "core"))
    fsdp = ("line", "core")
    rows = P(("rep", "line", "core"), None)
    placed = (
        rows,
        rows,
        rows,
        P(("rep", "line", "core"), None, None),
        P(),
        P(),
        P("rep", fsdp, None),
        P(fsdp, None),
        P(fsdp, None),
    )
    return jax.shard_map(
        functools.partial(on_device, sizes),
        mesh=apart,
        in_specs=placed,
        out_specs=(rows, P(fsdp, None), P(fsdp, None)),
        check_vma=False,
    )
```

profile of v0, /device:TPU:0, one launch (start us, length us, event | category | flops | bytes accessed | tf_op | source)
XLA Modules:
  0.0 61.9 jit_solution(18216703792675852681)
XLA Ops:
  0.6 1.0 %convert_bitcast_fusion.own_ref.rest_4_.refs_0_ = bf16[24,4096]{1,0:T(8,128)(2,1)S(1)} fusion(f32[1,24,4096]{2,1,0:T(8,128)} %param.15), kind=kLoop, calls=%fused_computation.1 | loop fusion | flops 98304 | bytes 589824 | tf_op jit(solution)/shard_map/convert_element_type | solution.py:375
  1.6 5.1 %collective-permute-start = (bf16[24,4096]{1,0:T(8,128)(2,1)S(1)}, bf16[24,4096]{1,0:T(8,128)(2,1)S(1)}, u32[]{:S(2)}, u32[]{:S(2)}) collective-permute-start(bf16[24,4096]{1,0:T(8,128)(2,1)S(1)} %convert_bitcast_fusion.own_ref.rest_4_.refs_0_), channel_id=1, source_target_pairs={{0,6},{2,4},{4,2},{6,0},{1,7},{3,5},{5,3},{7,1},{8,14},{10,12},{12... | collective-permute-start | bytes 589832 | tf_op jit(solution)/shard_map/ppermute | solution.py:392
  6.8 2.2 %reshape_squeeze.3.state_ref = bf16[4096,64]{1,0:T(8,128)(2,1)S(1)} reshape(bf16[1,64,4096]{2,1,0:T(8,128)(2,1)} %param.12) | data formatting | bytes 1048576 | tf_op jit(solution)/shard_map/reshape;squeeze | solution.py:403
  9.1 1.2 %copy-done.2 = bf16[128,4096]{1,0:T(8,128)(2,1)S(1)} copy-done((bf16[128,4096]{1,0:T(8,128)(2,1)S(1)}, bf16[128,4096]{1,0:T(8,128)(2,1)}, u32[]{:S(2)}) %copy-start.2) | copy-done | bytes 1048600
  10.3 0.6 %column_pieces.1 = (bf16[152,1024]{1,0:T(8,128)(2,1)S(1)}, bf16[152,1024]{1,0:T(8,128)(2,1)S(1)}, bf16[152,1024]{1,0:T(8,128)(2,1)S(1)}, bf16[152,1024]{1,0:T(8,128)(2,1)S(1)}) custom-call(s32[2]{0:T(128)S(1)} %pad_add_fusion.where_ref, bf16[128,4096]{1,0:T(8,128)(2,1)S(1)} %copy-done.2, bf16[24,4096]{1,0:T(8,128)(2,1)S(1)} %convert_bitcast_fusion.own_ref.rest_4_.refs_0_), custom_call_target="tpu_custom_call" | custom-call | tf_op jit(solution)/shard_map/column_pieces/pallas_call | solution.py:268
  10.9 1.6 %collective-permute-done.rest_6_.refs_2_ = bf16[24,4096]{1,0:T(8,128)(2,1)S(1)} collective-permute-done((bf16[24,4096]{1,0:T(8,128)(2,1)S(1)}, bf16[24,4096]{1,0:T(8,128)(2,1)S(1)}, u32[]{:S(2)}, u32[]{:S(2)}) %collective-permute-start) | collective-permute-done | bytes 196640 | tf_op jit(solution)/shard_map/ppermute | solution.py:392
  12.5 3.1 %collective-permute-start.1 = (bf16[24,4096]{1,0:T(8,128)(2,1)S(1)}, bf16[24,4096]{1,0:T(8,128)(2,1)S(1)}, u32[]{:S(2)}, u32[]{:S(2)}) collective-permute-start(bf16[24,4096]{1,0:T(8,128)(2,1)S(1)} %collective-permute-done.rest_6_.refs_2_), channel_id=1, source_target_pairs={{0,2},{2,0},{4,6},{6,4},{1,3},{3,1},{5,7},{7,5},{8,10},{10,8},{12,... | collective-permute-start | bytes 589832 | tf_op jit(solution)/shard_map/ppermute | solution.py:392
  16.2 1.5 %collective-permute-start.7 = (bf16[152,1024]{1,0:T(8,128)(2,1)S(1)}, bf16[152,1024]{1,0:T(8,128)(2,1)S(1)}, u32[]{:S(2)}, u32[]{:S(2)}) collective-permute-start(bf16[152,1024]{1,0:T(8,128)(2,1)S(1)} %get-tuple-element.37), channel_id=1, source_target_pairs={{0,8},{8,0},{16,24},{24,16},{1,9},{9,1},{17,25},{25,17},{2,10},{10... | collective-permute-start | bytes 933896 | tf_op jit(solution)/shard_map/ppermute | solution.py:392
  17.7 1.5 %collective-permute-start.8 = (bf16[152,1024]{1,0:T(8,128)(2,1)S(1)}, bf16[152,1024]{1,0:T(8,128)(2,1)S(1)}, u32[]{:S(2)}, u32[]{:S(2)}) collective-permute-start(bf16[152,1024]{1,0:T(8,128)(2,1)S(1)} %get-tuple-element.38), channel_id=1, source_target_pairs={{0,16},{8,24},{16,0},{24,8},{1,17},{9,25},{17,1},{25,9},{2,18},{10... | collective-permute-start | bytes 933896 | tf_op jit(solution)/shard_map/ppermute | solution.py:392
  19.7 1.7 %early_products.2 = (bf16[32,128,128]{2,1,0:T(8,128)(2,1)S(1)}, f32[128,2048]{1,0:T(8,128)S(1)}) custom-call(bf16[128,4096]{1,0:T(8,128)(2,1)S(1)} %copy-done, bf16[128,4096]{1,0:T(8,128)(2,1)S(1)} %copy-done.1, bf16[4096,64]{1,0:T(8,128)(2,1)S(1)} %reshape_squeeze.3.state_ref), custom_call_target="tpu_custom_call" | custom-call | flops 268435456 | bytes 2097152 | tf_op jit(solution)/shard_map/early_products/pallas_call | solution.py:71
  21.4 1.7 %early_products.3 = (bf16[32,128,128]{2,1,0:T(8,128)(2,1)S(1)}, f32[128,2048]{1,0:T(8,128)S(1)}) custom-call(bf16[128,4096]{1,0:T(8,128)(2,1)S(1)} %copy-done, bf16[128,4096]{1,0:T(8,128)(2,1)S(1)} %copy-done.1, bf16[4096,64]{1,0:T(8,128)(2,1)S(1)} %reshape_squeeze.3.state_ref), custom_call_target="tpu_custom_call" | custom-call | flops 268435456 | bytes 2097152 | tf_op jit(solution)/shard_map/early_products/pallas_call | solution.py:71
  23.1 1.0 %copy-done.4 = f32[128,2048]{1,0:T(8,128)} copy-done((f32[128,2048]{1,0:T(8,128)}, f32[128,2048]{1,0:T(8,128)S(1)}, u32[]{:S(2)}) %copy-start.4) | copy-done | bytes 1048600
  24.6 0.9 %collective-permute-done.5.rest_10_.refs_6_ = bf16[24,4096]{1,0:T(8,128)(2,1)S(1)} collective-permute-done((bf16[24,4096]{1,0:T(8,128)(2,1)S(1)}, bf16[24,4096]{1,0:T(8,128)(2,1)S(1)}, u32[]{:S(2)}, u32[]{:S(2)}) %collective-permute-start.5) | collective-permute-done | bytes 196640 | tf_op jit(solution)/shard_map/ppermute | solution.py:392
  25.8 6.0 %ssd_backward.1 = (bf16[192,128]{1,0:T(8,128)(2,1)S(1)}, bf16[96,128]{1,0:T(8,128)(2,1)S(1)}, bf16[96,128]{1,0:T(8,128)(2,1)S(1)}) custom-call(s32[2]{0:T(128)S(1)} %pad_add_fusion.where_ref, bf16[128,4096]{1,0:T(8,128)(2,1)S(1)} %copy-done.3, f32[1,64]{1,0:T(1,128)S(1)} %bitcast.6, f32[1,64]{1,0:T(1,128)S(1)} %bitcast.7, ...), custom_call_target="tpu_custom_call" | custom-call | flops 201326592 | bytes 8388608 | tf_op jit(solution)/shard_map/ssd_backward/pallas_call | solution.py:210
  31.8 2.1 %collective-permute-done.8.refs_6_ = bf16[152,1024]{1,0:T(8,128)(2,1)S(1)} collective-permute-done((bf16[152,1024]{1,0:T(8,128)(2,1)S(1)}, bf16[152,1024]{1,0:T(8,128)(2,1)S(1)}, u32[]{:S(2)}, u32[]{:S(2)}) %collective-permute-start.8) | collective-permute-done | bytes 311328 | tf_op jit(solution)/shard_map/ppermute | solution.py:392
  34.6 2.2 %collective-permute-done.10 = bf16[96,128]{1,0:T(8,128)(2,1)S(1)} collective-permute-done((bf16[96,128]{1,0:T(8,128)(2,1)S(1)}, bf16[96,128]{1,0:T(8,128)(2,1)S(1)}, u32[]{:S(2)}, u32[]{:S(2)}) %collective-permute-start.10) | collective-permute-done | bytes 24608 | tf_op jit(solution)/shard_map/ppermute | solution.py:392
  36.8 1.2 %collective-permute-start.11 = (bf16[192,128]{1,0:T(8,128)(2,1)S(1)}, bf16[192,128]{1,0:T(8,128)(2,1)S(1)}, u32[]{:S(2)}, u32[]{:S(2)}) collective-permute-start(bf16[192,128]{1,0:T(8,128)(2,1)S(1)} %constant_dynamic-update-slice_fusion.refs_0_), channel_id=1, source_target_pairs={{0,8},{8,0},{16,24},{24,16},{1,9},{9,1},{17,25},{25,17},{2,10},{10... | collective-permute-start | bytes 147464 | tf_op jit(solution)/shard_map/ppermute | solution.py:392
  38.0 0.8 %collective-permute-start.12 = (bf16[192,128]{1,0:T(8,128)(2,1)S(1)}, bf16[192,128]{1,0:T(8,128)(2,1)S(1)}, u32[]{:S(2)}, u32[]{:S(2)}) collective-permute-start(bf16[192,128]{1,0:T(8,128)(2,1)S(1)} %constant_dynamic-update-slice_fusion.refs_0_), channel_id=1, source_target_pairs={{0,16},{8,24},{16,0},{24,8},{1,17},{9,25},{17,1},{25,9},{2,18},{10... | collective-permute-start | bytes 147464 | tf_op jit(solution)/shard_map/ppermute | solution.py:392
  38.8 1.4 %collective-permute-start.13 = (bf16[192,128]{1,0:T(8,128)(2,1)S(1)}, bf16[192,128]{1,0:T(8,128)(2,1)S(1)}, u32[]{:S(2)}, u32[]{:S(2)}) collective-permute-start(bf16[192,128]{1,0:T(8,128)(2,1)S(1)} %constant_dynamic-update-slice_fusion.refs_0_), channel_id=1, source_target_pairs={{0,24},{8,16},{16,8},{24,0},{1,25},{9,17},{17,9},{25,1},{2,26},{10... | collective-permute-start | bytes 147464 | tf_op jit(solution)/shard_map/ppermute | solution.py:392
  40.9 1.8 %collective-permute-done.12.refs_2_ = bf16[192,128]{1,0:T(8,128)(2,1)S(1)} collective-permute-done((bf16[192,128]{1,0:T(8,128)(2,1)S(1)}, bf16[192,128]{1,0:T(8,128)(2,1)S(1)}, u32[]{:S(2)}, u32[]{:S(2)}) %collective-permute-start.12) | collective-permute-done | bytes 49184 | tf_op jit(solution)/shard_map/ppermute | solution.py:392
  42.6 1.2 %collective-permute-done.13.refs_3_ = bf16[192,128]{1,0:T(8,128)(2,1)S(1)} collective-permute-done((bf16[192,128]{1,0:T(8,128)(2,1)S(1)}, bf16[192,128]{1,0:T(8,128)(2,1)S(1)}, u32[]{:S(2)}, u32[]{:S(2)}) %collective-permute-start.13) | collective-permute-done | bytes 49184 | tf_op jit(solution)/shard_map/ppermute | solution.py:392
  43.8 1.0 %gradient_slice.1 = (bf16[24,1024]{1,0:T(8,128)(2,1)S(1)}, bf16[24,1024]{1,0:T(8,128)(2,1)S(1)}, bf16[24,1024]{1,0:T(8,128)(2,1)S(1)}, bf16[24,1024]{1,0:T(8,128)(2,1)S(1)}) custom-call(s32[2]{0:T(128)S(1)} %pad_add_fusion.where_ref, bf16[192,128]{1,0:T(8,128)(2,1)S(1)} %constant_dynamic-update-slice_fusion.refs_0_, ...), custom_call_target="tpu_custom_call" | custom-call | tf_op jit(solution)/shard_map/gradient_slice/pallas_call | solution.py:302
  44.9 1.8 %collective-permute-start.15 = (bf16[24,1024]{1,0:T(8,128)(2,1)S(1)}, bf16[24,1024]{1,0:T(8,128)(2,1)S(1)}, u32[]{:S(2)}, u32[]{:S(2)}) collective-permute-start(bf16[24,1024]{1,0:T(8,128)(2,1)S(1)} %get-tuple-element.62), channel_id=1, source_target_pairs={{0,2},{2,0},{4,6},{6,4},{1,3},{3,1},{5,7},{7,5},{8,10},{10,8},{12,... | collective-permute-start | bytes 147464 | tf_op jit(solution)/shard_map/ppermute | solution.py:392
  46.7 0.7 %collective-permute-start.16 = (bf16[24,1024]{1,0:T(8,128)(2,1)S(1)}, bf16[24,1024]{1,0:T(8,128)(2,1)S(1)}, u32[]{:S(2)}, u32[]{:S(2)}) collective-permute-start(bf16[24,1024]{1,0:T(8,128)(2,1)S(1)} %get-tuple-element.63), channel_id=1, source_target_pairs={{0,4},{2,6},{4,0},{6,2},{1,5},{3,7},{5,1},{7,3},{8,12},{10,14},{12... | collective-permute-start | bytes 147464 | tf_op jit(solution)/shard_map/ppermute | solution.py:392
  47.4 1.9 %collective-permute-start.17 = (bf16[24,1024]{1,0:T(8,128)(2,1)S(1)}, bf16[24,1024]{1,0:T(8,128)(2,1)S(1)}, u32[]{:S(2)}, u32[]{:S(2)}) collective-permute-start(bf16[24,1024]{1,0:T(8,128)(2,1)S(1)} %get-tuple-element.64), channel_id=1, source_target_pairs={{0,6},{2,4},{4,2},{6,0},{1,7},{3,5},{5,3},{7,1},{8,14},{10,12},{12... | collective-permute-start | bytes 147464 | tf_op jit(solution)/shard_map/ppermute | solution.py:392
  49.6 2.4 %collective-permute-done.16.refs_2_ = bf16[24,1024]{1,0:T(8,128)(2,1)S(1)} collective-permute-done((bf16[24,1024]{1,0:T(8,128)(2,1)S(1)}, bf16[24,1024]{1,0:T(8,128)(2,1)S(1)}, u32[]{:S(2)}, u32[]{:S(2)}) %collective-permute-start.16) | collective-permute-done | bytes 49184 | tf_op jit(solution)/shard_map/ppermute | solution.py:392
  51.9 1.4 %collective-permute-done.17.refs_3_ = bf16[24,1024]{1,0:T(8,128)(2,1)S(1)} collective-permute-done((bf16[24,1024]{1,0:T(8,128)(2,1)S(1)}, bf16[24,1024]{1,0:T(8,128)(2,1)S(1)}, u32[]{:S(2)}, u32[]{:S(2)}) %collective-permute-start.17) | collective-permute-done | bytes 49184 | tf_op jit(solution)/shard_map/ppermute | solution.py:392
  53.4 1.6 %collective-permute-start.18 = (bf16[24,1024]{1,0:T(8,128)(2,1)S(1)}, bf16[24,1024]{1,0:T(8,128)(2,1)S(1)}, u32[]{:S(2)}, u32[]{:S(2)}) collective-permute-start(bf16[24,1024]{1,0:T(8,128)(2,1)S(1)} %stepped_slice.1.refs_0_), channel_id=1, source_target_pairs={{0,8},{8,0},{16,24},{24,16},{1,9},{9,1},{17,25},{25,17},{2,10},{10... | collective-permute-start | bytes 147464 | tf_op jit(solution)/shard_map/ppermute | solution.py:392
  55.4 1.5 %collective-permute-start.20 = (bf16[24,1024]{1,0:T(8,128)(2,1)S(1)}, bf16[24,1024]{1,0:T(8,128)(2,1)S(1)}, u32[]{:S(2)}, u32[]{:S(2)}) collective-permute-start(bf16[24,1024]{1,0:T(8,128)(2,1)S(1)} %stepped_slice.1.refs_0_), channel_id=1, source_target_pairs={{0,24},{8,16},{16,8},{24,0},{1,25},{9,17},{17,9},{25,1},{2,26},{10... | collective-permute-start | bytes 147464 | tf_op jit(solution)/shard_map/ppermute | solution.py:392
  56.9 2.5 %block_gradient.1 = bf16[128,4096]{1,0:T(8,128)(2,1)} custom-call(bf16[192,128]{1,0:T(8,128)(2,1)S(1)} %get-tuple-element.53.grad_ref, bf16[24,4096]{1,0:T(8,128)(2,1)S(1)} %convert_bitcast_fusion.own_ref.rest_4_.refs_0_, bf16[24,4096]{1,0:T(8,128)(2,1)} %collective-permute-done.3.rest_5_.refs_1_, bf16[24,4096]{1,0:T(8,128)(2,1)S(1)} %collective-permute-done.rest_6_.refs_2_, ...), custom_call_target="tpu_custom_call" | custom-call | flops 201326592 | bytes 3145728 | tf_op jit(solution)/shard_map/block_gradient/pallas_call | solution.py:243
  59.5 1.0 %collective-permute-done.20.refs_3_ = bf16[24,1024]{1,0:T(8,128)(2,1)S(1)} collective-permute-done((bf16[24,1024]{1,0:T(8,128)(2,1)S(1)}, bf16[24,1024]{1,0:T(8,128)(2,1)S(1)}, u32[]{:S(2)}, u32[]{:S(2)}) %collective-permute-start.20) | collective-permute-done | bytes 49184 | tf_op jit(solution)/shard_map/ppermute | solution.py:392
  60.4 1.5 %outer_step.1 = (f32[24,4096]{1,0:T(8,128)}, f32[24,4096]{1,0:T(8,128)}) custom-call(s32[2]{0:T(128)S(1)} %pad_add_fusion.where_ref, f32[24,4096]{1,0:T(8,128)S(1)} %copy-done.5, f32[24,4096]{1,0:T(8,128)S(1)} %copy-done.6, bf16[24,1024]{1,0:T(8,128)(2,1)S(1)} %stepped_slice.1.refs_0_, bf16[24,1024]{1,0:T(8,128)(2,1)S(1)} %collective-permute-done.18.refs_1_, ...), custom_call_target="tpu_custom_call" | custom-call | tf_op jit(solution)/shard_map/outer_step/pallas_call | solution.py:350
  (46 shorter events, 4.1 us)
Async XLA Ops:
  1.6 10.9 %collective-permute-start = (bf16[24,4096]{1,0:T(8,128)(2,1)S(1)}, bf16[24,4096]{1,0:T(8,128)(2,1)S(1)}, u32[]{:S(2)}, u32[]{:S(2)}) collective-permute-start(bf16[24,4096]{1,0:T(8,128)(2,1)S(1)} %convert_bitcast_fusion.own_ref.rest_4_.refs_0_), channel_id=1, source_target_pairs={{0,6},{2,4},{4,2},{6,0},{1,7},{3,5},{5,3},{7,1},{8,14},{10,12},{12... | collective-permute-start | bytes 589832 | tf_op jit(solution)/shard_map/ppermute | solution.py:392
  6.8 9.4 %collective-permute-start.3 = (bf16[24,4096]{1,0:T(8,128)(2,1)S(1)}, bf16[24,4096]{1,0:T(8,128)(2,1)}, u32[]{:S(2)}, u32[]{:S(2)}) collective-permute-start(bf16[24,4096]{1,0:T(8,128)(2,1)S(1)} %convert_bitcast_fusion.own_ref.rest_4_.refs_0_), channel_id=1, source_target_pairs={{0,2},{2,0},{4,6},{6,4},{1,3},{3,1},{5,7},{7,5},{8,10},{10,8},{12,... | collective-permute-start | bytes 589832 | tf_op jit(solution)/shard_map/ppermute | solution.py:392
  6.8 12.4 %collective-permute-start.2 = (bf16[24,4096]{1,0:T(8,128)(2,1)S(1)}, bf16[24,4096]{1,0:T(8,128)(2,1)}, u32[]{:S(2)}, u32[]{:S(2)}) collective-permute-start(bf16[24,4096]{1,0:T(8,128)(2,1)S(1)} %convert_bitcast_fusion.own_ref.rest_4_.refs_0_), channel_id=1, source_target_pairs={{0,1},{1,0},{2,3},{3,2},{4,5},{5,4},{6,7},{7,6},{8,9},{9,8},{10,11... | collective-permute-start | bytes 589832 | tf_op jit(solution)/shard_map/ppermute | solution.py:392
  6.8 12.9 %copy-start = (bf16[128,4096]{1,0:T(8,128)(2,1)S(1)}, bf16[128,4096]{1,0:T(8,128)(2,1)}, u32[]{:S(2)}) copy-start(bf16[128,4096]{1,0:T(8,128)(2,1)} %cot_ref.3) | copy-start | bytes 3145732
  6.8 12.9 %copy-start.1 = (bf16[128,4096]{1,0:T(8,128)(2,1)S(1)}, bf16[128,4096]{1,0:T(8,128)(2,1)}, u32[]{:S(2)}) copy-start(bf16[128,4096]{1,0:T(8,128)(2,1)} %val_ref.3) | copy-start | bytes 3145732
  9.1 1.2 %copy-start.2 = (bf16[128,4096]{1,0:T(8,128)(2,1)S(1)}, bf16[128,4096]{1,0:T(8,128)(2,1)}, u32[]{:S(2)}) copy-start(bf16[128,4096]{1,0:T(8,128)(2,1)} %rows_ref.3) | copy-start | bytes 3145732
  12.5 11.5 %collective-permute-start.1 = (bf16[24,4096]{1,0:T(8,128)(2,1)S(1)}, bf16[24,4096]{1,0:T(8,128)(2,1)S(1)}, u32[]{:S(2)}, u32[]{:S(2)}) collective-permute-start(bf16[24,4096]{1,0:T(8,128)(2,1)S(1)} %collective-permute-done.rest_6_.refs_2_), channel_id=1, source_target_pairs={{0,2},{2,0},{4,6},{6,4},{1,3},{3,1},{5,7},{7,5},{8,10},{10,8},{12,... | collective-permute-start | bytes 589832 | tf_op jit(solution)/shard_map/ppermute | solution.py:392
  16.2 7.9 %collective-permute-start.4 = (bf16[24,4096]{1,0:T(8,128)(2,1)}, bf16[24,4096]{1,0:T(8,128)(2,1)S(1)}, u32[]{:S(2)}, u32[]{:S(2)}) collective-permute-start(bf16[24,4096]{1,0:T(8,128)(2,1)} %collective-permute-done.3.rest_5_.refs_1_), channel_id=1, source_target_pairs={{0,1},{1,0},{2,3},{3,2},{4,5},{5,4},{6,7},{7,6},{8,9},{9,8},{10,11... | collective-permute-start | bytes 589832 | tf_op jit(solution)/shard_map/ppermute | solution.py:392
  16.2 15.6 %collective-permute-start.7 = (bf16[152,1024]{1,0:T(8,128)(2,1)S(1)}, bf16[152,1024]{1,0:T(8,128)(2,1)S(1)}, u32[]{:S(2)}, u32[]{:S(2)}) collective-permute-start(bf16[152,1024]{1,0:T(8,128)(2,1)S(1)} %get-tuple-element.37), channel_id=1, source_target_pairs={{0,8},{8,0},{16,24},{24,16},{1,9},{9,1},{17,25},{25,17},{2,10},{10... | collective-permute-start | bytes 933896 | tf_op jit(solution)/shard_map/ppermute | solution.py:392
  17.7 16.2 %collective-permute-start.8 = (bf16[152,1024]{1,0:T(8,128)(2,1)S(1)}, bf16[152,1024]{1,0:T(8,128)(2,1)S(1)}, u32[]{:S(2)}, u32[]{:S(2)}) collective-permute-start(bf16[152,1024]{1,0:T(8,128)(2,1)S(1)} %get-tuple-element.38), channel_id=1, source_target_pairs={{0,16},{8,24},{16,0},{24,8},{1,17},{9,25},{17,1},{25,9},{2,18},{10... | collective-permute-start | bytes 933896 | tf_op jit(solution)/shard_map/ppermute | solution.py:392
  19.2 14.6 %collective-permute-start.9 = (bf16[152,1024]{1,0:T(8,128)(2,1)S(1)}, bf16[152,1024]{1,0:T(8,128)(2,1)S(1)}, u32[]{:S(2)}, u32[]{:S(2)}) collective-permute-start(bf16[152,1024]{1,0:T(8,128)(2,1)S(1)} %get-tuple-element.39), channel_id=1, source_target_pairs={{0,24},{8,16},{16,8},{24,0},{1,25},{9,17},{17,9},{25,1},{2,26},{10... | collective-permute-start | bytes 933896 | tf_op jit(solution)/shard_map/ppermute | solution.py:392
  21.3 4.4 %copy-start.3 = (bf16[128,4096]{1,0:T(8,128)(2,1)S(1)}, bf16[128,4096]{1,0:T(8,128)(2,1)}, u32[]{:S(2)}) copy-start(bf16[128,4096]{1,0:T(8,128)(2,1)} %rows_ref.3) | copy-start | bytes 3145732
  21.4 4.4 %copy-start.7 = (f32[64]{0:T(128)S(1)}, f32[64]{0:T(128)}, u32[]{:S(2)}) copy-start(f32[64]{0:T(128)} %param.13) | copy-start | bytes 772
  21.4 4.4 %copy-start.8 = (f32[64]{0:T(128)S(1)}, f32[64]{0:T(128)}, u32[]{:S(2)}) copy-start(f32[64]{0:T(128)} %param.14) | copy-start | bytes 772
  23.1 1.0 %copy-start.4 = (f32[128,2048]{1,0:T(8,128)}, f32[128,2048]{1,0:T(8,128)S(1)}, u32[]{:S(2)}) copy-start(f32[128,2048]{1,0:T(8,128)S(1)} %get-tuple-element.49.rest_3_) | copy-start | bytes 3145732
  24.1 1.4 %collective-permute-start.5 = (bf16[24,4096]{1,0:T(8,128)(2,1)S(1)}, bf16[24,4096]{1,0:T(8,128)(2,1)S(1)}, u32[]{:S(2)}, u32[]{:S(2)}) collective-permute-start(bf16[24,4096]{1,0:T(8,128)(2,1)S(1)} %collective-permute-done.rest_6_.refs_2_), channel_id=1, source_target_pairs={{0,1},{1,0},{2,3},{3,2},{4,5},{5,4},{6,7},{7,6},{8,9},{9,8},{10,11... | collective-permute-start | bytes 589832 | tf_op jit(solution)/shard_map/ppermute | solution.py:392
  24.1 1.7 %collective-permute-start.6 = (bf16[24,4096]{1,0:T(8,128)(2,1)S(1)}, bf16[24,4096]{1,0:T(8,128)(2,1)S(1)}, u32[]{:S(2)}, u32[]{:S(2)}) collective-permute-start(bf16[24,4096]{1,0:T(8,128)(2,1)S(1)} %collective-permute-done.1.rest_7_.refs_3_), channel_id=1, source_target_pairs={{0,1},{1,0},{2,3},{3,2},{4,5},{5,4},{6,7},{7,6},{8,9},{9,8},{10,11... | collective-permute-start | bytes 589832 | tf_op jit(solution)/shard_map/ppermute | solution.py:392
  34.0 9.8 %collective-permute-start.14 = (bf16[512,1024]{1,0:T(8,128)(2,1)S(1)}, bf16[512,1024]{1,0:T(8,128)(2,1)S(1)}, u32[]{:S(2)}, u32[]{:S(2)}) collective-permute-start(bf16[512,1024]{1,0:T(8,128)(2,1)S(1)} %pad_maximum_fusion), channel_id=1, source_target_pairs={{0,1},{1,0},{2,3},{3,2},{4,5},{5,4},{6,7},{7,6},{8,9},{9,8},{10,11... | collective-permute-start | bytes 3145736 | tf_op jit(solution)/shard_map/ppermute | solution.py:392
  34.1 2.7 %collective-permute-start.10 = (bf16[96,128]{1,0:T(8,128)(2,1)S(1)}, bf16[96,128]{1,0:T(8,128)(2,1)S(1)}, u32[]{:S(2)}, u32[]{:S(2)}) collective-permute-start(bf16[96,128]{1,0:T(8,128)(2,1)S(1)} %get-tuple-element.56), channel_id=1, source_target_pairs={{0,1},{1,0},{2,3},{3,2},{4,5},{5,4},{6,7},{7,6},{8,9},{9,8},{10,11... | collective-permute-start | bytes 73736 | tf_op jit(solution)/shard_map/ppermute | solution.py:392
  36.8 4.1 %collective-permute-start.11 = (bf16[192,128]{1,0:T(8,128)(2,1)S(1)}, bf16[192,128]{1,0:T(8,128)(2,1)S(1)}, u32[]{:S(2)}, u32[]{:S(2)}) collective-permute-start(bf16[192,128]{1,0:T(8,128)(2,1)S(1)} %constant_dynamic-update-slice_fusion.refs_0_), channel_id=1, source_target_pairs={{0,8},{8,0},{16,24},{24,16},{1,9},{9,1},{17,25},{25,17},{2,10},{10... | collective-permute-start | bytes 147464 | tf_op jit(solution)/shard_map/ppermute | solution.py:392
  38.0 4.6 %collective-permute-start.12 = (bf16[192,128]{1,0:T(8,128)(2,1)S(1)}, bf16[192,128]{1,0:T(8,128)(2,1)S(1)}, u32[]{:S(2)}, u32[]{:S(2)}) collective-permute-start(bf16[192,128]{1,0:T(8,128)(2,1)S(1)} %constant_dynamic-update-slice_fusion.refs_0_), channel_id=1, source_target_pairs={{0,16},{8,24},{16,0},{24,8},{1,17},{9,25},{17,1},{25,9},{2,18},{10... | collective-permute-start | bytes 147464 | tf_op jit(solution)/shard_map/ppermute | solution.py:392
  38.8 5.0 %collective-permute-start.13 = (bf16[192,128]{1,0:T(8,128)(2,1)S(1)}, bf16[192,128]{1,0:T(8,128)(2,1)S(1)}, u32[]{:S(2)}, u32[]{:S(2)}) collective-permute-start(bf16[192,128]{1,0:T(8,128)(2,1)S(1)} %constant_dynamic-update-slice_fusion.refs_0_), channel_id=1, source_target_pairs={{0,24},{8,16},{16,8},{24,0},{1,25},{9,17},{17,9},{25,1},{2,26},{10... | collective-permute-start | bytes 147464 | tf_op jit(solution)/shard_map/ppermute | solution.py:392
  44.9 4.7 %collective-permute-start.15 = (bf16[24,1024]{1,0:T(8,128)(2,1)S(1)}, bf16[24,1024]{1,0:T(8,128)(2,1)S(1)}, u32[]{:S(2)}, u32[]{:S(2)}) collective-permute-start(bf16[24,1024]{1,0:T(8,128)(2,1)S(1)} %get-tuple-element.62), channel_id=1, source_target_pairs={{0,2},{2,0},{4,6},{6,4},{1,3},{3,1},{5,7},{7,5},{8,10},{10,8},{12,... | collective-permute-start | bytes 147464 | tf_op jit(solution)/shard_map/ppermute | solution.py:392
  46.7 5.2 %collective-permute-start.16 = (bf16[24,1024]{1,0:T(8,128)(2,1)S(1)}, bf16[24,1024]{1,0:T(8,128)(2,1)S(1)}, u32[]{:S(2)}, u32[]{:S(2)}) collective-permute-start(bf16[24,1024]{1,0:T(8,128)(2,1)S(1)} %get-tuple-element.63), channel_id=1, source_target_pairs={{0,4},{2,6},{4,0},{6,2},{1,5},{3,7},{5,1},{7,3},{8,12},{10,14},{12... | collective-permute-start | bytes 147464 | tf_op jit(solution)/shard_map/ppermute | solution.py:392
  47.4 5.9 %collective-permute-start.17 = (bf16[24,1024]{1,0:T(8,128)(2,1)S(1)}, bf16[24,1024]{1,0:T(8,128)(2,1)S(1)}, u32[]{:S(2)}, u32[]{:S(2)}) collective-permute-start(bf16[24,1024]{1,0:T(8,128)(2,1)S(1)} %get-tuple-element.64), channel_id=1, source_target_pairs={{0,6},{2,4},{4,2},{6,0},{1,7},{3,5},{5,3},{7,1},{8,14},{10,12},{12... | collective-permute-start | bytes 147464 | tf_op jit(solution)/shard_map/ppermute | solution.py:392
  53.4 6.1 %collective-permute-start.18 = (bf16[24,1024]{1,0:T(8,128)(2,1)S(1)}, bf16[24,1024]{1,0:T(8,128)(2,1)S(1)}, u32[]{:S(2)}, u32[]{:S(2)}) collective-permute-start(bf16[24,1024]{1,0:T(8,128)(2,1)S(1)} %stepped_slice.1.refs_0_), channel_id=1, source_target_pairs={{0,8},{8,0},{16,24},{24,16},{1,9},{9,1},{17,25},{25,17},{2,10},{10... | collective-permute-start | bytes 147464 | tf_op jit(solution)/shard_map/ppermute | solution.py:392
  54.9 4.5 %collective-permute-start.19 = (bf16[24,1024]{1,0:T(8,128)(2,1)S(1)}, bf16[24,1024]{1,0:T(8,128)(2,1)S(1)}, u32[]{:S(2)}, u32[]{:S(2)}) collective-permute-start(bf16[24,1024]{1,0:T(8,128)(2,1)S(1)} %stepped_slice.1.refs_0_), channel_id=1, source_target_pairs={{0,16},{8,24},{16,0},{24,8},{1,17},{9,25},{17,1},{25,9},{2,18},{10... | collective-permute-start | bytes 147464 | tf_op jit(solution)/shard_map/ppermute | solution.py:392
  55.4 5.0 %collective-permute-start.20 = (bf16[24,1024]{1,0:T(8,128)(2,1)S(1)}, bf16[24,1024]{1,0:T(8,128)(2,1)S(1)}, u32[]{:S(2)}, u32[]{:S(2)}) collective-permute-start(bf16[24,1024]{1,0:T(8,128)(2,1)S(1)} %stepped_slice.1.refs_0_), channel_id=1, source_target_pairs={{0,24},{8,16},{16,8},{24,0},{1,25},{9,17},{17,9},{25,1},{2,26},{10... | collective-permute-start | bytes 147464 | tf_op jit(solution)/shard_map/ppermute | solution.py:392
  56.9 3.5 %copy-start.5 = (f32[24,4096]{1,0:T(8,128)S(1)}, f32[24,4096]{1,0:T(8,128)}, u32[]{:S(2)}) copy-start(f32[24,4096]{1,0:T(8,128)} %par_ref.1) | copy-start | bytes 1179652
  56.9 3.5 %copy-start.6 = (f32[24,4096]{1,0:T(8,128)S(1)}, f32[24,4096]{1,0:T(8,128)}, u32[]{:S(2)}) copy-start(f32[24,4096]{1,0:T(8,128)} %mom_ref.1) | copy-start | bytes 1179652
where the time goes:
time: 62.2 us; the launch traced here: 61.9 us
  starting transfers between devices  24.2 us (39%)
  waiting for transfers between devices  16.1 us (26%)
  Pallas kernels  15.1 us (24%)
  local copies, waits for them, and re-layouts  4.52 us (7%)
  other arithmetic  1.17 us (2%)
  between operations  0.82 us (1%)
    ppermute x21, starting transfers between devices, send(): return lax.ppermute(value, axis, [(i, i ^ k) for i in range(count)])  24.2 us
    ppermute x21, waiting for transfers between devices, send(): return lax.ppermute(value, axis, [(i, i ^ k) for i in range(count)])  16.1 us
    pallas_call x1, Pallas kernels, ssd_backward(): pl.pallas_call(functools.partial(ssd_kernel, order), in_specs=[pl.BlockSp...  5.96 us
    pallas_call x2, Pallas kernels, early_products(): pl.pallas_call(early_kernel, grid=(steps,), in_specs=[pl.BlockSpec((block...  3.34 us
    pallas_call x1, Pallas kernels, block_gradient(): pl.pallas_call(block_grad_kernel, in_specs=whole_vmem(1 + len(weights)),...  2.53 us
    unnamed x19, local copies, waits for them, and re-layouts  2.23 us
    another operation x1, local copies, waits for them, and re-layouts, on_device(): states = [start_state[b].reshape(seq_width, STATE) for b in range(blocks)]  2.2 us
    pallas_call x1, Pallas kernels, outer_step(): pl.pallas_call(outer_kernel, in_specs=[pl.BlockSpec(memory_space=pltpu.SM...  1.54 us
  transfers between devices with their start and end apart: 21, of which 13 were waited for; matrix products, arithmetic and copies ran while one was open for 4% of the time, Pallas kernels for 20%

commit v1 on v0

--- a/solution.py
+++ b/solution.py
@@ -85,9 +85,7 @@
             jax.ShapeDtypeStruct((block, width), jnp.float32),
         ],
         compiler_params=params(),
-        cost_estimate=pl.CostEstimate(
-            flops=2 * block * width * 4 * block, bytes_accessed=8 * block * width, transcendentals=0
-        ),
+        cost_estimate=pl.CostEstimate(flops=1, bytes_accessed=1, transcendentals=0),
         name="early_products",
     )(out_grad, ssd_input, state)
 
@@ -222,11 +220,7 @@
             pltpu.VMEM((cols, block), jnp.float32),
         ],
         compiler_params=params(),
-        cost_estimate=pl.CostEstimate(
-            flops=2 * block * cols * rows_in.shape[1],
-            bytes_accessed=16 * rows_in.size,
-            transcendentals=heads * block * block,
-        ),
+        cost_estimate=pl.CostEstimate(flops=1, bytes_accessed=1, transcendentals=0),
         name="ssd_backward",
     )(where, rows_in, step_bias.reshape(1, -1), decay_log.reshape(1, -1), *cross, *enter, *weights)
 
@@ -335,12 +329,14 @@
 
 
 def outer_kernel(where_ref, par_ref, mom_ref, *refs):
-    stepped, (new_par, new_mom) = refs[:-2], refs[-2:]
+    stepped, (new_par, new_mom, all_ref) = refs[:-3], refs[-3:]
     width = stepped[0].shape[1]
     for k, part in enumerate(stepped):
-        cols = pl.ds(pl.multiple_of((where_ref[0] ^ k) * width, 128), width)
+        all_ref[where_ref[0] ^ k] = part[...].astype(jnp.float32)
+    for r in range(len(stepped)):
+        cols = slice(r * width, (r + 1) * width)
         old = par_ref[:, cols]
-        pseudo = old - part[...].astype(jnp.float32)
+        pseudo = old - all_ref[r]
         fresh = momentum_decay * mom_ref[:, cols] + pseudo
         new_mom[:, cols] = fresh
         new_par[:, cols] = old - outer_rate * (pseudo + momentum_decay * fresh)
@@ -352,6 +348,7 @@
         in_specs=[pl.BlockSpec(memory_space=pltpu.SMEM)] + whole_vmem(2 + len(stepped)),
         out_specs=whole_vmem(2),
         out_shape=[jax.ShapeDtypeStruct(global_params.shape, jnp.float32)] * 2,
+        scratch_shapes=[pltpu.VMEM((len(stepped),) + stepped[0].shape, jnp.float32)],
         compiler_params=params(),
         name="outer_step",
     )(where, global_params, momentum, *stepped)
@@ -391,9 +388,13 @@
         count = dict(rep=replicas, line=chips, core=cores)[axis]
         return lax.ppermute(value, axis, [(i, i ^ k) for i in range(count)])
 
+    def send_each(values, axis):
+        values = [(k, v) for k, v in enumerate(values, 1)]
+        return [sent for sent in reversed([send(v, axis, k) for k, v in reversed(values)])]
+
     if fast:
+        far = send(own, "line", 3)
         near = send(own, "line", 1)
-        far = send(own, "line", 3)
         order = (0, 2, 6, 4, 1, 3, 7, 5)
     else:
         weights = [lax.all_gather(own, ("line", "core"), axis=0, tiled=True)]
@@ -411,10 +412,11 @@
     if fast:
         pieces = column_pieces(where, block_input, own_late, replicas)
         far, _ = lax.optimization_barrier((far, pieces))
-        pieces = [pieces[0]] + [send(pieces[k], "rep", k) for k in range(1, replicas)]
+        pieces = [pieces[0]] + send_each(pieces[1:], "rep")
+        far, early[0] = lax.optimization_barrier((far, early[0]))
         middle = send(far, "line", 1)
         twins = [send(own, "core", 1), send(near, "core", 1)]
-        middle, early, twins = lax.optimization_barrier((middle, early, twins))
+        middle, early[1], twins = lax.optimization_barrier((middle, early[1], twins))
         twins = twins + [send(far, "core", 1), send(middle, "core", 1)]
         weights = [own, near, far, middle] + twins
 
@@ -452,15 +454,15 @@
         return (block_grad, new_params, new_momentum)
 
     tokens = blocks * block
-    mine, pieces = lax.optimization_barrier((mine, pieces))
+    other = send(other, "core", 1)
+    other, pieces = lax.optimization_barrier((other, pieces))
     twin = send(jnp.concatenate([p[:tokens] for p in pieces], axis=0), "core", 1)
-
-    both = jnp.concatenate([mine, send(other, "core", 1)], axis=0)
-    plane = [both] + [send(both, "rep", k) for k in range(1, replicas)]
+    both = jnp.concatenate([mine, other], axis=0)
+    plane = [both] + send_each([both] * (replicas - 1), "rep")
     sums = gradient_slice(where, plane, pieces, twin, chips)
-    sums = [sums[0]] + [send(sums[k], "line", k) for k in range(1, chips)]
+    sums = [sums[0]] + send_each(sums[1:], "line")
     stepped = stepped_slice(sums, pieces)
-    stepped = [stepped] + [send(stepped, "rep", k) for k in range(1, replicas)]
+    stepped = [stepped] + send_each([stepped] * (replicas - 1), "rep")
     new_params, new_momentum = outer_step(where, global_params, momentum, stepped)
     return (block_grad, new_params, new_momentum)
 

time: 62.2 us -> 59.7 us (0.960)
  waiting for transfers between devices: 16.1 us -> 12.4 us
  local copies, waits for them, and re-layouts: 4.52 us -> 6.32 us
  starting transfers between devices: 24.2 us -> 23.4 us
    ppermute x21, waiting for transfers between devices: 16.1 us -> 12.4 us  [send(): return lax.ppermute(value, axis, [(i, i ^ k) for i in range(count)])]
    unnamed x19 -> x27, local copies, waits for them, and re-layouts: 2.23 us -> 4.19 us
    ppermute x21, starting transfers between devices: 24.2 us -> 23.4 us  [send(): return lax.ppermute(value, axis, [(i, i ^ k) for i in range(count)])]
  transfers between devices with their start and end apart: 21 -> 21, of which waited for: 13 -> 9; matrix products, arithmetic and copies ran while one was open for 4% -> 4% of each run, Pallas kernels for 20% -> 21%
where the time goes in v1:
time: 59.7 us; the launch traced here: 59.4 us
  starting transfers between devices  23.4 us (39%)
  Pallas kernels  15.1 us (25%)
  waiting for transfers between devices  12.4 us (21%)
  local copies, waits for them, and re-layouts  6.32 us (11%)
  other arithmetic  1.31 us (2%)
  between operations  0.88 us (1%)
    ppermute x21, starting transfers between devices, send(): return lax.ppermute(value, axis, [(i, i ^ k) for i in range(count)])  23.4 us
    ppermute x21, waiting for transfers between devices, send(): return lax.ppermute(value, axis, [(i, i ^ k) for i in range(count)])  12.4 us
    pallas_call x1, Pallas kernels, ssd_backward(): pl.pallas_call(functools.partial(ssd_kernel, order), in_specs=[pl.BlockSp...  5.95 us
    unnamed x27, local copies, waits for them, and re-layouts  4.19 us
    pallas_call x2, Pallas kernels, early_products(): pl.pallas_call(early_kernel, grid=(steps,), in_specs=[pl.BlockSpec((block...  3.34 us
    pallas_call x1, Pallas kernels, block_gradient(): pl.pallas_call(block_grad_kernel, in_specs=whole_vmem(1 + len(weights)),...  2.53 us
    another operation x1, local copies, waits for them, and re-layouts, on_device(): states = [start_state[b].reshape(seq_width, STATE) for b in range(blocks)]  2.05 us
    pallas_call x1, Pallas kernels, outer_step(): pl.pallas_call(outer_kernel, in_specs=[pl.BlockSpec(memory_space=pltpu.SM...  1.57 us
  transfers between devices with their start and end apart: 21, of which 9 were waited for; matrix products, arithmetic and copies ran while one was open for 4% of the time, Pallas kernels for 21%

profile of v1, /device:TPU:0, one launch (start us, length us, event | category | flops | bytes accessed | tf_op | source)
XLA Modules:
  0.0 59.4 jit_solution(6426302539341652935)
XLA Ops:
  0.7 1.2 %convert_bitcast_fusion.own_ref.rest_4_.refs_0_ = bf16[24,4096]{1,0:T(8,128)(2,1)S(1)} fusion(f32[1,24,4096]{2,1,0:T(8,128)} %param.15), kind=kLoop, calls=%fused_computation.1 | loop fusion | flops 98304 | bytes 589824 | tf_op jit(solution)/shard_map/convert_element_type | solution.py:372
  1.8 5.1 %collective-permute-start = (bf16[24,4096]{1,0:T(8,128)(2,1)S(1)}, bf16[24,4096]{1,0:T(8,128)(2,1)S(1)}, u32[]{:S(2)}, u32[]{:S(2)}) collective-permute-start(bf16[24,4096]{1,0:T(8,128)(2,1)S(1)} %convert_bitcast_fusion.own_ref.rest_4_.refs_0_), channel_id=1, source_target_pairs={{0,6},{2,4},{4,2},{6,0},{1,7},{3,5},{5,3},{7,1},{8,14},{10,12},{12... | collective-permute-start | bytes 589832 | tf_op jit(solution)/shard_map/ppermute | solution.py:389
  6.9 2.1 %reshape_squeeze.3.state_ref = bf16[4096,64]{1,0:T(8,128)(2,1)S(1)} reshape(bf16[1,64,4096]{2,1,0:T(8,128)(2,1)} %param.12) | data formatting | bytes 1048576 | tf_op jit(solution)/shard_map/reshape;squeeze | solution.py:404
  9.0 1.7 %early_products.2 = (bf16[32,128,128]{2,1,0:T(8,128)(2,1)S(1)}, f32[128,2048]{1,0:T(8,128)S(1)}) custom-call(bf16[128,4096]{1,0:T(8,128)(2,1)S(1)} %copy-done, bf16[128,4096]{1,0:T(8,128)(2,1)S(1)} %copy-done.1, bf16[4096,64]{1,0:T(8,128)(2,1)S(1)} %reshape_squeeze.3.state_ref), custom_call_target="tpu_custom_call" | custom-call | flops 1 | bytes 1 | tf_op jit(solution)/shard_map/early_products/pallas_call | solution.py:71
  10.7 1.0 %copy-done.4 = bf16[32,128,128]{2,1,0:T(8,128)(2,1)} copy-done((bf16[32,128,128]{2,1,0:T(8,128)(2,1)}, bf16[32,128,128]{2,1,0:T(8,128)(2,1)S(1)}, u32[]{:S(2)}) %copy-start.4) | copy-done | bytes 1048600
  11.7 1.0 %copy-done.6 = f32[128,2048]{1,0:T(8,128)} copy-done((f32[128,2048]{1,0:T(8,128)}, f32[128,2048]{1,0:T(8,128)S(1)}, u32[]{:S(2)}) %copy-start.6) | copy-done | bytes 1048600
  12.7 1.2 %copy-done.2 = bf16[128,4096]{1,0:T(8,128)(2,1)S(1)} copy-done((bf16[128,4096]{1,0:T(8,128)(2,1)S(1)}, bf16[128,4096]{1,0:T(8,128)(2,1)}, u32[]{:S(2)}) %copy-start.2) | copy-done | bytes 1048600
  14.0 0.6 %column_pieces.1 = (bf16[152,1024]{1,0:T(8,128)(2,1)S(1)}, bf16[152,1024]{1,0:T(8,128)(2,1)S(1)}, bf16[152,1024]{1,0:T(8,128)(2,1)S(1)}, bf16[152,1024]{1,0:T(8,128)(2,1)S(1)}) custom-call(s32[2]{0:T(128)S(1)} %pad_add_fusion.where_ref, bf16[128,4096]{1,0:T(8,128)(2,1)S(1)} %copy-done.2, bf16[24,4096]{1,0:T(8,128)(2,1)S(1)} %convert_bitcast_fusion.own_ref.rest_4_.refs_0_), custom_call_target="tpu_custom_call" | custom-call | tf_op jit(solution)/shard_map/column_pieces/pallas_call | solution.py:262
  14.7 2.1 %collective-permute-start.1 = (bf16[24,4096]{1,0:T(8,128)(2,1)S(1)}, bf16[24,4096]{1,0:T(8,128)(2,1)S(1)}, u32[]{:S(2)}, u32[]{:S(2)}) collective-permute-start(bf16[24,4096]{1,0:T(8,128)(2,1)S(1)} %collective-permute-done.rest_6_.refs_2_), channel_id=1, source_target_pairs={{0,2},{2,0},{4,6},{6,4},{1,3},{3,1},{5,7},{7,5},{8,10},{10,8},{12,... | collective-permute-start | bytes 589832 | tf_op jit(solution)/shard_map/ppermute | solution.py:389
  17.0 2.4 %collective-permute-start.10 = (bf16[152,1024]{1,0:T(8,128)(2,1)S(1)}, bf16[152,1024]{1,0:T(8,128)(2,1)S(1)}, u32[]{:S(2)}, u32[]{:S(2)}) collective-permute-start(bf16[152,1024]{1,0:T(8,128)(2,1)S(1)} %get-tuple-element.40), channel_id=1, source_target_pairs={{0,24},{8,16},{16,8},{24,0},{1,25},{9,17},{17,9},{25,1},{2,26},{10... | collective-permute-start | bytes 933896 | tf_op jit(solution)/shard_map/ppermute | solution.py:389
  20.5 1.7 %early_products.3 = (bf16[32,128,128]{2,1,0:T(8,128)(2,1)S(1)}, f32[128,2048]{1,0:T(8,128)S(1)}) custom-call(bf16[128,4096]{1,0:T(8,128)(2,1)S(1)} %copy-done, bf16[128,4096]{1,0:T(8,128)(2,1)S(1)} %copy-done.1, bf16[4096,64]{1,0:T(8,128)(2,1)S(1)} %reshape_squeeze.3.state_ref), custom_call_target="tpu_custom_call" | custom-call | flops 1 | bytes 1 | tf_op jit(solution)/shard_map/early_products/pallas_call | solution.py:71
  22.2 1.0 %copy-done.8 = f32[128,2048]{1,0:T(8,128)} copy-done((f32[128,2048]{1,0:T(8,128)}, f32[128,2048]{1,0:T(8,128)S(1)}, u32[]{:S(2)}) %copy-start.8) | copy-done | bytes 1048600
  23.6 0.9 %collective-permute-done.5.rest_10_.refs_6_ = bf16[24,4096]{1,0:T(8,128)(2,1)S(1)} collective-permute-done((bf16[24,4096]{1,0:T(8,128)(2,1)S(1)}, bf16[24,4096]{1,0:T(8,128)(2,1)S(1)}, u32[]{:S(2)}, u32[]{:S(2)}) %collective-permute-start.5) | collective-permute-done | bytes 196640 | tf_op jit(solution)/shard_map/ppermute | solution.py:389
  24.9 6.0 %ssd_backward.1 = (bf16[192,128]{1,0:T(8,128)(2,1)S(1)}, bf16[96,128]{1,0:T(8,128)(2,1)S(1)}, bf16[96,128]{1,0:T(8,128)(2,1)S(1)}) custom-call(s32[2]{0:T(128)S(1)} %pad_add_fusion.where_ref, bf16[128,4096]{1,0:T(8,128)(2,1)S(1)} %copy-done.3, f32[1,64]{1,0:T(1,128)S(1)} %bitcast.6, f32[1,64]{1,0:T(1,128)S(1)} %bitcast.7, ...), custom_call_target="tpu_custom_call" | custom-call | flops 1 | bytes 1 | tf_op jit(solution)/shard_map/ssd_backward/pallas_call | solution.py:208
  31.1 3.0 %collective-permute-done.8.refs_5_ = bf16[152,1024]{1,0:T(8,128)(2,1)S(1)} collective-permute-done((bf16[152,1024]{1,0:T(8,128)(2,1)S(1)}, bf16[152,1024]{1,0:T(8,128)(2,1)S(1)}, u32[]{:S(2)}, u32[]{:S(2)}) %collective-permute-start.8) | collective-permute-done | bytes 311328 | tf_op jit(solution)/shard_map/ppermute | solution.py:389
  34.5 1.6 %collective-permute-start.11 = (bf16[192,128]{1,0:T(8,128)(2,1)S(1)}, bf16[192,128]{1,0:T(8,128)(2,1)S(1)}, u32[]{:S(2)}, u32[]{:S(2)}) collective-permute-start(bf16[192,128]{1,0:T(8,128)(2,1)S(1)} %constant_dynamic-update-slice_fusion.refs_0_), channel_id=1, source_target_pairs={{0,8},{8,0},{16,24},{24,16},{1,9},{9,1},{17,25},{25,17},{2,10},{10... | collective-permute-start | bytes 147464 | tf_op jit(solution)/shard_map/ppermute | solution.py:389
  36.0 1.4 %collective-permute-start.12 = (bf16[192,128]{1,0:T(8,128)(2,1)S(1)}, bf16[192,128]{1,0:T(8,128)(2,1)S(1)}, u32[]{:S(2)}, u32[]{:S(2)}) collective-permute-start(bf16[192,128]{1,0:T(8,128)(2,1)S(1)} %constant_dynamic-update-slice_fusion.refs_0_), channel_id=1, source_target_pairs={{0,16},{8,24},{16,0},{24,8},{1,17},{9,25},{17,1},{25,9},{2,18},{10... | collective-permute-start | bytes 147464 | tf_op jit(solution)/shard_map/ppermute | solution.py:389
  37.5 0.6 collective-permute-start.13
  38.0 0.6 %collective-permute-done.11.refs_1_ = bf16[192,128]{1,0:T(8,128)(2,1)S(1)} collective-permute-done((bf16[192,128]{1,0:T(8,128)(2,1)S(1)}, bf16[192,128]{1,0:T(8,128)(2,1)S(1)}, u32[]{:S(2)}, u32[]{:S(2)}) %collective-permute-start.11) | collective-permute-done | bytes 49184 | tf_op jit(solution)/shard_map/ppermute | solution.py:389
  38.7 1.5 %collective-permute-done.12.refs_2_ = bf16[192,128]{1,0:T(8,128)(2,1)S(1)} collective-permute-done((bf16[192,128]{1,0:T(8,128)(2,1)S(1)}, bf16[192,128]{1,0:T(8,128)(2,1)S(1)}, u32[]{:S(2)}, u32[]{:S(2)}) %collective-permute-start.12) | collective-permute-done | bytes 49184 | tf_op jit(solution)/shard_map/ppermute | solution.py:389
  40.1 2.3 %collective-permute-done.13.refs_3_ = bf16[192,128]{1,0:T(8,128)(2,1)S(1)} collective-permute-done((bf16[192,128]{1,0:T(8,128)(2,1)S(1)}, bf16[192,128]{1,0:T(8,128)(2,1)S(1)}, u32[]{:S(2)}, u32[]{:S(2)}) %collective-permute-start.13) | collective-permute-done | bytes 49184 | tf_op jit(solution)/shard_map/ppermute | solution.py:389
  42.5 1.0 %gradient_slice.1 = (bf16[24,1024]{1,0:T(8,128)(2,1)S(1)}, bf16[24,1024]{1,0:T(8,128)(2,1)S(1)}, bf16[24,1024]{1,0:T(8,128)(2,1)S(1)}, bf16[24,1024]{1,0:T(8,128)(2,1)S(1)}) custom-call(s32[2]{0:T(128)S(1)} %pad_add_fusion.where_ref, bf16[192,128]{1,0:T(8,128)(2,1)S(1)} %constant_dynamic-update-slice_fusion.refs_0_, ...), custom_call_target="tpu_custom_call" | custom-call | tf_op jit(solution)/shard_map/gradient_slice/pallas_call | solution.py:296
  43.5 1.3 %collective-permute-start.15 = (bf16[24,1024]{1,0:T(8,128)(2,1)S(1)}, bf16[24,1024]{1,0:T(8,128)(2,1)S(1)}, u32[]{:S(2)}, u32[]{:S(2)}) collective-permute-start(bf16[24,1024]{1,0:T(8,128)(2,1)S(1)} %get-tuple-element.64), channel_id=1, source_target_pairs={{0,2},{2,0},{4,6},{6,4},{1,3},{3,1},{5,7},{7,5},{8,10},{10,8},{12,... | collective-permute-start | bytes 147464 | tf_op jit(solution)/shard_map/ppermute | solution.py:389
  44.7 1.0 %collective-permute-start.16 = (bf16[24,1024]{1,0:T(8,128)(2,1)S(1)}, bf16[24,1024]{1,0:T(8,128)(2,1)S(1)}, u32[]{:S(2)}, u32[]{:S(2)}) collective-permute-start(bf16[24,1024]{1,0:T(8,128)(2,1)S(1)} %get-tuple-element.65), channel_id=1, source_target_pairs={{0,4},{2,6},{4,0},{6,2},{1,5},{3,7},{5,1},{7,3},{8,12},{10,14},{12... | collective-permute-start | bytes 147464 | tf_op jit(solution)/shard_map/ppermute | solution.py:389
  45.7 2.2 %collective-permute-start.17 = (bf16[24,1024]{1,0:T(8,128)(2,1)S(1)}, bf16[24,1024]{1,0:T(8,128)(2,1)S(1)}, u32[]{:S(2)}, u32[]{:S(2)}) collective-permute-start(bf16[24,1024]{1,0:T(8,128)(2,1)S(1)} %get-tuple-element.66), channel_id=1, source_target_pairs={{0,6},{2,4},{4,2},{6,0},{1,7},{3,5},{5,3},{7,1},{8,14},{10,12},{12... | collective-permute-start | bytes 147464 | tf_op jit(solution)/shard_map/ppermute | solution.py:389
  48.0 2.3 %collective-permute-done.16.refs_2_ = bf16[24,1024]{1,0:T(8,128)(2,1)S(1)} collective-permute-done((bf16[24,1024]{1,0:T(8,128)(2,1)S(1)}, bf16[24,1024]{1,0:T(8,128)(2,1)S(1)}, u32[]{:S(2)}, u32[]{:S(2)}) %collective-permute-start.16) | collective-permute-done | bytes 49184 | tf_op jit(solution)/shard_map/ppermute | solution.py:389
  50.3 1.3 %collective-permute-done.17.refs_3_ = bf16[24,1024]{1,0:T(8,128)(2,1)S(1)} collective-permute-done((bf16[24,1024]{1,0:T(8,128)(2,1)S(1)}, bf16[24,1024]{1,0:T(8,128)(2,1)S(1)}, u32[]{:S(2)}, u32[]{:S(2)}) %collective-permute-start.17) | collective-permute-done | bytes 49184 | tf_op jit(solution)/shard_map/ppermute | solution.py:389
  51.7 0.6 %collective-permute-start.18 = (bf16[24,1024]{1,0:T(8,128)(2,1)S(1)}, bf16[24,1024]{1,0:T(8,128)(2,1)S(1)}, u32[]{:S(2)}, u32[]{:S(2)}) collective-permute-start(bf16[24,1024]{1,0:T(8,128)(2,1)S(1)} %stepped_slice.1.refs_0_), channel_id=1, source_target_pairs={{0,8},{8,0},{16,24},{24,16},{1,9},{9,1},{17,25},{25,17},{2,10},{10... | collective-permute-start | bytes 147464 | tf_op jit(solution)/shard_map/ppermute | solution.py:389
  52.3 0.6 %collective-permute-start.19 = (bf16[24,1024]{1,0:T(8,128)(2,1)S(1)}, bf16[24,1024]{1,0:T(8,128)(2,1)S(1)}, u32[]{:S(2)}, u32[]{:S(2)}) collective-permute-start(bf16[24,1024]{1,0:T(8,128)(2,1)S(1)} %stepped_slice.1.refs_0_), channel_id=1, source_target_pairs={{0,16},{8,24},{16,0},{24,8},{1,17},{9,25},{17,1},{25,9},{2,18},{10... | collective-permute-start | bytes 147464 | tf_op jit(solution)/shard_map/ppermute | solution.py:389
  52.9 2.3 %collective-permute-start.20 = (bf16[24,1024]{1,0:T(8,128)(2,1)S(1)}, bf16[24,1024]{1,0:T(8,128)(2,1)S(1)}, u32[]{:S(2)}, u32[]{:S(2)}) collective-permute-start(bf16[24,1024]{1,0:T(8,128)(2,1)S(1)} %stepped_slice.1.refs_0_), channel_id=1, source_target_pairs={{0,24},{8,16},{16,8},{24,0},{1,25},{9,17},{17,9},{25,1},{2,26},{10... | collective-permute-start | bytes 147464 | tf_op jit(solution)/shard_map/ppermute | solution.py:389
  55.2 2.5 %block_gradient.1 = bf16[128,4096]{1,0:T(8,128)(2,1)} custom-call(bf16[192,128]{1,0:T(8,128)(2,1)S(1)} %get-tuple-element.55.grad_ref, bf16[24,4096]{1,0:T(8,128)(2,1)S(1)} %convert_bitcast_fusion.own_ref.rest_4_.refs_0_, bf16[24,4096]{1,0:T(8,128)(2,1)} %collective-permute-done.3.rest_5_.refs_1_, bf16[24,4096]{1,0:T(8,128)(2,1)S(1)} %collective-permute-done.rest_6_.refs_2_, ...), custom_call_target="tpu_custom_call" | custom-call | flops 201326592 | bytes 3145728 | tf_op jit(solution)/shard_map/block_gradient/pallas_call | solution.py:237
  57.9 1.6 %outer_step.1 = (f32[24,4096]{1,0:T(8,128)}, f32[24,4096]{1,0:T(8,128)}) custom-call(s32[2]{0:T(128)S(1)} %pad_add_fusion.where_ref, f32[24,4096]{1,0:T(8,128)S(1)} %copy-done.9, f32[24,4096]{1,0:T(8,128)S(1)} %copy-done.10, bf16[24,1024]{1,0:T(8,128)(2,1)S(1)} %stepped_slice.1.refs_0_, bf16[24,1024]{1,0:T(8,128)(2,1)S(1)} %collective-permute-done.18.refs_1_, ...), custom_call_target="tpu_custom_call" | custom-call | tf_op jit(solution)/shard_map/outer_step/pallas_call | solution.py:346
  (54 shorter events, 2.9 us)
Async XLA Ops:
  0.6 8.4 %copy-start.1 = (bf16[128,4096]{1,0:T(8,128)(2,1)S(1)}, bf16[128,4096]{1,0:T(8,128)(2,1)}, u32[]{:S(2)}) copy-start(bf16[128,4096]{1,0:T(8,128)(2,1)} %val_ref.3) | copy-start | bytes 3145732
  0.6 8.4 %copy-start = (bf16[128,4096]{1,0:T(8,128)(2,1)S(1)}, bf16[128,4096]{1,0:T(8,128)(2,1)}, u32[]{:S(2)}) copy-start(bf16[128,4096]{1,0:T(8,128)(2,1)} %cot_ref.3) | copy-start | bytes 3145732
  1.8 12.8 %collective-permute-start = (bf16[24,4096]{1,0:T(8,128)(2,1)S(1)}, bf16[24,4096]{1,0:T(8,128)(2,1)S(1)}, u32[]{:S(2)}, u32[]{:S(2)}) collective-permute-start(bf16[24,4096]{1,0:T(8,128)(2,1)S(1)} %convert_bitcast_fusion.own_ref.rest_4_.refs_0_), channel_id=1, source_target_pairs={{0,6},{2,4},{4,2},{6,0},{1,7},{3,5},{5,3},{7,1},{8,14},{10,12},{12... | collective-permute-start | bytes 589832 | tf_op jit(solution)/shard_map/ppermute | solution.py:389
  6.9 9.8 %collective-permute-start.3 = (bf16[24,4096]{1,0:T(8,128)(2,1)S(1)}, bf16[24,4096]{1,0:T(8,128)(2,1)}, u32[]{:S(2)}, u32[]{:S(2)}) collective-permute-start(bf16[24,4096]{1,0:T(8,128)(2,1)S(1)} %convert_bitcast_fusion.own_ref.rest_4_.refs_0_), channel_id=1, source_target_pairs={{0,2},{2,0},{4,6},{6,4},{1,3},{3,1},{5,7},{7,5},{8,10},{10,8},{12,... | collective-permute-start | bytes 589832 | tf_op jit(solution)/shard_map/ppermute | solution.py:389
  6.9 13.0 %collective-permute-start.2 = (bf16[24,4096]{1,0:T(8,128)(2,1)S(1)}, bf16[24,4096]{1,0:T(8,128)(2,1)}, u32[]{:S(2)}, u32[]{:S(2)}) collective-permute-start(bf16[24,4096]{1,0:T(8,128)(2,1)S(1)} %convert_bitcast_fusion.own_ref.rest_4_.refs_0_), channel_id=1, source_target_pairs={{0,1},{1,0},{2,3},{3,2},{4,5},{5,4},{6,7},{7,6},{8,9},{9,8},{10,11... | collective-permute-start | bytes 589832 | tf_op jit(solution)/shard_map/ppermute | solution.py:389
  11.7 1.0 %copy-start.6 = (f32[128,2048]{1,0:T(8,128)}, f32[128,2048]{1,0:T(8,128)S(1)}, u32[]{:S(2)}) copy-start(f32[128,2048]{1,0:T(8,128)S(1)} %get-tuple-element.50.rest_2_) | copy-start | bytes 3145732
  12.7 1.2 %copy-start.2 = (bf16[128,4096]{1,0:T(8,128)(2,1)S(1)}, bf16[128,4096]{1,0:T(8,128)(2,1)}, u32[]{:S(2)}) copy-start(bf16[128,4096]{1,0:T(8,128)(2,1)} %rows_ref.3) | copy-start | bytes 3145732
  14.6 10.3 %copy-start.3 = (bf16[128,4096]{1,0:T(8,128)(2,1)S(1)}, bf16[128,4096]{1,0:T(8,128)(2,1)}, u32[]{:S(2)}) copy-start(bf16[128,4096]{1,0:T(8,128)(2,1)} %rows_ref.3) | copy-start | bytes 3145732
  14.6 10.3 %copy-start.5 = (bf16[32,128,128]{2,1,0:T(8,128)(2,1)S(1)}, bf16[32,128,128]{2,1,0:T(8,128)(2,1)}, u32[]{:S(2)}) copy-start(bf16[32,128,128]{2,1,0:T(8,128)(2,1)} %copy-done.4) | copy-start | bytes 3145732
  14.6 10.2 %copy-start.7 = (f32[128,2048]{1,0:T(8,128)S(1)}, f32[128,2048]{1,0:T(8,128)}, u32[]{:S(2)}) copy-start(f32[128,2048]{1,0:T(8,128)} %copy-done.6) | copy-start | bytes 3145732
  14.6 10.2 %copy-start.11 = (f32[64]{0:T(128)S(1)}, f32[64]{0:T(128)}, u32[]{:S(2)}) copy-start(f32[64]{0:T(128)} %param.13) | copy-start | bytes 772
  14.6 10.2 %copy-start.12 = (f32[64]{0:T(128)S(1)}, f32[64]{0:T(128)}, u32[]{:S(2)}) copy-start(f32[64]{0:T(128)} %param.14) | copy-start | bytes 772
  14.7 8.5 %collective-permute-start.1 = (bf16[24,4096]{1,0:T(8,128)(2,1)S(1)}, bf16[24,4096]{1,0:T(8,128)(2,1)S(1)}, u32[]{:S(2)}, u32[]{:S(2)}) collective-permute-start(bf16[24,4096]{1,0:T(8,128)(2,1)S(1)} %collective-permute-done.rest_6_.refs_2_), channel_id=1, source_target_pairs={{0,2},{2,0},{4,6},{6,4},{1,3},{3,1},{5,7},{7,5},{8,10},{10,8},{12,... | collective-permute-start | bytes 589832 | tf_op jit(solution)/shard_map/ppermute | solution.py:389
  16.8 6.4 %collective-permute-start.4 = (bf16[24,4096]{1,0:T(8,128)(2,1)}, bf16[24,4096]{1,0:T(8,128)(2,1)S(1)}, u32[]{:S(2)}, u32[]{:S(2)}) collective-permute-start(bf16[24,4096]{1,0:T(8,128)(2,1)} %collective-permute-done.3.rest_5_.refs_1_), channel_id=1, source_target_pairs={{0,1},{1,0},{2,3},{3,2},{4,5},{5,4},{6,7},{7,6},{8,9},{9,8},{10,11... | collective-permute-start | bytes 589832 | tf_op jit(solution)/shard_map/ppermute | solution.py:389
  17.0 14.2 %collective-permute-start.10 = (bf16[152,1024]{1,0:T(8,128)(2,1)S(1)}, bf16[152,1024]{1,0:T(8,128)(2,1)S(1)}, u32[]{:S(2)}, u32[]{:S(2)}) collective-permute-start(bf16[152,1024]{1,0:T(8,128)(2,1)S(1)} %get-tuple-element.40), channel_id=1, source_target_pairs={{0,24},{8,16},{16,8},{24,0},{1,25},{9,17},{17,9},{25,1},{2,26},{10... | collective-permute-start | bytes 933896 | tf_op jit(solution)/shard_map/ppermute | solution.py:389
  19.4 14.8 %collective-permute-start.8 = (bf16[152,1024]{1,0:T(8,128)(2,1)S(1)}, bf16[152,1024]{1,0:T(8,128)(2,1)S(1)}, u32[]{:S(2)}, u32[]{:S(2)}) collective-permute-start(bf16[152,1024]{1,0:T(8,128)(2,1)S(1)} %get-tuple-element.38), channel_id=1, source_target_pairs={{0,8},{8,0},{16,24},{24,16},{1,9},{9,1},{17,25},{25,17},{2,10},{10... | collective-permute-start | bytes 933896 | tf_op jit(solution)/shard_map/ppermute | solution.py:389
  20.0 14.2 %collective-permute-start.9 = (bf16[152,1024]{1,0:T(8,128)(2,1)S(1)}, bf16[152,1024]{1,0:T(8,128)(2,1)S(1)}, u32[]{:S(2)}, u32[]{:S(2)}) collective-permute-start(bf16[152,1024]{1,0:T(8,128)(2,1)S(1)} %get-tuple-element.39), channel_id=1, source_target_pairs={{0,16},{8,24},{16,0},{24,8},{1,17},{9,25},{17,1},{25,9},{2,18},{10... | collective-permute-start | bytes 933896 | tf_op jit(solution)/shard_map/ppermute | solution.py:389
  23.1 1.4 %collective-permute-start.5 = (bf16[24,4096]{1,0:T(8,128)(2,1)S(1)}, bf16[24,4096]{1,0:T(8,128)(2,1)S(1)}, u32[]{:S(2)}, u32[]{:S(2)}) collective-permute-start(bf16[24,4096]{1,0:T(8,128)(2,1)S(1)} %collective-permute-done.rest_6_.refs_2_), channel_id=1, source_target_pairs={{0,1},{1,0},{2,3},{3,2},{4,5},{5,4},{6,7},{7,6},{8,9},{9,8},{10,11... | collective-permute-start | bytes 589832 | tf_op jit(solution)/shard_map/ppermute | solution.py:389
  23.1 1.7 %collective-permute-start.6 = (bf16[24,4096]{1,0:T(8,128)(2,1)S(1)}, bf16[24,4096]{1,0:T(8,128)(2,1)S(1)}, u32[]{:S(2)}, u32[]{:S(2)}) collective-permute-start(bf16[24,4096]{1,0:T(8,128)(2,1)S(1)} %collective-permute-done.1.rest_7_.refs_3_), channel_id=1, source_target_pairs={{0,1},{1,0},{2,3},{3,2},{4,5},{5,4},{6,7},{7,6},{8,9},{9,8},{10,11... | collective-permute-start | bytes 589832 | tf_op jit(solution)/shard_map/ppermute | solution.py:389
  30.8 3.4 %collective-permute-start.7 = (bf16[96,128]{1,0:T(8,128)(2,1)S(1)}, bf16[96,128]{1,0:T(8,128)(2,1)S(1)}, u32[]{:S(2)}, u32[]{:S(2)}) collective-permute-start(bf16[96,128]{1,0:T(8,128)(2,1)S(1)} %get-tuple-element.57), channel_id=1, source_target_pairs={{0,1},{1,0},{2,3},{3,2},{4,5},{5,4},{6,7},{7,6},{8,9},{9,8},{10,11... | collective-permute-start | bytes 73736 | tf_op jit(solution)/shard_map/ppermute | solution.py:389
  34.4 8.1 %collective-permute-start.14 = (bf16[512,1024]{1,0:T(8,128)(2,1)S(1)}, bf16[512,1024]{1,0:T(8,128)(2,1)S(1)}, u32[]{:S(2)}, u32[]{:S(2)}) collective-permute-start(bf16[512,1024]{1,0:T(8,128)(2,1)S(1)} %pad_maximum_fusion), channel_id=1, source_target_pairs={{0,1},{1,0},{2,3},{3,2},{4,5},{5,4},{6,7},{7,6},{8,9},{9,8},{10,11... | collective-permute-start | bytes 3145736 | tf_op jit(solution)/shard_map/ppermute | solution.py:389
  34.5 4.2 %collective-permute-start.11 = (bf16[192,128]{1,0:T(8,128)(2,1)S(1)}, bf16[192,128]{1,0:T(8,128)(2,1)S(1)}, u32[]{:S(2)}, u32[]{:S(2)}) collective-permute-start(bf16[192,128]{1,0:T(8,128)(2,1)S(1)} %constant_dynamic-update-slice_fusion.refs_0_), channel_id=1, source_target_pairs={{0,8},{8,0},{16,24},{24,16},{1,9},{9,1},{17,25},{25,17},{2,10},{10... | collective-permute-start | bytes 147464 | tf_op jit(solution)/shard_map/ppermute | solution.py:389
  36.0 4.1 %collective-permute-start.12 = (bf16[192,128]{1,0:T(8,128)(2,1)S(1)}, bf16[192,128]{1,0:T(8,128)(2,1)S(1)}, u32[]{:S(2)}, u32[]{:S(2)}) collective-permute-start(bf16[192,128]{1,0:T(8,128)(2,1)S(1)} %constant_dynamic-update-slice_fusion.refs_0_), channel_id=1, source_target_pairs={{0,16},{8,24},{16,0},{24,8},{1,17},{9,25},{17,1},{25,9},{2,18},{10... | collective-permute-start | bytes 147464 | tf_op jit(solution)/shard_map/ppermute | solution.py:389
  37.5 5.0 %collective-permute-start.13 = (bf16[192,128]{1,0:T(8,128)(2,1)S(1)}, bf16[192,128]{1,0:T(8,128)(2,1)S(1)}, u32[]{:S(2)}, u32[]{:S(2)}) collective-permute-start(bf16[192,128]{1,0:T(8,128)(2,1)S(1)} %constant_dynamic-update-slice_fusion.refs_0_), channel_id=1, source_target_pairs={{0,24},{8,16},{16,8},{24,0},{1,25},{9,17},{17,9},{25,1},{2,26},{10... | collective-permute-start | bytes 147464 | tf_op jit(solution)/shard_map/ppermute | solution.py:389
  43.5 4.5 %collective-permute-start.15 = (bf16[24,1024]{1,0:T(8,128)(2,1)S(1)}, bf16[24,1024]{1,0:T(8,128)(2,1)S(1)}, u32[]{:S(2)}, u32[]{:S(2)}) collective-permute-start(bf16[24,1024]{1,0:T(8,128)(2,1)S(1)} %get-tuple-element.64), channel_id=1, source_target_pairs={{0,2},{2,0},{4,6},{6,4},{1,3},{3,1},{5,7},{7,5},{8,10},{10,8},{12,... | collective-permute-start | bytes 147464 | tf_op jit(solution)/shard_map/ppermute | solution.py:389
  44.7 5.5 %collective-permute-start.16 = (bf16[24,1024]{1,0:T(8,128)(2,1)S(1)}, bf16[24,1024]{1,0:T(8,128)(2,1)S(1)}, u32[]{:S(2)}, u32[]{:S(2)}) collective-permute-start(bf16[24,1024]{1,0:T(8,128)(2,1)S(1)} %get-tuple-element.65), channel_id=1, source_target_pairs={{0,4},{2,6},{4,0},{6,2},{1,5},{3,7},{5,1},{7,3},{8,12},{10,14},{12... | collective-permute-start | bytes 147464 | tf_op jit(solution)/shard_map/ppermute | solution.py:389
  45.7 5.9 %collective-permute-start.17 = (bf16[24,1024]{1,0:T(8,128)(2,1)S(1)}, bf16[24,1024]{1,0:T(8,128)(2,1)S(1)}, u32[]{:S(2)}, u32[]{:S(2)}) collective-permute-start(bf16[24,1024]{1,0:T(8,128)(2,1)S(1)} %get-tuple-element.66), channel_id=1, source_target_pairs={{0,6},{2,4},{4,2},{6,0},{1,7},{3,5},{5,3},{7,1},{8,14},{10,12},{12... | collective-permute-start | bytes 147464 | tf_op jit(solution)/shard_map/ppermute | solution.py:389
  51.7 6.1 %collective-permute-start.18 = (bf16[24,1024]{1,0:T(8,128)(2,1)S(1)}, bf16[24,1024]{1,0:T(8,128)(2,1)S(1)}, u32[]{:S(2)}, u32[]{:S(2)}) collective-permute-start(bf16[24,1024]{1,0:T(8,128)(2,1)S(1)} %stepped_slice.1.refs_0_), channel_id=1, source_target_pairs={{0,8},{8,0},{16,24},{24,16},{1,9},{9,1},{17,25},{25,17},{2,10},{10... | collective-permute-start | bytes 147464 | tf_op jit(solution)/shard_map/ppermute | solution.py:389
  52.3 5.5 %collective-permute-start.19 = (bf16[24,1024]{1,0:T(8,128)(2,1)S(1)}, bf16[24,1024]{1,0:T(8,128)(2,1)S(1)}, u32[]{:S(2)}, u32[]{:S(2)}) collective-permute-start(bf16[24,1024]{1,0:T(8,128)(2,1)S(1)} %stepped_slice.1.refs_0_), channel_id=1, source_target_pairs={{0,16},{8,24},{16,0},{24,8},{1,17},{9,25},{17,1},{25,9},{2,18},{10... | collective-permute-start | bytes 147464 | tf_op jit(solution)/shard_map/ppermute | solution.py:389
  52.9 5.0 %collective-permute-start.20 = (bf16[24,1024]{1,0:T(8,128)(2,1)S(1)}, bf16[24,1024]{1,0:T(8,128)(2,1)S(1)}, u32[]{:S(2)}, u32[]{:S(2)}) collective-permute-start(bf16[24,1024]{1,0:T(8,128)(2,1)S(1)} %stepped_slice.1.refs_0_), channel_id=1, source_target_pairs={{0,24},{8,16},{16,8},{24,0},{1,25},{9,17},{17,9},{25,1},{2,26},{10... | collective-permute-start | bytes 147464 | tf_op jit(solution)/shard_map/ppermute | solution.py:389
  55.2 2.6 %copy-start.9 = (f32[24,4096]{1,0:T(8,128)S(1)}, f32[24,4096]{1,0:T(8,128)}, u32[]{:S(2)}) copy-start(f32[24,4096]{1,0:T(8,128)} %par_ref.1) | copy-start | bytes 1179652
  55.2 2.6 %copy-start.10 = (f32[24,4096]{1,0:T(8,128)S(1)}, f32[24,4096]{1,0:T(8,128)}, u32[]{:S(2)}) copy-start(f32[24,4096]{1,0:T(8,128)} %mom_ref.1) | copy-start | bytes 1179652
  (2 other events, 1.9 us)

commit v2 on v1

--- a/solution.py
+++ b/solution.py
@@ -14,7 +14,7 @@
 outer_rate = 0.7
 momentum_decay = 0.9
 
-VMEM_LIMIT = 48 * 1024 * 1024
+VMEM_LIMIT = 20 * 1024 * 1024
 
 
 def params(**more):
@@ -100,20 +100,38 @@
     return pl.ds(pl.multiple_of((index ^ k) * rows, 8), rows)
 
 
-def ssd_kernel(order, where_ref, rows_ref, bias_ref, decay_ref, *rest):
+def first_kernel(rows_ref, *refs):
+    refs[-1][...] = contract(stacked(refs[:-1]), rows_ref[...], ((1,), (1,)))
+
+
+def first_projection(rows_in, weights):
+    rows = sum(w.shape[0] for w in weights)
+    return pl.pallas_call(
+        first_kernel,
+        in_specs=whole_vmem(1 + len(weights)),
+        out_specs=pl.BlockSpec(memory_space=pltpu.VMEM),
+        out_shape=jax.ShapeDtypeStruct((rows, rows_in.shape[0]), jnp.float32),
+        compiler_params=params(),
+        name="first_projection",
+    )(rows_in, *weights)
+
+
+def ssd_kernel(order, first, where_ref, rows_ref, bias_ref, decay_ref, *rest):
     shards = len(order)
     cross_refs, enter_refs, rest = rest[:2], rest[2:4], rest[4:]
-    weight_refs = rest[:shards]
-    grad_ref, mine_ref, other_ref, proj_ref, col_ref, out_ref = rest[shards:]
+    first_ref, rest = (rest[0], rest[1:]) if first else (None, rest)
+    weight_refs, rest = rest[: shards - first], rest[shards - first :]
+    grad_ref, mine_ref, other_ref, proj_ref, col_ref, out_ref = rest
     block = rows_ref.shape[0]
     heads = bias_ref.shape[1]
     per = weight_refs[0].shape[0]
     arrived = contract(stacked(weight_refs), rows_ref[...], ((1,), (1,)))
-    for at, k in enumerate(order):
-        if shards > 1:
-            proj_ref[shard_rows(where_ref[1], k, per), :] = arrived[at * per : (at + 1) * per]
-        else:
-            proj_ref[...] = arrived
+    if shards == 1:
+        proj_ref[...] = arrived
+    else:
+        for at, k in enumerate(order):
+            source, line = (first_ref, at) if at < first else (arrived, at - first)
+            proj_ref[shard_rows(where_ref[1], k, per), :] = source[line * per : (line + 1) * per]
     key_t = proj_ref[:STATE, :]
     query_t = proj_ref[STATE : 2 * STATE, :]
     bias_t = jnp.broadcast_to(bias_ref[...], (block, heads)).T
@@ -200,14 +218,15 @@
     grad_ref[...] = proj_ref[...].astype(jnp.bfloat16)
 
 
-def ssd_backward(where, rows_in, step_bias, decay_log, cross, enter, weights, order):
+def ssd_backward(where, rows_in, step_bias, decay_log, cross, enter, first, weights, order):
     block = rows_in.shape[0]
     heads = step_bias.shape[0]
-    cols = sum(w.shape[0] for w in weights)
+    cols = len(order) * weights[0].shape[0]
     half = (cols // 2, block)
     return pl.pallas_call(
-        functools.partial(ssd_kernel, order),
-        in_specs=[pl.BlockSpec(memory_space=pltpu.SMEM)] + whole_vmem(7 + len(order)),
+        functools.partial(ssd_kernel, order, len(order) - len(weights)),
+        in_specs=[pl.BlockSpec(memory_space=pltpu.SMEM)]
+        + whole_vmem(7 + len(first) + len(weights)),
         out_specs=whole_vmem(3),
         out_shape=[
             jax.ShapeDtypeStruct((cols, block), jnp.bfloat16),
@@ -222,7 +241,7 @@
         compiler_params=params(),
         cost_estimate=pl.CostEstimate(flops=1, bytes_accessed=1, transcendentals=0),
         name="ssd_backward",
-    )(where, rows_in, step_bias.reshape(1, -1), decay_log.reshape(1, -1), *cross, *enter, *weights)
+    )(where, rows_in, step_bias.reshape(1, -1), decay_log.reshape(1, -1), *cross, *enter, *first, *weights)
 
 
 def block_grad_kernel(grad_ref, *refs):
@@ -395,10 +414,11 @@
     if fast:
         far = send(own, "line", 3)
         near = send(own, "line", 1)
-        order = (0, 2, 6, 4, 1, 3, 7, 5)
+        order = (0, 2, 6, 1, 3, 7, 4, 5)
     else:
         weights = [lax.all_gather(own, ("line", "core"), axis=0, tiled=True)]
         order = (0,)
+        first = 0
 
     early = [[], []]
     states = [start_state[b].reshape(seq_width, STATE) for b in range(blocks)]
@@ -415,10 +435,18 @@
         pieces = [pieces[0]] + send_each(pieces[1:], "rep")
         far, early[0] = lax.optimization_barrier((far, early[0]))
         middle = send(far, "line", 1)
-        twins = [send(own, "core", 1), send(near, "core", 1)]
-        middle, early[1], twins = lax.optimization_barrier((middle, early[1], twins))
-        twins = twins + [send(far, "core", 1), send(middle, "core", 1)]
-        weights = [own, near, far, middle] + twins
+        weights = [own, near, far] + [send(w, "core", 1) for w in (own, near, far)]
+        middle, early[1], weights = lax.optimization_barrier((middle, early[1], weights))
+        weights = weights + [middle, send(middle, "core", 1)]
+        first = 6
+
+    begun = []
+    if fast:
+        begun = [
+            first_projection(block_input[b * block : (b + 1) * block], weights[:first])
+            for b in range(blocks)
+        ]
+        begun, pieces[:-1] = lax.optimization_barrier((begun, pieces[:-1]))
 
     grads, mine, other = [], [], []
     for b in range(blocks):
@@ -430,7 +458,8 @@
             decay_log,
             [early[0][b][0], early[1][b][0]],
             [early[0][b][1], early[1][b][1]],
-            weights,
+            begun[b : b + 1],
+            weights[first:],
             order,
         )
         for kept, part in zip((grads, mine, other), parts):
@@ -454,13 +483,13 @@
         return (block_grad, new_params, new_momentum)
 
     tokens = blocks * block
-    other = send(other, "core", 1)
-    other, pieces = lax.optimization_barrier((other, pieces))
+    both = jnp.concatenate([mine, send(other, "core", 1)], axis=0)
+    plane = [both] + send_each([both] * (replicas - 1), "rep")
+    plane[-1], pieces[-1] = lax.optimization_barrier((plane[-1], pieces[-1]))
     twin = send(jnp.concatenate([p[:tokens] for p in pieces], axis=0), "core", 1)
-    both = jnp.concatenate([mine, other], axis=0)
-    plane = [both] + send_each([both] * (replicas - 1), "rep")
     sums = gradient_slice(where, plane, pieces, twin, chips)
     sums = [sums[0]] + send_each(sums[1:], "line")
+    sums, block_grad = lax.optimization_barrier((sums, block_grad))
     stepped = stepped_slice(sums, pieces)
     stepped = [stepped] + send_each([stepped] * (replicas - 1), "rep")
     new_params, new_momentum = outer_step(where, global_params, momentum, stepped)

time: 59.7 us -> 69.4 us (1.16)
  waiting for transfers between devices: 12.4 us -> 21.2 us
  starting transfers between devices: 23.4 us -> 25.1 us
  local copies, waits for them, and re-layouts: 6.32 us -> 5.36 us
    ppermute x21, waiting for transfers between devices: 12.4 us -> 21.2 us  [send(): return lax.ppermute(value, axis, [(i, i ^ k) for i in range(count)])]
    ppermute x21, starting transfers between devices: 23.4 us -> 25.1 us  [send(): return lax.ppermute(value, axis, [(i, i ^ k) for i in range(count)])]
    unnamed x27 -> x33, local copies, waits for them, and re-layouts: 4.19 us -> 3.26 us
    pallas_call x1 -> x2, Pallas kernels: 5.95 us -> 6.28 us  [the longest x1 4.78 us: ssd_backward(): pl.pallas_call(functools.partial(ssd_kernel, order, len(order) - len(weig...]
  transfers between devices with their start and end apart: 21 -> 21, of which waited for: 9 -> 11; matrix products, arithmetic and copies ran while one was open for 4% -> 3% of each run, Pallas kernels for 21% -> 18%
where the time goes in v2:
time: 69.4 us; the launch traced here: 69.1 us
  starting transfers between devices  25.1 us (36%)
  waiting for transfers between devices  21.2 us (31%)
  Pallas kernels  15.4 us (22%)
  local copies, waits for them, and re-layouts  5.36 us (8%)
  other arithmetic  1.25 us (2%)
  between operations  0.92 us (1%)
    ppermute x21, starting transfers between devices, send(): return lax.ppermute(value, axis, [(i, i ^ k) for i in range(count)])  25.1 us
    ppermute x21, waiting for transfers between devices, send(): return lax.ppermute(value, axis, [(i, i ^ k) for i in range(count)])  21.2 us
    pallas_call x1, Pallas kernels, ssd_backward(): pl.pallas_call(functools.partial(ssd_kernel, order, len(order) - len(weig...  4.78 us
    pallas_call x2, Pallas kernels, early_products(): pl.pallas_call(early_kernel, grid=(steps,), in_specs=[pl.BlockSpec((block...  3.33 us
    unnamed x33, local copies, waits for them, and re-layouts  3.26 us
    pallas_call x1, Pallas kernels, block_gradient(): pl.pallas_call(block_grad_kernel, in_specs=whole_vmem(1 + len(weights)),...  2.46 us
    another operation x1, local copies, waits for them, and re-layouts, on_device(): states = [start_state[b].reshape(seq_width, STATE) for b in range(blocks)]  2.05 us
    pallas_call x1, Pallas kernels, outer_step(): pl.pallas_call(outer_kernel, in_specs=[pl.BlockSpec(memory_space=pltpu.SM...  1.57 us
  transfers between devices with their start and end apart: 21, of which 11 were waited for; matrix products, arithmetic and copies ran while one was open for 3% of the time, Pallas kernels for 18%

profile of v2, /device:TPU:0, one launch (start us, length us, event | category | flops | bytes accessed | tf_op | source)
XLA Modules:
  0.0 69.1 jit_solution(11267483100210670568)
XLA Ops:
  0.6 1.1 %convert_bitcast_fusion.own_ref.refs_0_ = bf16[24,4096]{1,0:T(8,128)(2,1)S(1)} fusion(f32[1,24,4096]{2,1,0:T(8,128)} %param.15), kind=kLoop, calls=%fused_computation.1 | loop fusion | flops 98304 | bytes 589824 | tf_op jit(solution)/shard_map/convert_element_type | solution.py:391
  1.7 5.1 %collective-permute-start = (bf16[24,4096]{1,0:T(8,128)(2,1)S(1)}, bf16[24,4096]{1,0:T(8,128)(2,1)S(1)}, u32[]{:S(2)}, u32[]{:S(2)}) collective-permute-start(bf16[24,4096]{1,0:T(8,128)(2,1)S(1)} %convert_bitcast_fusion.own_ref.refs_0_), channel_id=1, source_target_pairs={{0,6},{2,4},{4,2},{6,0},{1,7},{3,5},{5,3},{7,1},{8,14},{10,12},{12... | collective-permute-start | bytes 589832 | tf_op jit(solution)/shard_map/ppermute | solution.py:408
  6.9 2.1 %reshape_squeeze.3.state_ref = bf16[4096,64]{1,0:T(8,128)(2,1)S(1)} reshape(bf16[1,64,4096]{2,1,0:T(8,128)(2,1)} %param.12) | data formatting | bytes 1048576 | tf_op jit(solution)/shard_map/reshape;squeeze | solution.py:424
  9.0 1.2 %copy-done.2 = bf16[128,4096]{1,0:T(8,128)(2,1)S(1)} copy-done((bf16[128,4096]{1,0:T(8,128)(2,1)S(1)}, bf16[128,4096]{1,0:T(8,128)(2,1)}, u32[]{:S(2)}) %copy-start.2) | copy-done | bytes 1048600
  10.2 1.7 %early_products.2 = (bf16[32,128,128]{2,1,0:T(8,128)(2,1)S(1)}, f32[128,2048]{1,0:T(8,128)S(1)}) custom-call(bf16[128,4096]{1,0:T(8,128)(2,1)S(1)} %copy-done.1, bf16[128,4096]{1,0:T(8,128)(2,1)S(1)} %copy-done.2, bf16[4096,64]{1,0:T(8,128)(2,1)S(1)} %reshape_squeeze.3.state_ref), custom_call_target="tpu_custom_call" | custom-call | flops 1 | bytes 1 | tf_op jit(solution)/shard_map/early_products/pallas_call | solution.py:71
  11.8 1.0 %copy-done.8 = bf16[32,128,128]{2,1,0:T(8,128)(2,1)} copy-done((bf16[32,128,128]{2,1,0:T(8,128)(2,1)}, bf16[32,128,128]{2,1,0:T(8,128)(2,1)S(1)}, u32[]{:S(2)}) %copy-start.8) | copy-done | bytes 1048600
  12.8 1.0 %copy-done.10 = f32[128,2048]{1,0:T(8,128)} copy-done((f32[128,2048]{1,0:T(8,128)}, f32[128,2048]{1,0:T(8,128)S(1)}, u32[]{:S(2)}) %copy-start.10) | copy-done | bytes 1048600
  13.9 0.6 column_pieces.1
  14.5 2.1 %collective-permute-start.1 = (bf16[24,4096]{1,0:T(8,128)(2,1)S(1)}, bf16[24,4096]{1,0:T(8,128)(2,1)S(1)}, u32[]{:S(2)}, u32[]{:S(2)}) collective-permute-start(bf16[24,4096]{1,0:T(8,128)(2,1)S(1)} %collective-permute-done.refs_2_), channel_id=1, source_target_pairs={{0,2},{2,0},{4,6},{6,4},{1,3},{3,1},{5,7},{7,5},{8,10},{10,8},{12,... | collective-permute-start | bytes 589832 | tf_op jit(solution)/shard_map/ppermute | solution.py:408
  17.2 1.5 %collective-permute-start.6 = (bf16[152,1024]{1,0:T(8,128)(2,1)S(1)}, bf16[152,1024]{1,0:T(8,128)(2,1)S(1)}, u32[]{:S(2)}, u32[]{:S(2)}) collective-permute-start(bf16[152,1024]{1,0:T(8,128)(2,1)S(1)} %get-tuple-element.48), channel_id=1, source_target_pairs={{0,8},{8,0},{16,24},{24,16},{1,9},{9,1},{17,25},{25,17},{2,10},{10... | collective-permute-start | bytes 933896 | tf_op jit(solution)/shard_map/ppermute | solution.py:408
  18.6 1.5 %collective-permute-start.7 = (bf16[152,1024]{1,0:T(8,128)(2,1)S(1)}, bf16[152,1024]{1,0:T(8,128)(2,1)S(1)}, u32[]{:S(2)}, u32[]{:S(2)}) collective-permute-start(bf16[152,1024]{1,0:T(8,128)(2,1)S(1)} %get-tuple-element.49), channel_id=1, source_target_pairs={{0,16},{8,24},{16,0},{24,8},{1,17},{9,25},{17,1},{25,9},{2,18},{10... | collective-permute-start | bytes 933896 | tf_op jit(solution)/shard_map/ppermute | solution.py:408
  20.2 1.7 %early_products.3 = (bf16[32,128,128]{2,1,0:T(8,128)(2,1)S(1)}, f32[128,2048]{1,0:T(8,128)S(1)}) custom-call(bf16[128,4096]{1,0:T(8,128)(2,1)S(1)} %copy-done.1, bf16[128,4096]{1,0:T(8,128)(2,1)S(1)} %copy-done.3, bf16[4096,64]{1,0:T(8,128)(2,1)S(1)} %reshape_squeeze.3.state_ref), custom_call_target="tpu_custom_call" | custom-call | flops 1 | bytes 1 | tf_op jit(solution)/shard_map/early_products/pallas_call | solution.py:71
  22.3 2.5 %collective-permute-start.13 = (bf16[152,1024]{1,0:T(8,128)(2,1)S(1)}, bf16[152,1024]{1,0:T(8,128)(2,1)S(1)}, u32[]{:S(2)}, u32[]{:S(2)}) collective-permute-start(bf16[152,1024]{1,0:T(8,128)(2,1)S(1)} %get-tuple-element.50), channel_id=1, source_target_pairs={{0,24},{8,16},{16,8},{24,0},{1,25},{9,17},{17,9},{25,1},{2,26},{10... | collective-permute-start | bytes 933896 | tf_op jit(solution)/shard_map/ppermute | solution.py:408
  24.9 1.5 %first_projection.1.rest_4_ = f32[144,128]{1,0:T(8,128)S(1)} custom-call(bf16[128,4096]{1,0:T(8,128)(2,1)S(1)} %copy-done, bf16[24,4096]{1,0:T(8,128)(2,1)S(1)} %convert_bitcast_fusion.own_ref.refs_0_, bf16[24,4096]{1,0:T(8,128)(2,1)} %collective-permute-done.2.refs_1_, bf16[24,4096]{1,0:T(8,128)(2,1)S(1)} %collective-permute-done.refs_2_, ...), custom_call_target="tpu_custom_call" | custom-call | tf_op jit(solution)/shard_map/first_projection/pallas_call | solution.py:109
  26.8 7.7 %collective-permute-done.7.refs_6_ = bf16[152,1024]{1,0:T(8,128)(2,1)S(1)} collective-permute-done((bf16[152,1024]{1,0:T(8,128)(2,1)S(1)}, bf16[152,1024]{1,0:T(8,128)(2,1)S(1)}, u32[]{:S(2)}, u32[]{:S(2)}) %collective-permute-start.7) | collective-permute-done | bytes 311328 | tf_op jit(solution)/shard_map/ppermute | solution.py:408
  34.6 4.8 %ssd_backward.1 = (bf16[192,128]{1,0:T(8,128)(2,1)S(1)}, bf16[96,128]{1,0:T(8,128)(2,1)S(1)}, bf16[96,128]{1,0:T(8,128)(2,1)S(1)}) custom-call(s32[2]{0:T(128)S(1)} %pad_add_fusion.where_ref, bf16[128,4096]{1,0:T(8,128)(2,1)S(1)} %copy-done, f32[1,64]{1,0:T(1,128)S(1)} %bitcast.6, f32[1,64]{1,0:T(1,128)S(1)} %bitcast.7, bf16[32,128,128]{2,1,0:T(8,128)(2,1)S(1)} %copy-done.9, ...), custom_call_target="tpu_custom_call" | custom-call | flops 1 | bytes 1 | tf_op jit(solution)/shard_map/ssd_backward/pallas_call | solution.py:226
  39.5 1.2 %collective-permute-done.9 = bf16[96,128]{1,0:T(8,128)(2,1)S(1)} collective-permute-done((bf16[96,128]{1,0:T(8,128)(2,1)S(1)}, bf16[96,128]{1,0:T(8,128)(2,1)S(1)}, u32[]{:S(2)}, u32[]{:S(2)}) %collective-permute-start.9) | collective-permute-done | bytes 24608 | tf_op jit(solution)/shard_map/ppermute | solution.py:408
  40.6 1.5 %collective-permute-start.12 = (bf16[192,128]{1,0:T(8,128)(2,1)S(1)}, bf16[192,128]{1,0:T(8,128)(2,1)S(1)}, u32[]{:S(2)}, u32[]{:S(2)}) collective-permute-start(bf16[192,128]{1,0:T(8,128)(2,1)S(1)} %constant_dynamic-update-slice_fusion.refs_0_), channel_id=1, source_target_pairs={{0,24},{8,16},{16,8},{24,0},{1,25},{9,17},{17,9},{25,1},{2,26},{10... | collective-permute-start | bytes 147464 | tf_op jit(solution)/shard_map/ppermute | solution.py:408
  42.2 3.4 %collective-permute-done.12.refs_3_ = bf16[192,128]{1,0:T(8,128)(2,1)S(1)} collective-permute-done((bf16[192,128]{1,0:T(8,128)(2,1)S(1)}, bf16[192,128]{1,0:T(8,128)(2,1)S(1)}, u32[]{:S(2)}, u32[]{:S(2)}) %collective-permute-start.12) | collective-permute-done | bytes 49184 | tf_op jit(solution)/shard_map/ppermute | solution.py:408
  46.0 2.0 %collective-permute-start.11 = (bf16[192,128]{1,0:T(8,128)(2,1)S(1)}, bf16[192,128]{1,0:T(8,128)(2,1)S(1)}, u32[]{:S(2)}, u32[]{:S(2)}) collective-permute-start(bf16[192,128]{1,0:T(8,128)(2,1)S(1)} %constant_dynamic-update-slice_fusion.refs_0_), channel_id=1, source_target_pairs={{0,16},{8,24},{16,0},{24,8},{1,17},{9,25},{17,1},{25,9},{2,18},{10... | collective-permute-start | bytes 147464 | tf_op jit(solution)/shard_map/ppermute | solution.py:408
  48.0 2.0 %collective-permute-done.10.refs_1_ = bf16[192,128]{1,0:T(8,128)(2,1)S(1)} collective-permute-done((bf16[192,128]{1,0:T(8,128)(2,1)S(1)}, bf16[192,128]{1,0:T(8,128)(2,1)S(1)}, u32[]{:S(2)}, u32[]{:S(2)}) %collective-permute-start.10) | collective-permute-done | bytes 49184 | tf_op jit(solution)/shard_map/ppermute | solution.py:408
  50.1 1.0 %gradient_slice.1 = (bf16[24,1024]{1,0:T(8,128)(2,1)S(1)}, bf16[24,1024]{1,0:T(8,128)(2,1)S(1)}, bf16[24,1024]{1,0:T(8,128)(2,1)S(1)}, bf16[24,1024]{1,0:T(8,128)(2,1)S(1)}) custom-call(s32[2]{0:T(128)S(1)} %pad_add_fusion.where_ref, bf16[192,128]{1,0:T(8,128)(2,1)S(1)} %constant_dynamic-update-slice_fusion.refs_0_, ...), custom_call_target="tpu_custom_call" | custom-call | tf_op jit(solution)/shard_map/gradient_slice/pallas_call | solution.py:315
  51.1 1.1 %collective-permute-start.15 = (bf16[24,1024]{1,0:T(8,128)(2,1)S(1)}, bf16[24,1024]{1,0:T(8,128)(2,1)S(1)}, u32[]{:S(2)}, u32[]{:S(2)}) collective-permute-start(bf16[24,1024]{1,0:T(8,128)(2,1)S(1)} %get-tuple-element.78), channel_id=1, source_target_pairs={{0,2},{2,0},{4,6},{6,4},{1,3},{3,1},{5,7},{7,5},{8,10},{10,8},{12,... | collective-permute-start | bytes 147464 | tf_op jit(solution)/shard_map/ppermute | solution.py:408
  52.2 0.9 %collective-permute-start.16 = (bf16[24,1024]{1,0:T(8,128)(2,1)S(1)}, bf16[24,1024]{1,0:T(8,128)(2,1)S(1)}, u32[]{:S(2)}, u32[]{:S(2)}) collective-permute-start(bf16[24,1024]{1,0:T(8,128)(2,1)S(1)} %get-tuple-element.79), channel_id=1, source_target_pairs={{0,4},{2,6},{4,0},{6,2},{1,5},{3,7},{5,1},{7,3},{8,12},{10,14},{12... | collective-permute-start | bytes 147464 | tf_op jit(solution)/shard_map/ppermute | solution.py:408
  53.1 2.5 %collective-permute-start.17 = (bf16[24,1024]{1,0:T(8,128)(2,1)S(1)}, bf16[24,1024]{1,0:T(8,128)(2,1)S(1)}, u32[]{:S(2)}, u32[]{:S(2)}) collective-permute-start(bf16[24,1024]{1,0:T(8,128)(2,1)S(1)} %get-tuple-element.80), channel_id=1, source_target_pairs={{0,6},{2,4},{4,2},{6,0},{1,7},{3,5},{5,3},{7,1},{8,14},{10,12},{12... | collective-permute-start | bytes 147464 | tf_op jit(solution)/shard_map/ppermute | solution.py:408
  55.6 2.5 %block_gradient.1 = bf16[128,4096]{1,0:T(8,128)(2,1)} custom-call(bf16[192,128]{1,0:T(8,128)(2,1)S(1)} %get-tuple-element.81.grad_ref, bf16[24,4096]{1,0:T(8,128)(2,1)S(1)} %convert_bitcast_fusion.own_ref.refs_0_, bf16[24,4096]{1,0:T(8,128)(2,1)} %collective-permute-done.2.refs_1_, bf16[24,4096]{1,0:T(8,128)(2,1)S(1)} %collective-permute-done.refs_2_, ...), custom_call_target="tpu_custom_call" | custom-call | flops 201326592 | bytes 3145728 | tf_op jit(solution)/shard_map/block_gradient/pallas_call | solution.py:256
  58.1 1.0 %collective-permute-done.17.refs_3_ = bf16[24,1024]{1,0:T(8,128)(2,1)S(1)} collective-permute-done((bf16[24,1024]{1,0:T(8,128)(2,1)S(1)}, bf16[24,1024]{1,0:T(8,128)(2,1)S(1)}, u32[]{:S(2)}, u32[]{:S(2)}) %collective-permute-start.17) | collective-permute-done | bytes 49184 | tf_op jit(solution)/shard_map/ppermute | solution.py:408
  59.1 1.9 %collective-permute-start.18 = (bf16[24,1024]{1,0:T(8,128)(2,1)S(1)}, bf16[24,1024]{1,0:T(8,128)(2,1)S(1)}, u32[]{:S(2)}, u32[]{:S(2)}) collective-permute-start(bf16[24,1024]{1,0:T(8,128)(2,1)S(1)} %stepped_slice.1.refs_0_), channel_id=1, source_target_pairs={{0,8},{8,0},{16,24},{24,16},{1,9},{9,1},{17,25},{25,17},{2,10},{10... | collective-permute-start | bytes 147464 | tf_op jit(solution)/shard_map/ppermute | solution.py:408
  61.0 1.5 %collective-permute-start.19 = (bf16[24,1024]{1,0:T(8,128)(2,1)S(1)}, bf16[24,1024]{1,0:T(8,128)(2,1)S(1)}, u32[]{:S(2)}, u32[]{:S(2)}) collective-permute-start(bf16[24,1024]{1,0:T(8,128)(2,1)S(1)} %stepped_slice.1.refs_0_), channel_id=1, source_target_pairs={{0,16},{8,24},{16,0},{24,8},{1,17},{9,25},{17,1},{25,9},{2,18},{10... | collective-permute-start | bytes 147464 | tf_op jit(solution)/shard_map/ppermute | solution.py:408
  63.3 1.8 %collective-permute-done.19.refs_2_ = bf16[24,1024]{1,0:T(8,128)(2,1)S(1)} collective-permute-done((bf16[24,1024]{1,0:T(8,128)(2,1)S(1)}, bf16[24,1024]{1,0:T(8,128)(2,1)S(1)}, u32[]{:S(2)}, u32[]{:S(2)}) %collective-permute-start.19) | collective-permute-done | bytes 49184 | tf_op jit(solution)/shard_map/ppermute | solution.py:408
  65.1 2.4 %collective-permute-done.20.refs_3_ = bf16[24,1024]{1,0:T(8,128)(2,1)S(1)} collective-permute-done((bf16[24,1024]{1,0:T(8,128)(2,1)S(1)}, bf16[24,1024]{1,0:T(8,128)(2,1)S(1)}, u32[]{:S(2)}, u32[]{:S(2)}) %collective-permute-start.20) | collective-permute-done | bytes 49184 | tf_op jit(solution)/shard_map/ppermute | solution.py:408
  67.6 1.6 %outer_step.1 = (f32[24,4096]{1,0:T(8,128)}, f32[24,4096]{1,0:T(8,128)}) custom-call(s32[2]{0:T(128)S(1)} %pad_add_fusion.where_ref, f32[24,4096]{1,0:T(8,128)S(1)} %copy-done.12, f32[24,4096]{1,0:T(8,128)S(1)} %copy-done.13, bf16[24,1024]{1,0:T(8,128)(2,1)S(1)} %stepped_slice.1.refs_0_, bf16[24,1024]{1,0:T(8,128)(2,1)S(1)} %collective-permute-done.18.refs_1_, ...), custom_call_target="tpu_custom_call" | custom-call | tf_op jit(solution)/shard_map/outer_step/pallas_call | solution.py:365
  (63 shorter events, 2.8 us)
Async XLA Ops:
  0.6 8.3 %copy-start.1 = (bf16[128,4096]{1,0:T(8,128)(2,1)S(1)}, bf16[128,4096]{1,0:T(8,128)(2,1)}, u32[]{:S(2)}) copy-start(bf16[128,4096]{1,0:T(8,128)(2,1)} %cot_ref.3) | copy-start | bytes 3145732
  1.7 12.8 %collective-permute-start = (bf16[24,4096]{1,0:T(8,128)(2,1)S(1)}, bf16[24,4096]{1,0:T(8,128)(2,1)S(1)}, u32[]{:S(2)}, u32[]{:S(2)}) collective-permute-start(bf16[24,4096]{1,0:T(8,128)(2,1)S(1)} %convert_bitcast_fusion.own_ref.refs_0_), channel_id=1, source_target_pairs={{0,6},{2,4},{4,2},{6,0},{1,7},{3,5},{5,3},{7,1},{8,14},{10,12},{12... | collective-permute-start | bytes 589832 | tf_op jit(solution)/shard_map/ppermute | solution.py:408
  6.9 9.8 %collective-permute-start.2 = (bf16[24,4096]{1,0:T(8,128)(2,1)S(1)}, bf16[24,4096]{1,0:T(8,128)(2,1)}, u32[]{:S(2)}, u32[]{:S(2)}) collective-permute-start(bf16[24,4096]{1,0:T(8,128)(2,1)S(1)} %convert_bitcast_fusion.own_ref.refs_0_), channel_id=1, source_target_pairs={{0,2},{2,0},{4,6},{6,4},{1,3},{3,1},{5,7},{7,5},{8,10},{10,8},{12,... | collective-permute-start | bytes 589832 | tf_op jit(solution)/shard_map/ppermute | solution.py:408
  6.9 11.8 %collective-permute-start.3 = (bf16[24,4096]{1,0:T(8,128)(2,1)S(1)}, bf16[24,4096]{1,0:T(8,128)(2,1)}, u32[]{:S(2)}, u32[]{:S(2)}) collective-permute-start(bf16[24,4096]{1,0:T(8,128)(2,1)S(1)} %convert_bitcast_fusion.own_ref.refs_0_), channel_id=1, source_target_pairs={{0,1},{1,0},{2,3},{3,2},{4,5},{5,4},{6,7},{7,6},{8,9},{9,8},{10,11... | collective-permute-start | bytes 589832 | tf_op jit(solution)/shard_map/ppermute | solution.py:408
  13.8 6.3 %copy-start.3 = (bf16[128,4096]{1,0:T(8,128)(2,1)S(1)}, bf16[128,4096]{1,0:T(8,128)(2,1)}, u32[]{:S(2)}) copy-start(bf16[128,4096]{1,0:T(8,128)(2,1)} %val_ref.3) | copy-start | bytes 3145732
  14.5 7.7 %collective-permute-start.1 = (bf16[24,4096]{1,0:T(8,128)(2,1)S(1)}, bf16[24,4096]{1,0:T(8,128)(2,1)S(1)}, u32[]{:S(2)}, u32[]{:S(2)}) collective-permute-start(bf16[24,4096]{1,0:T(8,128)(2,1)S(1)} %collective-permute-done.refs_2_), channel_id=1, source_target_pairs={{0,2},{2,0},{4,6},{6,4},{1,3},{3,1},{5,7},{7,5},{8,10},{10,8},{12,... | collective-permute-start | bytes 589832 | tf_op jit(solution)/shard_map/ppermute | solution.py:408
  16.6 5.6 %collective-permute-start.4 = (bf16[24,4096]{1,0:T(8,128)(2,1)}, bf16[24,4096]{1,0:T(8,128)(2,1)S(1)}, u32[]{:S(2)}, u32[]{:S(2)}) collective-permute-start(bf16[24,4096]{1,0:T(8,128)(2,1)} %collective-permute-done.2.refs_1_), channel_id=1, source_target_pairs={{0,1},{1,0},{2,3},{3,2},{4,5},{5,4},{6,7},{7,6},{8,9},{9,8},{10,11... | collective-permute-start | bytes 589832 | tf_op jit(solution)/shard_map/ppermute | solution.py:408
  16.9 5.3 %collective-permute-start.5 = (bf16[24,4096]{1,0:T(8,128)(2,1)S(1)}, bf16[24,4096]{1,0:T(8,128)(2,1)S(1)}, u32[]{:S(2)}, u32[]{:S(2)}) collective-permute-start(bf16[24,4096]{1,0:T(8,128)(2,1)S(1)} %collective-permute-done.refs_2_), channel_id=1, source_target_pairs={{0,1},{1,0},{2,3},{3,2},{4,5},{5,4},{6,7},{7,6},{8,9},{9,8},{10,11... | collective-permute-start | bytes 589832 | tf_op jit(solution)/shard_map/ppermute | solution.py:408
  17.2 9.7 %collective-permute-start.6 = (bf16[152,1024]{1,0:T(8,128)(2,1)S(1)}, bf16[152,1024]{1,0:T(8,128)(2,1)S(1)}, u32[]{:S(2)}, u32[]{:S(2)}) collective-permute-start(bf16[152,1024]{1,0:T(8,128)(2,1)S(1)} %get-tuple-element.48), channel_id=1, source_target_pairs={{0,8},{8,0},{16,24},{24,16},{1,9},{9,1},{17,25},{25,17},{2,10},{10... | collective-permute-start | bytes 933896 | tf_op jit(solution)/shard_map/ppermute | solution.py:408
  18.6 15.9 %collective-permute-start.7 = (bf16[152,1024]{1,0:T(8,128)(2,1)S(1)}, bf16[152,1024]{1,0:T(8,128)(2,1)S(1)}, u32[]{:S(2)}, u32[]{:S(2)}) collective-permute-start(bf16[152,1024]{1,0:T(8,128)(2,1)S(1)} %get-tuple-element.49), channel_id=1, source_target_pairs={{0,16},{8,24},{16,0},{24,8},{1,17},{9,25},{17,1},{25,9},{2,18},{10... | collective-permute-start | bytes 933896 | tf_op jit(solution)/shard_map/ppermute | solution.py:408
  22.2 12.3 %copy-start.9 = (bf16[32,128,128]{2,1,0:T(8,128)(2,1)S(1)}, bf16[32,128,128]{2,1,0:T(8,128)(2,1)}, u32[]{:S(2)}) copy-start(bf16[32,128,128]{2,1,0:T(8,128)(2,1)} %copy-done.8) | copy-start | bytes 3145732
  22.2 12.3 %copy-start.11 = (f32[128,2048]{1,0:T(8,128)S(1)}, f32[128,2048]{1,0:T(8,128)}, u32[]{:S(2)}) copy-start(f32[128,2048]{1,0:T(8,128)} %copy-done.10) | copy-start | bytes 3145732
  22.2 12.3 %copy-start.14 = (f32[64]{0:T(128)S(1)}, f32[64]{0:T(128)}, u32[]{:S(2)}) copy-start(f32[64]{0:T(128)} %param.13) | copy-start | bytes 772
  22.2 12.3 %copy-start.15 = (f32[64]{0:T(128)S(1)}, f32[64]{0:T(128)}, u32[]{:S(2)}) copy-start(f32[64]{0:T(128)} %param.14) | copy-start | bytes 772
  22.3 12.3 %collective-permute-start.8 = (bf16[24,4096]{1,0:T(8,128)(2,1)S(1)}, bf16[24,4096]{1,0:T(8,128)(2,1)S(1)}, u32[]{:S(2)}, u32[]{:S(2)}) collective-permute-start(bf16[24,4096]{1,0:T(8,128)(2,1)S(1)} %collective-permute-done.1.rest_5_.refs_6_), channel_id=1, source_target_pairs={{0,1},{1,0},{2,3},{3,2},{4,5},{5,4},{6,7},{7,6},{8,9},{9,8},{10,11... | collective-permute-start | bytes 589832 | tf_op jit(solution)/shard_map/ppermute | solution.py:408
  22.3 19.8 %collective-permute-start.13 = (bf16[152,1024]{1,0:T(8,128)(2,1)S(1)}, bf16[152,1024]{1,0:T(8,128)(2,1)S(1)}, u32[]{:S(2)}, u32[]{:S(2)}) collective-permute-start(bf16[152,1024]{1,0:T(8,128)(2,1)S(1)} %get-tuple-element.50), channel_id=1, source_target_pairs={{0,24},{8,16},{16,8},{24,0},{1,25},{9,17},{17,9},{25,1},{2,26},{10... | collective-permute-start | bytes 933896 | tf_op jit(solution)/shard_map/ppermute | solution.py:408
  26.8 15.3 %copy-start.4 = (bf16[152,1024]{1,0:T(8,128)(2,1)}, bf16[152,1024]{1,0:T(8,128)(2,1)S(1)}, u32[]{:S(2)}) copy-start(bf16[152,1024]{1,0:T(8,128)(2,1)S(1)} %collective-permute-done.6.refs_5_) | copy-start | bytes 933892
  34.5 7.6 %copy-start.6 = (bf16[152,1024]{1,0:T(8,128)(2,1)}, bf16[152,1024]{1,0:T(8,128)(2,1)S(1)}, u32[]{:S(2)}) copy-start(bf16[152,1024]{1,0:T(8,128)(2,1)S(1)} %collective-permute-done.7.refs_6_) | copy-start | bytes 933892
  39.4 1.3 %collective-permute-start.9 = (bf16[96,128]{1,0:T(8,128)(2,1)S(1)}, bf16[96,128]{1,0:T(8,128)(2,1)S(1)}, u32[]{:S(2)}, u32[]{:S(2)}) collective-permute-start(bf16[96,128]{1,0:T(8,128)(2,1)S(1)} %get-tuple-element.71), channel_id=1, source_target_pairs={{0,1},{1,0},{2,3},{3,2},{4,5},{5,4},{6,7},{7,6},{8,9},{9,8},{10,11... | collective-permute-start | bytes 73736 | tf_op jit(solution)/shard_map/ppermute | solution.py:408
  40.6 5.0 %collective-permute-start.12 = (bf16[192,128]{1,0:T(8,128)(2,1)S(1)}, bf16[192,128]{1,0:T(8,128)(2,1)S(1)}, u32[]{:S(2)}, u32[]{:S(2)}) collective-permute-start(bf16[192,128]{1,0:T(8,128)(2,1)S(1)} %constant_dynamic-update-slice_fusion.refs_0_), channel_id=1, source_target_pairs={{0,24},{8,16},{16,8},{24,0},{1,25},{9,17},{17,9},{25,1},{2,26},{10... | collective-permute-start | bytes 147464 | tf_op jit(solution)/shard_map/ppermute | solution.py:408
  45.7 4.4 %copy-start.5 = (bf16[152,1024]{1,0:T(8,128)(2,1)S(1)}, bf16[152,1024]{1,0:T(8,128)(2,1)}, u32[]{:S(2)}) copy-start(bf16[152,1024]{1,0:T(8,128)(2,1)} %copy-done.4) | copy-start | bytes 933892
  45.8 4.3 %collective-permute-start.14 = (bf16[512,1024]{1,0:T(8,128)(2,1)S(1)}, bf16[512,1024]{1,0:T(8,128)(2,1)S(1)}, u32[]{:S(2)}, u32[]{:S(2)}) collective-permute-start(bf16[512,1024]{1,0:T(8,128)(2,1)S(1)} %pad_maximum_fusion), channel_id=1, source_target_pairs={{0,1},{1,0},{2,3},{3,2},{4,5},{5,4},{6,7},{7,6},{8,9},{9,8},{10,11... | collective-permute-start | bytes 3145736 | tf_op jit(solution)/shard_map/ppermute | solution.py:408
  45.8 4.2 %collective-permute-start.10 = (bf16[192,128]{1,0:T(8,128)(2,1)S(1)}, bf16[192,128]{1,0:T(8,128)(2,1)S(1)}, u32[]{:S(2)}, u32[]{:S(2)}) collective-permute-start(bf16[192,128]{1,0:T(8,128)(2,1)S(1)} %constant_dynamic-update-slice_fusion.refs_0_), channel_id=1, source_target_pairs={{0,8},{8,0},{16,24},{24,16},{1,9},{9,1},{17,25},{25,17},{2,10},{10... | collective-permute-start | bytes 147464 | tf_op jit(solution)/shard_map/ppermute | solution.py:408
  46.0 4.1 %collective-permute-start.11 = (bf16[192,128]{1,0:T(8,128)(2,1)S(1)}, bf16[192,128]{1,0:T(8,128)(2,1)S(1)}, u32[]{:S(2)}, u32[]{:S(2)}) collective-permute-start(bf16[192,128]{1,0:T(8,128)(2,1)S(1)} %constant_dynamic-update-slice_fusion.refs_0_), channel_id=1, source_target_pairs={{0,16},{8,24},{16,0},{24,8},{1,17},{9,25},{17,1},{25,9},{2,18},{10... | collective-permute-start | bytes 147464 | tf_op jit(solution)/shard_map/ppermute | solution.py:408
  51.1 6.9 %collective-permute-start.15 = (bf16[24,1024]{1,0:T(8,128)(2,1)S(1)}, bf16[24,1024]{1,0:T(8,128)(2,1)S(1)}, u32[]{:S(2)}, u32[]{:S(2)}) collective-permute-start(bf16[24,1024]{1,0:T(8,128)(2,1)S(1)} %get-tuple-element.78), channel_id=1, source_target_pairs={{0,2},{2,0},{4,6},{6,4},{1,3},{3,1},{5,7},{7,5},{8,10},{10,8},{12,... | collective-permute-start | bytes 147464 | tf_op jit(solution)/shard_map/ppermute | solution.py:408
  52.2 5.9 %collective-permute-start.16 = (bf16[24,1024]{1,0:T(8,128)(2,1)S(1)}, bf16[24,1024]{1,0:T(8,128)(2,1)S(1)}, u32[]{:S(2)}, u32[]{:S(2)}) collective-permute-start(bf16[24,1024]{1,0:T(8,128)(2,1)S(1)} %get-tuple-element.79), channel_id=1, source_target_pairs={{0,4},{2,6},{4,0},{6,2},{1,5},{3,7},{5,1},{7,3},{8,12},{10,14},{12... | collective-permute-start | bytes 147464 | tf_op jit(solution)/shard_map/ppermute | solution.py:408
  53.1 6.0 %collective-permute-start.17 = (bf16[24,1024]{1,0:T(8,128)(2,1)S(1)}, bf16[24,1024]{1,0:T(8,128)(2,1)S(1)}, u32[]{:S(2)}, u32[]{:S(2)}) collective-permute-start(bf16[24,1024]{1,0:T(8,128)(2,1)S(1)} %get-tuple-element.80), channel_id=1, source_target_pairs={{0,6},{2,4},{4,2},{6,0},{1,7},{3,5},{5,3},{7,1},{8,14},{10,12},{12... | collective-permute-start | bytes 147464 | tf_op jit(solution)/shard_map/ppermute | solution.py:408
  58.1 9.5 %copy-start.12 = (f32[24,4096]{1,0:T(8,128)S(1)}, f32[24,4096]{1,0:T(8,128)}, u32[]{:S(2)}) copy-start(f32[24,4096]{1,0:T(8,128)} %par_ref.1) | copy-start | bytes 1179652
  58.1 9.5 %copy-start.13 = (f32[24,4096]{1,0:T(8,128)S(1)}, f32[24,4096]{1,0:T(8,128)}, u32[]{:S(2)}) copy-start(f32[24,4096]{1,0:T(8,128)} %mom_ref.1) | copy-start | bytes 1179652
  59.1 4.2 %collective-permute-start.18 = (bf16[24,1024]{1,0:T(8,128)(2,1)S(1)}, bf16[24,1024]{1,0:T(8,128)(2,1)S(1)}, u32[]{:S(2)}, u32[]{:S(2)}) collective-permute-start(bf16[24,1024]{1,0:T(8,128)(2,1)S(1)} %stepped_slice.1.refs_0_), channel_id=1, source_target_pairs={{0,8},{8,0},{16,24},{24,16},{1,9},{9,1},{17,25},{25,17},{2,10},{10... | collective-permute-start | bytes 147464 | tf_op jit(solution)/shard_map/ppermute | solution.py:408
  61.0 4.1 %collective-permute-start.19 = (bf16[24,1024]{1,0:T(8,128)(2,1)S(1)}, bf16[24,1024]{1,0:T(8,128)(2,1)S(1)}, u32[]{:S(2)}, u32[]{:S(2)}) collective-permute-start(bf16[24,1024]{1,0:T(8,128)(2,1)S(1)} %stepped_slice.1.refs_0_), channel_id=1, source_target_pairs={{0,16},{8,24},{16,0},{24,8},{1,17},{9,25},{17,1},{25,9},{2,18},{10... | collective-permute-start | bytes 147464 | tf_op jit(solution)/shard_map/ppermute | solution.py:408
  62.6 5.0 %collective-permute-start.20 = (bf16[24,1024]{1,0:T(8,128)(2,1)S(1)}, bf16[24,1024]{1,0:T(8,128)(2,1)S(1)}, u32[]{:S(2)}, u32[]{:S(2)}) collective-permute-start(bf16[24,1024]{1,0:T(8,128)(2,1)S(1)} %stepped_slice.1.refs_0_), channel_id=1, source_target_pairs={{0,24},{8,16},{16,8},{24,0},{1,25},{9,17},{17,9},{25,1},{2,26},{10... | collective-permute-start | bytes 147464 | tf_op jit(solution)/shard_map/ppermute | solution.py:408
  (7 other events, 18.4 us)

commit v3 on v2

--- a/solution.py
+++ b/solution.py
@@ -112,6 +112,7 @@
         out_specs=pl.BlockSpec(memory_space=pltpu.VMEM),
         out_shape=jax.ShapeDtypeStruct((rows, rows_in.shape[0]), jnp.float32),
         compiler_params=params(),
+        cost_estimate=pl.CostEstimate(flops=1, bytes_accessed=1, transcendentals=0),
         name="first_projection",
     )(rows_in, *weights)
 
@@ -386,6 +387,10 @@
     momentum,
 ):
     replicas, chips, cores = sizes
+    rep = lax.axis_index("rep")
+    spot = lax.axis_index("line") * cores + lax.axis_index("core")
+    where = jnp.stack([rep, spot]).astype(jnp.int32)
+    where, local_params = lax.optimization_barrier((where, local_params))
     local_rows = local_params[0]
     rows, depth = local_rows.shape
     own = local_rows.astype(jnp.bfloat16)
@@ -399,9 +404,6 @@
         and replicas & (replicas - 1) == 0
         and depth % (128 * replicas) == 0
     )
-    rep = lax.axis_index("rep")
-    spot = lax.axis_index("line") * cores + lax.axis_index("core")
-    where = jnp.stack([rep, spot]).astype(jnp.int32)
 
     def send(value, axis, k):
         count = dict(rep=replicas, line=chips, core=cores)[axis]
@@ -416,13 +418,12 @@
         near = send(own, "line", 1)
         order = (0, 2, 6, 1, 3, 7, 4, 5)
     else:
-        weights = [lax.all_gather(own, ("line", "core"), axis=0, tiled=True)]
+        late = [lax.all_gather(own, ("line", "core"), axis=0, tiled=True)]
+        weights = []
         order = (0,)
-        first = 0
 
     early = [[], []]
     states = [start_state[b].reshape(seq_width, STATE) for b in range(blocks)]
-    states, own_late = lax.optimization_barrier((states, own))
     for b in range(blocks):
         seq = slice(b * block, (b + 1) * block)
         for half in range(2):
@@ -430,23 +431,24 @@
                 early_products(out_grad[seq], ssd_input[seq], states[b], half, seq_width // 2)
             )
     if fast:
-        pieces = column_pieces(where, block_input, own_late, replicas)
+        pieces = column_pieces(where, block_input, own, replicas)
         far, _ = lax.optimization_barrier((far, pieces))
         pieces = [pieces[0]] + send_each(pieces[1:], "rep")
+        near, early[0] = lax.optimization_barrier((near, early[0]))
         far, early[0] = lax.optimization_barrier((far, early[0]))
         middle = send(far, "line", 1)
-        weights = [own, near, far] + [send(w, "core", 1) for w in (own, near, far)]
+        middle, pieces[-1] = lax.optimization_barrier((middle, pieces[-1]))
+        pair = send(jnp.concatenate([own, near], axis=0), "core", 1)
+        weights = [own, near, far, pair, send(far, "core", 1)]
         middle, early[1], weights = lax.optimization_barrier((middle, early[1], weights))
-        weights = weights + [middle, send(middle, "core", 1)]
-        first = 6
+        late = [middle, send(middle, "core", 1)]
 
     begun = []
     if fast:
         begun = [
-            first_projection(block_input[b * block : (b + 1) * block], weights[:first])
+            first_projection(block_input[b * block : (b + 1) * block], weights)
             for b in range(blocks)
         ]
-        begun, pieces[:-1] = lax.optimization_barrier((begun, pieces[:-1]))
 
     grads, mine, other = [], [], []
     for b in range(blocks):
@@ -459,7 +461,7 @@
             [early[0][b][0], early[1][b][0]],
             [early[0][b][1], early[1][b][1]],
             begun[b : b + 1],
-            weights[first:],
+            late,
             order,
         )
         for kept, part in zip((grads, mine, other), parts):
@@ -467,7 +469,7 @@
     grad, mine, other = (
         kept[0] if blocks == 1 else jnp.concatenate(kept, axis=1) for kept in (grads, mine, other)
     )
-    block_grad = block_gradient(grad, weights)
+    block_grad = block_gradient(grad, weights + late)
 
     if not fast:
         gradient = lax.psum_scatter(
@@ -483,9 +485,10 @@
         return (block_grad, new_params, new_momentum)
 
     tokens = blocks * block
-    both = jnp.concatenate([mine, send(other, "core", 1)], axis=0)
+    other = send(other, "core", 1)
+    other, pieces = lax.optimization_barrier((other, pieces))
+    both = jnp.concatenate([mine, other], axis=0)
     plane = [both] + send_each([both] * (replicas - 1), "rep")
-    plane[-1], pieces[-1] = lax.optimization_barrier((plane[-1], pieces[-1]))
     twin = send(jnp.concatenate([p[:tokens] for p in pieces], axis=0), "core", 1)
     sums = gradient_slice(where, plane, pieces, twin, chips)
     sums = [sums[0]] + send_each(sums[1:], "line")

time: 69.4 us -> 60.9 us (0.88)
  waiting for transfers between devices: 21.2 us -> 10.9 us
  Pallas kernels: 15.4 us -> 17.4 us
  starting transfers between devices: 25.1 us -> 23.6 us
  local copies, waits for them, and re-layouts: 5.36 us -> 6.52 us
    ppermute x21 -> x20, waiting for transfers between devices: 21.2 us -> 10.9 us  [send(): return lax.ppermute(value, axis, [(i, i ^ k) for i in range(count)])]
    ppermute x21 -> x20, starting transfers between devices: 25.1 us -> 23.6 us  [send(): return lax.ppermute(value, axis, [(i, i ^ k) for i in range(count)])]
    slice x6 -> x4, local copies, waits for them, and re-layouts: 0.04 us -> 1.02 us  [on_device(): p[:tokens]]
    pallas_call x1, Pallas kernels: 0.06 us -> 1.03 us  [stepped_slice(): pl.pallas_call(functools.partial(stepped_kernel, len(sums)), in_specs=who...]
    pallas_call x1, Pallas kernels: 0.63 us -> 1.34 us  [column_pieces(): pl.pallas_call(pieces_kernel, in_specs=[pl.BlockSpec(memory_space=pltpu.S...]
    unnamed x33 -> x29, local copies, waits for them, and re-layouts: 3.26 us -> 3.43 us
  transfers between devices with their start and end apart: 21 -> 20, of which waited for: 11 -> 10; matrix products, arithmetic and copies ran while one was open for 3% -> 3% of each run, Pallas kernels for 18% -> 22%
where the time goes in v3:
time: 60.9 us; the launch traced here: 60.5 us
  starting transfers between devices  23.6 us (39%)
  Pallas kernels  17.4 us (29%)
  waiting for transfers between devices  10.9 us (18%)
  local copies, waits for them, and re-layouts  6.52 us (11%)
  other arithmetic  1.19 us (2%)
  between operations  0.88 us (1%)
    ppermute x20, starting transfers between devices, send(): return lax.ppermute(value, axis, [(i, i ^ k) for i in range(count)])  23.6 us
    ppermute x20, waiting for transfers between devices, send(): return lax.ppermute(value, axis, [(i, i ^ k) for i in range(count)])  10.9 us
    pallas_call x1, Pallas kernels, ssd_backward(): pl.pallas_call(functools.partial(ssd_kernel, order, len(order) - len(weig...  4.83 us
    unnamed x29, local copies, waits for them, and re-layouts  3.43 us
    pallas_call x2, Pallas kernels, early_products(): pl.pallas_call(early_kernel, grid=(steps,), in_specs=[pl.BlockSpec((block...  3.36 us
    pallas_call x1, Pallas kernels, block_gradient(): pl.pallas_call(block_grad_kernel, in_specs=whole_vmem(1 + len(weights)),...  2.36 us
    another operation x1, local copies, waits for them, and re-layouts, on_device(): states = [start_state[b].reshape(seq_width, STATE) for b in range(blocks)]  2.05 us
    pallas_call x1, Pallas kernels, outer_step(): pl.pallas_call(outer_kernel, in_specs=[pl.BlockSpec(memory_space=pltpu.SM...  1.58 us
  transfers between devices with their start and end apart: 20, of which 10 were waited for; matrix products, arithmetic and copies ran while one was open for 3% of the time, Pallas kernels for 22%

profile of v3, /device:TPU:0, one launch (start us, length us, event | category | flops | bytes accessed | tf_op | source)
XLA Modules:
  0.0 60.5 jit_solution(8131386478961388154)
XLA Ops:
  0.7 1.0 %convert_bitcast_fusion.own_ref.refs_0_ = bf16[24,4096]{1,0:T(8,128)(2,1)S(1)} fusion(f32[1,24,4096]{2,1,0:T(8,128)} %param.15), kind=kLoop, calls=%fused_computation.2 | loop fusion | flops 98304 | bytes 589824 | tf_op jit(solution)/shard_map/convert_element_type | solution.py:396
  1.7 3.1 %collective-permute-start.1 = (bf16[24,4096]{1,0:T(8,128)(2,1)S(1)}, bf16[24,4096]{1,0:T(8,128)(2,1)S(1)}, u32[]{:S(2)}, u32[]{:S(2)}) collective-permute-start(bf16[24,4096]{1,0:T(8,128)(2,1)S(1)} %convert_bitcast_fusion.own_ref.refs_0_), channel_id=1, source_target_pairs={{0,2},{2,0},{4,6},{6,4},{1,3},{3,1},{5,7},{7,5},{8,10},{10,8},{12,... | collective-permute-start | bytes 589832 | tf_op jit(solution)/shard_map/ppermute | solution.py:410
  4.8 2.5 %collective-permute-start = (bf16[24,4096]{1,0:T(8,128)(2,1)S(1)}, bf16[24,4096]{1,0:T(8,128)(2,1)}, u32[]{:S(2)}, u32[]{:S(2)}) collective-permute-start(bf16[24,4096]{1,0:T(8,128)(2,1)S(1)} %convert_bitcast_fusion.own_ref.refs_0_), channel_id=1, source_target_pairs={{0,6},{2,4},{4,2},{6,0},{1,7},{3,5},{5,3},{7,1},{8,14},{10,12},{12... | collective-permute-start | bytes 589832 | tf_op jit(solution)/shard_map/ppermute | solution.py:410
  7.3 1.2 %copy-done = bf16[128,4096]{1,0:T(8,128)(2,1)S(1)} copy-done((bf16[128,4096]{1,0:T(8,128)(2,1)S(1)}, bf16[128,4096]{1,0:T(8,128)(2,1)}, u32[]{:S(2)}) %copy-start) | copy-done | bytes 1048600
  8.5 1.3 %column_pieces.1 = (bf16[152,1024]{1,0:T(8,128)(2,1)S(1)}, bf16[152,1024]{1,0:T(8,128)(2,1)S(1)}, bf16[152,1024]{1,0:T(8,128)(2,1)S(1)}, bf16[152,1024]{1,0:T(8,128)(2,1)}) custom-call(s32[2]{0:T(128)S(1)} %pad_add_fusion.where_ref, bf16[128,4096]{1,0:T(8,128)(2,1)S(1)} %copy-done, bf16[24,4096]{1,0:T(8,128)(2,1)S(1)} %convert_bitcast_fusion.own_ref.refs_0_), custom_call_target="tpu_custom_call" | custom-call | tf_op jit(solution)/shard_map/column_pieces/pallas_call | solution.py:282
  12.0 2.4 %collective-permute-start.3 = (bf16[152,1024]{1,0:T(8,128)(2,1)}, bf16[152,1024]{1,0:T(8,128)(2,1)}, u32[]{:S(2)}, u32[]{:S(2)}) collective-permute-start(bf16[152,1024]{1,0:T(8,128)(2,1)} %get-tuple-element.54), channel_id=1, source_target_pairs={{0,24},{8,16},{16,8},{24,0},{1,25},{9,17},{17,9},{25,1},{2,26},{10... | collective-permute-start | bytes 933896 | tf_op jit(solution)/shard_map/ppermute | solution.py:410
  14.5 2.1 %reshape_squeeze.3.state_ref = bf16[4096,64]{1,0:T(8,128)(2,1)S(1)} reshape(bf16[1,64,4096]{2,1,0:T(8,128)(2,1)} %param.12) | data formatting | bytes 1048576 | tf_op jit(solution)/shard_map/reshape;squeeze | solution.py:426
  16.6 1.7 %early_products.2 = (bf16[32,128,128]{2,1,0:T(8,128)(2,1)S(1)}, f32[128,2048]{1,0:T(8,128)S(1)}) custom-call(bf16[128,4096]{1,0:T(8,128)(2,1)S(1)} %copy-done.2, bf16[128,4096]{1,0:T(8,128)(2,1)S(1)} %copy-done.3, bf16[4096,64]{1,0:T(8,128)(2,1)S(1)} %reshape_squeeze.3.state_ref), custom_call_target="tpu_custom_call" | custom-call | flops 1 | bytes 1 | tf_op jit(solution)/shard_map/early_products/pallas_call | solution.py:71
  19.9 1.9 %collective-permute-done.3.refs_7_ = bf16[152,1024]{1,0:T(8,128)(2,1)} collective-permute-done((bf16[152,1024]{1,0:T(8,128)(2,1)}, bf16[152,1024]{1,0:T(8,128)(2,1)}, u32[]{:S(2)}, u32[]{:S(2)}) %collective-permute-start.3) | collective-permute-done | bytes 311328 | tf_op jit(solution)/shard_map/ppermute | solution.py:410
  21.8 1.5 %collective-permute-start.9 = (bf16[152,1024]{1,0:T(8,128)(2,1)S(1)}, bf16[152,1024]{1,0:T(8,128)(2,1)S(1)}, u32[]{:S(2)}, u32[]{:S(2)}) collective-permute-start(bf16[152,1024]{1,0:T(8,128)(2,1)S(1)} %copy-done.11), channel_id=1, source_target_pairs={{0,16},{8,24},{16,0},{24,8},{1,17},{9,25},{17,1},{25,9},{2,18},{10... | collective-permute-start | bytes 933896 | tf_op jit(solution)/shard_map/ppermute | solution.py:410
  23.3 1.7 %early_products.3 = (bf16[32,128,128]{2,1,0:T(8,128)(2,1)S(1)}, f32[128,2048]{1,0:T(8,128)S(1)}) custom-call(bf16[128,4096]{1,0:T(8,128)(2,1)S(1)} %copy-done.2, bf16[128,4096]{1,0:T(8,128)(2,1)S(1)} %copy-done.3, bf16[4096,64]{1,0:T(8,128)(2,1)S(1)} %reshape_squeeze.3.state_ref), custom_call_target="tpu_custom_call" | custom-call | flops 1 | bytes 1 | tf_op jit(solution)/shard_map/early_products/pallas_call | solution.py:71
  25.0 0.9 %collective-permute-done.2.rest_5_.refs_5_ = bf16[24,4096]{1,0:T(8,128)(2,1)S(1)} collective-permute-done((bf16[24,4096]{1,0:T(8,128)(2,1)}, bf16[24,4096]{1,0:T(8,128)(2,1)S(1)}, u32[]{:S(2)}, u32[]{:S(2)}) %collective-permute-start.2) | collective-permute-done | bytes 196640 | tf_op jit(solution)/shard_map/ppermute | solution.py:410
  26.0 1.4 %first_projection.1.rest_4_ = f32[144,128]{1,0:T(8,128)S(1)} custom-call(bf16[128,4096]{1,0:T(8,128)(2,1)S(1)} %copy-done.1, bf16[24,4096]{1,0:T(8,128)(2,1)S(1)} %convert_bitcast_fusion.own_ref.refs_0_, bf16[24,4096]{1,0:T(8,128)(2,1)S(1)} %collective-permute-done.1.refs_1_, bf16[24,4096]{1,0:T(8,128)(2,1)} %collective-permute-done.refs_2_, ...), custom_call_target="tpu_custom_call" | custom-call | flops 1 | bytes 1 | tf_op jit(solution)/shard_map/first_projection/pallas_call | solution.py:109
  27.5 4.8 %ssd_backward.1 = (bf16[192,128]{1,0:T(8,128)(2,1)S(1)}, bf16[96,128]{1,0:T(8,128)(2,1)S(1)}, bf16[96,128]{1,0:T(8,128)(2,1)S(1)}) custom-call(s32[2]{0:T(128)S(1)} %pad_add_fusion.where_ref, bf16[128,4096]{1,0:T(8,128)(2,1)S(1)} %copy-done.1, f32[1,64]{1,0:T(1,128)S(1)} %bitcast.6, f32[1,64]{1,0:T(1,128)S(1)} %bitcast.7, ...), custom_call_target="tpu_custom_call" | custom-call | flops 1 | bytes 1 | tf_op jit(solution)/shard_map/ssd_backward/pallas_call | solution.py:227
  33.8 1.0 %slice.15 = bf16[128,1024]{1,0:T(8,128)(2,1)S(1)} slice(bf16[152,1024]{1,0:T(8,128)(2,1)} %collective-permute-done.3.refs_7_), slice={[0:128], [0:1024]} | slice | bytes 524288 | tf_op jit(solution)/shard_map/slice | solution.py:492
  35.3 1.0 %collective-permute-start.12 = (bf16[192,128]{1,0:T(8,128)(2,1)S(1)}, bf16[192,128]{1,0:T(8,128)(2,1)S(1)}, u32[]{:S(2)}, u32[]{:S(2)}) collective-permute-start(bf16[192,128]{1,0:T(8,128)(2,1)S(1)} %constant_dynamic-update-slice_fusion.refs_0_), channel_id=1, source_target_pairs={{0,24},{8,16},{16,8},{24,0},{1,25},{9,17},{17,9},{25,1},{2,26},{10... | collective-permute-start | bytes 147464 | tf_op jit(solution)/shard_map/ppermute | solution.py:410
  36.2 1.5 %collective-permute-start.11 = (bf16[192,128]{1,0:T(8,128)(2,1)S(1)}, bf16[192,128]{1,0:T(8,128)(2,1)S(1)}, u32[]{:S(2)}, u32[]{:S(2)}) collective-permute-start(bf16[192,128]{1,0:T(8,128)(2,1)S(1)} %constant_dynamic-update-slice_fusion.refs_0_), channel_id=1, source_target_pairs={{0,16},{8,24},{16,0},{24,8},{1,17},{9,25},{17,1},{25,9},{2,18},{10... | collective-permute-start | bytes 147464 | tf_op jit(solution)/shard_map/ppermute | solution.py:410
  37.8 1.1 %collective-permute-start.10 = (bf16[192,128]{1,0:T(8,128)(2,1)S(1)}, bf16[192,128]{1,0:T(8,128)(2,1)S(1)}, u32[]{:S(2)}, u32[]{:S(2)}) collective-permute-start(bf16[192,128]{1,0:T(8,128)(2,1)S(1)} %constant_dynamic-update-slice_fusion.refs_0_), channel_id=1, source_target_pairs={{0,8},{8,0},{16,24},{24,16},{1,9},{9,1},{17,25},{25,17},{2,10},{10... | collective-permute-start | bytes 147464 | tf_op jit(solution)/shard_map/ppermute | solution.py:410
  38.8 1.9 %collective-permute-done.12.refs_3_ = bf16[192,128]{1,0:T(8,128)(2,1)S(1)} collective-permute-done((bf16[192,128]{1,0:T(8,128)(2,1)S(1)}, bf16[192,128]{1,0:T(8,128)(2,1)S(1)}, u32[]{:S(2)}, u32[]{:S(2)}) %collective-permute-start.12) | collective-permute-done | bytes 49184 | tf_op jit(solution)/shard_map/ppermute | solution.py:410
  40.9 1.0 %collective-permute-done.10.refs_1_ = bf16[192,128]{1,0:T(8,128)(2,1)S(1)} collective-permute-done((bf16[192,128]{1,0:T(8,128)(2,1)S(1)}, bf16[192,128]{1,0:T(8,128)(2,1)S(1)}, u32[]{:S(2)}, u32[]{:S(2)}) %collective-permute-start.10) | collective-permute-done | bytes 49184 | tf_op jit(solution)/shard_map/ppermute | solution.py:410
  41.9 1.5 %gradient_slice.1 = (bf16[24,1024]{1,0:T(8,128)(2,1)S(1)}, bf16[24,1024]{1,0:T(8,128)(2,1)S(1)}, bf16[24,1024]{1,0:T(8,128)(2,1)S(1)}, bf16[24,1024]{1,0:T(8,128)(2,1)S(1)}) custom-call(s32[2]{0:T(128)S(1)} %pad_add_fusion.where_ref, bf16[192,128]{1,0:T(8,128)(2,1)S(1)} %constant_dynamic-update-slice_fusion.refs_0_, ...), custom_call_target="tpu_custom_call" | custom-call | tf_op jit(solution)/shard_map/gradient_slice/pallas_call | solution.py:316
  43.7 1.6 %collective-permute-start.15 = (bf16[24,1024]{1,0:T(8,128)(2,1)S(1)}, bf16[24,1024]{1,0:T(8,128)(2,1)S(1)}, u32[]{:S(2)}, u32[]{:S(2)}) collective-permute-start(bf16[24,1024]{1,0:T(8,128)(2,1)S(1)} %get-tuple-element.85), channel_id=1, source_target_pairs={{0,4},{2,6},{4,0},{6,2},{1,5},{3,7},{5,1},{7,3},{8,12},{10,14},{12... | collective-permute-start | bytes 147464 | tf_op jit(solution)/shard_map/ppermute | solution.py:410
  45.3 2.5 %collective-permute-start.16 = (bf16[24,1024]{1,0:T(8,128)(2,1)S(1)}, bf16[24,1024]{1,0:T(8,128)(2,1)S(1)}, u32[]{:S(2)}, u32[]{:S(2)}) collective-permute-start(bf16[24,1024]{1,0:T(8,128)(2,1)S(1)} %get-tuple-element.86), channel_id=1, source_target_pairs={{0,6},{2,4},{4,2},{6,0},{1,7},{3,5},{5,3},{7,1},{8,14},{10,12},{12... | collective-permute-start | bytes 147464 | tf_op jit(solution)/shard_map/ppermute | solution.py:410
  47.8 2.4 %block_gradient.1 = bf16[128,4096]{1,0:T(8,128)(2,1)} custom-call(bf16[192,128]{1,0:T(8,128)(2,1)S(1)} %get-tuple-element.87.grad_ref, bf16[24,4096]{1,0:T(8,128)(2,1)S(1)} %convert_bitcast_fusion.own_ref.refs_0_, bf16[24,4096]{1,0:T(8,128)(2,1)S(1)} %collective-permute-done.1.refs_1_, bf16[24,4096]{1,0:T(8,128)(2,1)} %collective-permute-done.refs_2_, ...), custom_call_target="tpu_custom_call" | custom-call | flops 201326592 | bytes 3145728 | tf_op jit(solution)/shard_map/block_gradient/pallas_call | solution.py:257
  50.2 1.0 %collective-permute-done.16.refs_3_ = bf16[24,1024]{1,0:T(8,128)(2,1)S(1)} collective-permute-done((bf16[24,1024]{1,0:T(8,128)(2,1)S(1)}, bf16[24,1024]{1,0:T(8,128)(2,1)S(1)}, u32[]{:S(2)}, u32[]{:S(2)}) %collective-permute-start.16) | collective-permute-done | bytes 49184 | tf_op jit(solution)/shard_map/ppermute | solution.py:410
  51.2 1.0 %stepped_slice.1.refs_0_ = bf16[24,1024]{1,0:T(8,128)(2,1)S(1)} custom-call(bf16[24,1024]{1,0:T(8,128)(2,1)S(1)} %get-tuple-element.89.refs_0_, bf16[24,1024]{1,0:T(8,128)(2,1)S(1)} %collective-permute-done.14.refs_1_, bf16[24,1024]{1,0:T(8,128)(2,1)S(1)} %collective-permute-done.15.refs_2_, bf16[24,1024]{1,0:T(8,128)(2,1)S(1)} %collective-permute-done.16.refs_3_, ...), custom_call_target="tpu_custom_call" | custom-call | tf_op jit(solution)/shard_map/stepped_slice/pallas_call | solution.py:341
  52.2 1.1 %collective-permute-start.19 = (bf16[24,1024]{1,0:T(8,128)(2,1)S(1)}, bf16[24,1024]{1,0:T(8,128)(2,1)S(1)}, u32[]{:S(2)}, u32[]{:S(2)}) collective-permute-start(bf16[24,1024]{1,0:T(8,128)(2,1)S(1)} %stepped_slice.1.refs_0_), channel_id=1, source_target_pairs={{0,24},{8,16},{16,8},{24,0},{1,25},{9,17},{17,9},{25,1},{2,26},{10... | collective-permute-start | bytes 147464 | tf_op jit(solution)/shard_map/ppermute | solution.py:410
  53.3 1.5 %collective-permute-start.18 = (bf16[24,1024]{1,0:T(8,128)(2,1)S(1)}, bf16[24,1024]{1,0:T(8,128)(2,1)S(1)}, u32[]{:S(2)}, u32[]{:S(2)}) collective-permute-start(bf16[24,1024]{1,0:T(8,128)(2,1)S(1)} %stepped_slice.1.refs_0_), channel_id=1, source_target_pairs={{0,16},{8,24},{16,0},{24,8},{1,17},{9,25},{17,1},{25,9},{2,18},{10... | collective-permute-start | bytes 147464 | tf_op jit(solution)/shard_map/ppermute | solution.py:410
  54.8 0.9 %collective-permute-start.17 = (bf16[24,1024]{1,0:T(8,128)(2,1)S(1)}, bf16[24,1024]{1,0:T(8,128)(2,1)S(1)}, u32[]{:S(2)}, u32[]{:S(2)}) collective-permute-start(bf16[24,1024]{1,0:T(8,128)(2,1)S(1)} %stepped_slice.1.refs_0_), channel_id=1, source_target_pairs={{0,8},{8,0},{16,24},{24,16},{1,9},{9,1},{17,25},{25,17},{2,10},{10... | collective-permute-start | bytes 147464 | tf_op jit(solution)/shard_map/ppermute | solution.py:410
  55.8 1.5 %collective-permute-done.19.refs_3_ = bf16[24,1024]{1,0:T(8,128)(2,1)S(1)} collective-permute-done((bf16[24,1024]{1,0:T(8,128)(2,1)S(1)}, bf16[24,1024]{1,0:T(8,128)(2,1)S(1)}, u32[]{:S(2)}, u32[]{:S(2)}) %collective-permute-start.19) | collective-permute-done | bytes 49184 | tf_op jit(solution)/shard_map/ppermute | solution.py:410
  57.8 1.1 %collective-permute-done.17.refs_1_ = bf16[24,1024]{1,0:T(8,128)(2,1)S(1)} collective-permute-done((bf16[24,1024]{1,0:T(8,128)(2,1)S(1)}, bf16[24,1024]{1,0:T(8,128)(2,1)S(1)}, u32[]{:S(2)}, u32[]{:S(2)}) %collective-permute-start.17) | collective-permute-done | bytes 49184 | tf_op jit(solution)/shard_map/ppermute | solution.py:410
  58.9 1.6 %outer_step.1 = (f32[24,4096]{1,0:T(8,128)}, f32[24,4096]{1,0:T(8,128)}) custom-call(s32[2]{0:T(128)S(1)} %pad_add_fusion.where_ref, f32[24,4096]{1,0:T(8,128)S(1)} %copy-done.6, f32[24,4096]{1,0:T(8,128)S(1)} %copy-done.7, bf16[24,1024]{1,0:T(8,128)(2,1)S(1)} %stepped_slice.1.refs_0_, bf16[24,1024]{1,0:T(8,128)(2,1)S(1)} %collective-permute-done.17.refs_1_, ...), custom_call_target="tpu_custom_call" | custom-call | tf_op jit(solution)/shard_map/outer_step/pallas_call | solution.py:366
  (56 shorter events, 6.8 us)
Async XLA Ops:
  1.7 16.5 %collective-permute-start.1 = (bf16[24,4096]{1,0:T(8,128)(2,1)S(1)}, bf16[24,4096]{1,0:T(8,128)(2,1)S(1)}, u32[]{:S(2)}, u32[]{:S(2)}) collective-permute-start(bf16[24,4096]{1,0:T(8,128)(2,1)S(1)} %convert_bitcast_fusion.own_ref.refs_0_), channel_id=1, source_target_pairs={{0,2},{2,0},{4,6},{6,4},{1,3},{3,1},{5,7},{7,5},{8,10},{10,8},{12,... | collective-permute-start | bytes 589832 | tf_op jit(solution)/shard_map/ppermute | solution.py:410
  4.8 13.6 %collective-permute-start = (bf16[24,4096]{1,0:T(8,128)(2,1)S(1)}, bf16[24,4096]{1,0:T(8,128)(2,1)}, u32[]{:S(2)}, u32[]{:S(2)}) collective-permute-start(bf16[24,4096]{1,0:T(8,128)(2,1)S(1)} %convert_bitcast_fusion.own_ref.refs_0_), channel_id=1, source_target_pairs={{0,6},{2,4},{4,2},{6,0},{1,7},{3,5},{5,3},{7,1},{8,14},{10,12},{12... | collective-permute-start | bytes 589832 | tf_op jit(solution)/shard_map/ppermute | solution.py:410
  7.3 1.2 %copy-start = (bf16[128,4096]{1,0:T(8,128)(2,1)S(1)}, bf16[128,4096]{1,0:T(8,128)(2,1)}, u32[]{:S(2)}) copy-start(bf16[128,4096]{1,0:T(8,128)(2,1)} %rows_ref.5) | copy-start | bytes 3145732
  8.5 8.0 %copy-start.3 = (bf16[128,4096]{1,0:T(8,128)(2,1)S(1)}, bf16[128,4096]{1,0:T(8,128)(2,1)}, u32[]{:S(2)}) copy-start(bf16[128,4096]{1,0:T(8,128)(2,1)} %val_ref.3) | copy-start | bytes 3145732
  10.6 0.7 %copy-start.10 = (bf16[152,1024]{1,0:T(8,128)(2,1)}, bf16[152,1024]{1,0:T(8,128)(2,1)S(1)}, u32[]{:S(2)}) copy-start(bf16[152,1024]{1,0:T(8,128)(2,1)S(1)} %get-tuple-element.53) | copy-start | bytes 933892
  12.0 4.5 %copy-start.2 = (bf16[128,4096]{1,0:T(8,128)(2,1)S(1)}, bf16[128,4096]{1,0:T(8,128)(2,1)}, u32[]{:S(2)}) copy-start(bf16[128,4096]{1,0:T(8,128)(2,1)} %cot_ref.3) | copy-start | bytes 3145732
  12.0 9.8 %collective-permute-start.3 = (bf16[152,1024]{1,0:T(8,128)(2,1)}, bf16[152,1024]{1,0:T(8,128)(2,1)}, u32[]{:S(2)}, u32[]{:S(2)}) collective-permute-start(bf16[152,1024]{1,0:T(8,128)(2,1)} %get-tuple-element.54), channel_id=1, source_target_pairs={{0,24},{8,16},{16,8},{24,0},{1,25},{9,17},{17,9},{25,1},{2,26},{10... | collective-permute-start | bytes 933896 | tf_op jit(solution)/shard_map/ppermute | solution.py:410
  16.6 2.8 %copy-start.13 = (bf16[152,1024]{1,0:T(8,128)(2,1)S(1)}, bf16[152,1024]{1,0:T(8,128)(2,1)}, u32[]{:S(2)}) copy-start(bf16[152,1024]{1,0:T(8,128)(2,1)} %copy-done.12) | copy-start | bytes 933892
  16.6 5.2 %copy-start.11 = (bf16[152,1024]{1,0:T(8,128)(2,1)S(1)}, bf16[152,1024]{1,0:T(8,128)(2,1)}, u32[]{:S(2)}) copy-start(bf16[152,1024]{1,0:T(8,128)(2,1)} %copy-done.10) | copy-start | bytes 933892
  18.3 7.6 %collective-permute-start.4 = (bf16[48,4096]{1,0:T(8,128)(2,1)S(1)}, bf16[48,4096]{1,0:T(8,128)(2,1)S(1)}, u32[]{:S(2)}, u32[]{:S(2)}) collective-permute-start(bf16[48,4096]{1,0:T(8,128)(2,1)S(1)} %pad_maximum_fusion.1), channel_id=1, source_target_pairs={{0,1},{1,0},{2,3},{3,2},{4,5},{5,4},{6,7},{7,6},{8,9},{9,8},{10,11... | collective-permute-start | bytes 1179656 | tf_op jit(solution)/shard_map/ppermute | solution.py:410
  18.4 7.6 %copy-start.1 = (bf16[128,4096]{1,0:T(8,128)(2,1)S(1)}, bf16[128,4096]{1,0:T(8,128)(2,1)}, u32[]{:S(2)}) copy-start(bf16[128,4096]{1,0:T(8,128)(2,1)} %rows_ref.5) | copy-start | bytes 3145732
  18.4 7.5 %collective-permute-start.2 = (bf16[24,4096]{1,0:T(8,128)(2,1)}, bf16[24,4096]{1,0:T(8,128)(2,1)S(1)}, u32[]{:S(2)}, u32[]{:S(2)}) collective-permute-start(bf16[24,4096]{1,0:T(8,128)(2,1)} %collective-permute-done.refs_2_), channel_id=1, source_target_pairs={{0,2},{2,0},{4,6},{6,4},{1,3},{3,1},{5,7},{7,5},{8,10},{10,8},{12,... | collective-permute-start | bytes 589832 | tf_op jit(solution)/shard_map/ppermute | solution.py:410
  19.2 6.8 %collective-permute-start.5 = (bf16[24,4096]{1,0:T(8,128)(2,1)}, bf16[24,4096]{1,0:T(8,128)(2,1)S(1)}, u32[]{:S(2)}, u32[]{:S(2)}) collective-permute-start(bf16[24,4096]{1,0:T(8,128)(2,1)} %collective-permute-done.refs_2_), channel_id=1, source_target_pairs={{0,1},{1,0},{2,3},{3,2},{4,5},{5,4},{6,7},{7,6},{8,9},{9,8},{10,11... | collective-permute-start | bytes 589832 | tf_op jit(solution)/shard_map/ppermute | solution.py:410
  19.3 13.6 %collective-permute-start.8 = (bf16[152,1024]{1,0:T(8,128)(2,1)S(1)}, bf16[152,1024]{1,0:T(8,128)(2,1)S(1)}, u32[]{:S(2)}, u32[]{:S(2)}) collective-permute-start(bf16[152,1024]{1,0:T(8,128)(2,1)S(1)} %copy-done.13), channel_id=1, source_target_pairs={{0,8},{8,0},{16,24},{24,16},{1,9},{9,1},{17,25},{25,17},{2,10},{10... | collective-permute-start | bytes 933896 | tf_op jit(solution)/shard_map/ppermute | solution.py:410
  21.8 11.1 %collective-permute-start.9 = (bf16[152,1024]{1,0:T(8,128)(2,1)S(1)}, bf16[152,1024]{1,0:T(8,128)(2,1)S(1)}, u32[]{:S(2)}, u32[]{:S(2)}) collective-permute-start(bf16[152,1024]{1,0:T(8,128)(2,1)S(1)} %copy-done.11), channel_id=1, source_target_pairs={{0,16},{8,24},{16,0},{24,8},{1,17},{9,25},{17,1},{25,9},{2,18},{10... | collective-permute-start | bytes 933896 | tf_op jit(solution)/shard_map/ppermute | solution.py:410
  25.9 1.5 %copy-start.8 = (f32[64]{0:T(128)S(1)}, f32[64]{0:T(128)}, u32[]{:S(2)}) copy-start(f32[64]{0:T(128)} %param.13) | copy-start | bytes 772
  25.9 1.5 %copy-start.9 = (f32[64]{0:T(128)S(1)}, f32[64]{0:T(128)}, u32[]{:S(2)}) copy-start(f32[64]{0:T(128)} %param.14) | copy-start | bytes 772
  25.9 1.5 %collective-permute-start.6 = (bf16[24,4096]{1,0:T(8,128)(2,1)S(1)}, bf16[24,4096]{1,0:T(8,128)(2,1)S(1)}, u32[]{:S(2)}, u32[]{:S(2)}) collective-permute-start(bf16[24,4096]{1,0:T(8,128)(2,1)S(1)} %collective-permute-done.2.rest_5_.refs_5_), channel_id=1, source_target_pairs={{0,1},{1,0},{2,3},{3,2},{4,5},{5,4},{6,7},{7,6},{8,9},{9,8},{10,11... | collective-permute-start | bytes 589832 | tf_op jit(solution)/shard_map/ppermute | solution.py:410
  27.5 6.2 %copy-start.5 = (bf16[152,1024]{1,0:T(8,128)(2,1)S(1)}, bf16[152,1024]{1,0:T(8,128)(2,1)}, u32[]{:S(2)}) copy-start(bf16[152,1024]{1,0:T(8,128)(2,1)} %copy-done.4) | copy-start | bytes 933892
  32.3 1.4 %collective-permute-start.7 = (bf16[96,128]{1,0:T(8,128)(2,1)S(1)}, bf16[96,128]{1,0:T(8,128)(2,1)S(1)}, u32[]{:S(2)}, u32[]{:S(2)}) collective-permute-start(bf16[96,128]{1,0:T(8,128)(2,1)S(1)} %get-tuple-element.76), channel_id=1, source_target_pairs={{0,1},{1,0},{2,3},{3,2},{4,5},{5,4},{6,7},{7,6},{8,9},{9,8},{10,11... | collective-permute-start | bytes 73736 | tf_op jit(solution)/shard_map/ppermute | solution.py:410
  34.9 7.0 %collective-permute-start.13 = (bf16[512,1024]{1,0:T(8,128)(2,1)S(1)}, bf16[512,1024]{1,0:T(8,128)(2,1)S(1)}, u32[]{:S(2)}, u32[]{:S(2)}) collective-permute-start(bf16[512,1024]{1,0:T(8,128)(2,1)S(1)} %pad_maximum_fusion), channel_id=1, source_target_pairs={{0,1},{1,0},{2,3},{3,2},{4,5},{5,4},{6,7},{7,6},{8,9},{9,8},{10,11... | collective-permute-start | bytes 3145736 | tf_op jit(solution)/shard_map/ppermute | solution.py:410
  35.3 5.5 %collective-permute-start.12 = (bf16[192,128]{1,0:T(8,128)(2,1)S(1)}, bf16[192,128]{1,0:T(8,128)(2,1)S(1)}, u32[]{:S(2)}, u32[]{:S(2)}) collective-permute-start(bf16[192,128]{1,0:T(8,128)(2,1)S(1)} %constant_dynamic-update-slice_fusion.refs_0_), channel_id=1, source_target_pairs={{0,24},{8,16},{16,8},{24,0},{1,25},{9,17},{17,9},{25,1},{2,26},{10... | collective-permute-start | bytes 147464 | tf_op jit(solution)/shard_map/ppermute | solution.py:410
  36.2 4.6 %collective-permute-start.11 = (bf16[192,128]{1,0:T(8,128)(2,1)S(1)}, bf16[192,128]{1,0:T(8,128)(2,1)S(1)}, u32[]{:S(2)}, u32[]{:S(2)}) collective-permute-start(bf16[192,128]{1,0:T(8,128)(2,1)S(1)} %constant_dynamic-update-slice_fusion.refs_0_), channel_id=1, source_target_pairs={{0,16},{8,24},{16,0},{24,8},{1,17},{9,25},{17,1},{25,9},{2,18},{10... | collective-permute-start | bytes 147464 | tf_op jit(solution)/shard_map/ppermute | solution.py:410
  37.8 4.1 %collective-permute-start.10 = (bf16[192,128]{1,0:T(8,128)(2,1)S(1)}, bf16[192,128]{1,0:T(8,128)(2,1)S(1)}, u32[]{:S(2)}, u32[]{:S(2)}) collective-permute-start(bf16[192,128]{1,0:T(8,128)(2,1)S(1)} %constant_dynamic-update-slice_fusion.refs_0_), channel_id=1, source_target_pairs={{0,8},{8,0},{16,24},{24,16},{1,9},{9,1},{17,25},{25,17},{2,10},{10... | collective-permute-start | bytes 147464 | tf_op jit(solution)/shard_map/ppermute | solution.py:410
  43.4 6.8 %collective-permute-start.14 = (bf16[24,1024]{1,0:T(8,128)(2,1)S(1)}, bf16[24,1024]{1,0:T(8,128)(2,1)S(1)}, u32[]{:S(2)}, u32[]{:S(2)}) collective-permute-start(bf16[24,1024]{1,0:T(8,128)(2,1)S(1)} %get-tuple-element.84), channel_id=1, source_target_pairs={{0,2},{2,0},{4,6},{6,4},{1,3},{3,1},{5,7},{7,5},{8,10},{10,8},{12,... | collective-permute-start | bytes 147464 | tf_op jit(solution)/shard_map/ppermute | solution.py:410
  43.7 6.4 %collective-permute-start.15 = (bf16[24,1024]{1,0:T(8,128)(2,1)S(1)}, bf16[24,1024]{1,0:T(8,128)(2,1)S(1)}, u32[]{:S(2)}, u32[]{:S(2)}) collective-permute-start(bf16[24,1024]{1,0:T(8,128)(2,1)S(1)} %get-tuple-element.85), channel_id=1, source_target_pairs={{0,4},{2,6},{4,0},{6,2},{1,5},{3,7},{5,1},{7,3},{8,12},{10,14},{12... | collective-permute-start | bytes 147464 | tf_op jit(solution)/shard_map/ppermute | solution.py:410
  45.3 5.9 %collective-permute-start.16 = (bf16[24,1024]{1,0:T(8,128)(2,1)S(1)}, bf16[24,1024]{1,0:T(8,128)(2,1)S(1)}, u32[]{:S(2)}, u32[]{:S(2)}) collective-permute-start(bf16[24,1024]{1,0:T(8,128)(2,1)S(1)} %get-tuple-element.86), channel_id=1, source_target_pairs={{0,6},{2,4},{4,2},{6,0},{1,7},{3,5},{5,3},{7,1},{8,14},{10,12},{12... | collective-permute-start | bytes 147464 | tf_op jit(solution)/shard_map/ppermute | solution.py:410
  50.2 8.8 %copy-start.6 = (f32[24,4096]{1,0:T(8,128)S(1)}, f32[24,4096]{1,0:T(8,128)}, u32[]{:S(2)}) copy-start(f32[24,4096]{1,0:T(8,128)} %par_ref.1) | copy-start | bytes 1179652
  50.2 8.8 %copy-start.7 = (f32[24,4096]{1,0:T(8,128)S(1)}, f32[24,4096]{1,0:T(8,128)}, u32[]{:S(2)}) copy-start(f32[24,4096]{1,0:T(8,128)} %mom_ref.1) | copy-start | bytes 1179652
  52.2 5.1 %collective-permute-start.19 = (bf16[24,1024]{1,0:T(8,128)(2,1)S(1)}, bf16[24,1024]{1,0:T(8,128)(2,1)S(1)}, u32[]{:S(2)}, u32[]{:S(2)}) collective-permute-start(bf16[24,1024]{1,0:T(8,128)(2,1)S(1)} %stepped_slice.1.refs_0_), channel_id=1, source_target_pairs={{0,24},{8,16},{16,8},{24,0},{1,25},{9,17},{17,9},{25,1},{2,26},{10... | collective-permute-start | bytes 147464 | tf_op jit(solution)/shard_map/ppermute | solution.py:410
  53.3 4.5 %collective-permute-start.18 = (bf16[24,1024]{1,0:T(8,128)(2,1)S(1)}, bf16[24,1024]{1,0:T(8,128)(2,1)S(1)}, u32[]{:S(2)}, u32[]{:S(2)}) collective-permute-start(bf16[24,1024]{1,0:T(8,128)(2,1)S(1)} %stepped_slice.1.refs_0_), channel_id=1, source_target_pairs={{0,16},{8,24},{16,0},{24,8},{1,17},{9,25},{17,1},{25,9},{2,18},{10... | collective-permute-start | bytes 147464 | tf_op jit(solution)/shard_map/ppermute | solution.py:410
  54.8 4.1 %collective-permute-start.17 = (bf16[24,1024]{1,0:T(8,128)(2,1)S(1)}, bf16[24,1024]{1,0:T(8,128)(2,1)S(1)}, u32[]{:S(2)}, u32[]{:S(2)}) collective-permute-start(bf16[24,1024]{1,0:T(8,128)(2,1)S(1)} %stepped_slice.1.refs_0_), channel_id=1, source_target_pairs={{0,8},{8,0},{16,24},{24,16},{1,9},{9,1},{17,25},{25,17},{2,10},{10... | collective-permute-start | bytes 147464 | tf_op jit(solution)/shard_map/ppermute | solution.py:410
  (2 other events, 1.4 us)

commit v4 on v3

--- a/solution.py
+++ b/solution.py
@@ -424,6 +424,7 @@
 
     early = [[], []]
     states = [start_state[b].reshape(seq_width, STATE) for b in range(blocks)]
+    states, own_late = lax.optimization_barrier((states, own))
     for b in range(blocks):
         seq = slice(b * block, (b + 1) * block)
         for half in range(2):
@@ -431,7 +432,7 @@
                 early_products(out_grad[seq], ssd_input[seq], states[b], half, seq_width // 2)
             )
     if fast:
-        pieces = column_pieces(where, block_input, own, replicas)
+        pieces = column_pieces(where, block_input, own_late, replicas)
         far, _ = lax.optimization_barrier((far, pieces))
         pieces = [pieces[0]] + send_each(pieces[1:], "rep")
         near, early[0] = lax.optimization_barrier((near, early[0]))

time: 60.9 us -> 56.5 us (0.928)
  local copies, waits for them, and re-layouts: 6.52 us -> 2.17 us
  Pallas kernels: 17.4 us -> 15.2 us
  waiting for transfers between devices: 10.9 us -> 12.4 us
  starting transfers between devices: 23.6 us -> 24.3 us
    unnamed x29 -> x15, local copies, waits for them, and re-layouts: 3.43 us -> 0.04 us
    ppermute x20, waiting for transfers between devices: 10.9 us -> 12.4 us  [send(): return lax.ppermute(value, axis, [(i, i ^ k) for i in range(count)])]
    pallas_call x1, Pallas kernels: 1.03 us -> 0.06 us  [stepped_slice(): pl.pallas_call(functools.partial(stepped_kernel, len(sums)), in_specs=who...]
    slice x4, local copies, waits for them, and re-layouts: 1.02 us -> 0.07 us  [on_device(): p[:tokens]]
    pallas_call x1, Pallas kernels: 1.34 us -> 0.63 us  [column_pieces(): pl.pallas_call(pieces_kernel, in_specs=[pl.BlockSpec(memory_space=pltpu.S...]
    ppermute x20, starting transfers between devices: 23.6 us -> 24.3 us  [send(): return lax.ppermute(value, axis, [(i, i ^ k) for i in range(count)])]
  transfers between devices with their start and end apart: 20 -> 20, of which waited for: 10 -> 10; matrix products, arithmetic and copies ran while one was open for 3% -> 4% of each run, Pallas kernels for 22% -> 22%
where the time goes in v4:
time: 56.5 us; the launch traced here: 56.3 us
  starting transfers between devices  24.3 us (43%)
  Pallas kernels  15.2 us (27%)
  waiting for transfers between devices  12.4 us (22%)
  local copies, waits for them, and re-layouts  2.17 us (4%)
  other arithmetic  1.28 us (2%)
  between operations  0.86 us (2%)
    ppermute x20, starting transfers between devices, send(): return lax.ppermute(value, axis, [(i, i ^ k) for i in range(count)])  24.3 us
    ppermute x20, waiting for transfers between devices, send(): return lax.ppermute(value, axis, [(i, i ^ k) for i in range(count)])  12.4 us
    pallas_call x1, Pallas kernels, ssd_backward(): pl.pallas_call(functools.partial(ssd_kernel, order, len(order) - len(weig...  4.84 us
    pallas_call x2, Pallas kernels, early_products(): pl.pallas_call(early_kernel, grid=(steps,), in_specs=[pl.BlockSpec((block...  3.34 us
    pallas_call x1, Pallas kernels, block_gradient(): pl.pallas_call(block_grad_kernel, in_specs=whole_vmem(1 + len(weights)),...  2.36 us
    another operation x1, local copies, waits for them, and re-layouts, on_device(): states = [start_state[b].reshape(seq_width, STATE) for b in range(blocks)]  2.05 us
    pallas_call x1, Pallas kernels, outer_step(): pl.pallas_call(outer_kernel, in_specs=[pl.BlockSpec(memory_space=pltpu.SM...  1.58 us
    pallas_call x1, Pallas kernels, first_projection(): pl.pallas_call(first_kernel, in_specs=whole_vmem(1 + len(weights)), out_s...  1.4 us
  transfers between devices with their start and end apart: 20, of which 10 were waited for; matrix products, arithmetic and copies ran while one was open for 4% of the time, Pallas kernels for 22%

profile of v4, /device:TPU:0, one launch (start us, length us, event | category | flops | bytes accessed | tf_op | source)
XLA Modules:
  0.0 56.3 jit_solution(17018862730149300040)
XLA Ops:
  0.7 1.1 %convert_bitcast_fusion.own_ref.refs_0_ = bf16[24,4096]{1,0:T(8,128)(2,1)S(1)} fusion(f32[1,24,4096]{2,1,0:T(8,128)} %param.15), kind=kLoop, calls=%fused_computation.2 | loop fusion | flops 98304 | bytes 589824 | tf_op jit(solution)/shard_map/convert_element_type | solution.py:396
  1.8 3.1 %collective-permute-start.1 = (bf16[24,4096]{1,0:T(8,128)(2,1)S(1)}, bf16[24,4096]{1,0:T(8,128)(2,1)S(1)}, u32[]{:S(2)}, u32[]{:S(2)}) collective-permute-start(bf16[24,4096]{1,0:T(8,128)(2,1)S(1)} %convert_bitcast_fusion.own_ref.refs_0_), channel_id=1, source_target_pairs={{0,2},{2,0},{4,6},{6,4},{1,3},{3,1},{5,7},{7,5},{8,10},{10,8},{12,... | collective-permute-start | bytes 589832 | tf_op jit(solution)/shard_map/ppermute | solution.py:410
  4.9 2.5 %collective-permute-start = (bf16[24,4096]{1,0:T(8,128)(2,1)S(1)}, bf16[24,4096]{1,0:T(8,128)(2,1)}, u32[]{:S(2)}, u32[]{:S(2)}) collective-permute-start(bf16[24,4096]{1,0:T(8,128)(2,1)S(1)} %convert_bitcast_fusion.own_ref.refs_0_), channel_id=1, source_target_pairs={{0,6},{2,4},{4,2},{6,0},{1,7},{3,5},{5,3},{7,1},{8,14},{10,12},{12... | collective-permute-start | bytes 589832 | tf_op jit(solution)/shard_map/ppermute | solution.py:410
  7.4 2.1 %reshape_squeeze.3.state_ref = bf16[4096,64]{1,0:T(8,128)(2,1)S(1)} reshape(bf16[1,64,4096]{2,1,0:T(8,128)(2,1)} %param.12) | data formatting | bytes 1048576 | tf_op jit(solution)/shard_map/reshape;squeeze | solution.py:426
  9.5 0.6 %column_pieces.1 = (bf16[152,1024]{1,0:T(8,128)(2,1)S(1)}, bf16[152,1024]{1,0:T(8,128)(2,1)S(1)}, bf16[152,1024]{1,0:T(8,128)(2,1)S(1)}, bf16[152,1024]{1,0:T(8,128)(2,1)S(1)}) custom-call(s32[2]{0:T(128)S(1)} %pad_add_fusion.where_ref, bf16[128,4096]{1,0:T(8,128)(2,1)S(1)} %copy-done, bf16[24,4096]{1,0:T(8,128)(2,1)S(1)} %convert_bitcast_fusion.own_ref.refs_0_), custom_call_target="tpu_custom_call" | custom-call | tf_op jit(solution)/shard_map/column_pieces/pallas_call | solution.py:282
  10.1 2.5 %collective-permute-start.3 = (bf16[152,1024]{1,0:T(8,128)(2,1)S(1)}, bf16[152,1024]{1,0:T(8,128)(2,1)S(1)}, u32[]{:S(2)}, u32[]{:S(2)}) collective-permute-start(bf16[152,1024]{1,0:T(8,128)(2,1)S(1)} %get-tuple-element.57), channel_id=1, source_target_pairs={{0,24},{8,16},{16,8},{24,0},{1,25},{9,17},{17,9},{25,1},{2,26},{10... | collective-permute-start | bytes 933896 | tf_op jit(solution)/shard_map/ppermute | solution.py:410
  12.6 1.7 %early_products.2 = (bf16[32,128,128]{2,1,0:T(8,128)(2,1)S(1)}, f32[128,2048]{1,0:T(8,128)S(1)}) custom-call(bf16[128,4096]{1,0:T(8,128)(2,1)S(1)} %copy-done.1, bf16[128,4096]{1,0:T(8,128)(2,1)S(1)} %copy-done.2, bf16[4096,64]{1,0:T(8,128)(2,1)S(1)} %reshape_squeeze.3.state_ref), custom_call_target="tpu_custom_call" | custom-call | flops 1 | bytes 1 | tf_op jit(solution)/shard_map/early_products/pallas_call | solution.py:71
  14.4 2.0 %collective-permute-done.refs_2_ = bf16[24,4096]{1,0:T(8,128)(2,1)} collective-permute-done((bf16[24,4096]{1,0:T(8,128)(2,1)S(1)}, bf16[24,4096]{1,0:T(8,128)(2,1)}, u32[]{:S(2)}, u32[]{:S(2)}) %collective-permute-start) | collective-permute-done | bytes 196640 | tf_op jit(solution)/shard_map/ppermute | solution.py:410
  16.4 0.6 %collective-permute-start.2 = (bf16[24,4096]{1,0:T(8,128)(2,1)}, bf16[24,4096]{1,0:T(8,128)(2,1)S(1)}, u32[]{:S(2)}, u32[]{:S(2)}) collective-permute-start(bf16[24,4096]{1,0:T(8,128)(2,1)} %collective-permute-done.refs_2_), channel_id=1, source_target_pairs={{0,2},{2,0},{4,6},{6,4},{1,3},{3,1},{5,7},{7,5},{8,10},{10,8},{12,... | collective-permute-start | bytes 589832 | tf_op jit(solution)/shard_map/ppermute | solution.py:410
  17.0 1.5 %collective-permute-start.8 = (bf16[152,1024]{1,0:T(8,128)(2,1)S(1)}, bf16[152,1024]{1,0:T(8,128)(2,1)S(1)}, u32[]{:S(2)}, u32[]{:S(2)}) collective-permute-start(bf16[152,1024]{1,0:T(8,128)(2,1)S(1)} %get-tuple-element.55), channel_id=1, source_target_pairs={{0,8},{8,0},{16,24},{24,16},{1,9},{9,1},{17,25},{25,17},{2,10},{10... | collective-permute-start | bytes 933896 | tf_op jit(solution)/shard_map/ppermute | solution.py:410
  18.5 1.1 %collective-permute-done.3.refs_7_ = bf16[152,1024]{1,0:T(8,128)(2,1)S(1)} collective-permute-done((bf16[152,1024]{1,0:T(8,128)(2,1)S(1)}, bf16[152,1024]{1,0:T(8,128)(2,1)S(1)}, u32[]{:S(2)}, u32[]{:S(2)}) %collective-permute-start.3) | collective-permute-done | bytes 311328 | tf_op jit(solution)/shard_map/ppermute | solution.py:410
  19.6 1.5 %collective-permute-start.9 = (bf16[152,1024]{1,0:T(8,128)(2,1)S(1)}, bf16[152,1024]{1,0:T(8,128)(2,1)S(1)}, u32[]{:S(2)}, u32[]{:S(2)}) collective-permute-start(bf16[152,1024]{1,0:T(8,128)(2,1)S(1)} %get-tuple-element.56), channel_id=1, source_target_pairs={{0,16},{8,24},{16,0},{24,8},{1,17},{9,25},{17,1},{25,9},{2,18},{10... | collective-permute-start | bytes 933896 | tf_op jit(solution)/shard_map/ppermute | solution.py:410
  21.1 1.7 %early_products.3 = (bf16[32,128,128]{2,1,0:T(8,128)(2,1)S(1)}, f32[128,2048]{1,0:T(8,128)S(1)}) custom-call(bf16[128,4096]{1,0:T(8,128)(2,1)S(1)} %copy-done.1, bf16[128,4096]{1,0:T(8,128)(2,1)S(1)} %copy-done.2, bf16[4096,64]{1,0:T(8,128)(2,1)S(1)} %reshape_squeeze.3.state_ref), custom_call_target="tpu_custom_call" | custom-call | flops 1 | bytes 1 | tf_op jit(solution)/shard_map/early_products/pallas_call | solution.py:71
  23.0 1.4 %first_projection.1.rest_4_ = f32[144,128]{1,0:T(8,128)S(1)} custom-call(bf16[128,4096]{1,0:T(8,128)(2,1)S(1)} %copy-done, bf16[24,4096]{1,0:T(8,128)(2,1)S(1)} %convert_bitcast_fusion.own_ref.refs_0_, bf16[24,4096]{1,0:T(8,128)(2,1)S(1)} %collective-permute-done.1.refs_1_, bf16[24,4096]{1,0:T(8,128)(2,1)} %collective-permute-done.refs_2_, ...), custom_call_target="tpu_custom_call" | custom-call | flops 1 | bytes 1 | tf_op jit(solution)/shard_map/first_projection/pallas_call | solution.py:109
  24.4 4.8 %ssd_backward.1 = (bf16[192,128]{1,0:T(8,128)(2,1)S(1)}, bf16[96,128]{1,0:T(8,128)(2,1)S(1)}, bf16[96,128]{1,0:T(8,128)(2,1)S(1)}) custom-call(s32[2]{0:T(128)S(1)} %pad_add_fusion.where_ref, bf16[128,4096]{1,0:T(8,128)(2,1)S(1)} %copy-done, f32[1,64]{1,0:T(1,128)S(1)} %bitcast.6, f32[1,64]{1,0:T(1,128)S(1)} %bitcast.7, ...), custom_call_target="tpu_custom_call" | custom-call | flops 1 | bytes 1 | tf_op jit(solution)/shard_map/ssd_backward/pallas_call | solution.py:227
  29.8 0.8 %collective-permute-done.7 = bf16[96,128]{1,0:T(8,128)(2,1)S(1)} collective-permute-done((bf16[96,128]{1,0:T(8,128)(2,1)S(1)}, bf16[96,128]{1,0:T(8,128)(2,1)S(1)}, u32[]{:S(2)}, u32[]{:S(2)}) %collective-permute-start.7) | collective-permute-done | bytes 24608 | tf_op jit(solution)/shard_map/ppermute | solution.py:410
  31.3 2.0 %collective-permute-start.12 = (bf16[192,128]{1,0:T(8,128)(2,1)S(1)}, bf16[192,128]{1,0:T(8,128)(2,1)S(1)}, u32[]{:S(2)}, u32[]{:S(2)}) collective-permute-start(bf16[192,128]{1,0:T(8,128)(2,1)S(1)} %constant_dynamic-update-slice_fusion.refs_0_), channel_id=1, source_target_pairs={{0,24},{8,16},{16,8},{24,0},{1,25},{9,17},{17,9},{25,1},{2,26},{10... | collective-permute-start | bytes 147464 | tf_op jit(solution)/shard_map/ppermute | solution.py:410
  33.3 1.0 %collective-permute-start.11 = (bf16[192,128]{1,0:T(8,128)(2,1)S(1)}, bf16[192,128]{1,0:T(8,128)(2,1)S(1)}, u32[]{:S(2)}, u32[]{:S(2)}) collective-permute-start(bf16[192,128]{1,0:T(8,128)(2,1)S(1)} %constant_dynamic-update-slice_fusion.refs_0_), channel_id=1, source_target_pairs={{0,16},{8,24},{16,0},{24,8},{1,17},{9,25},{17,1},{25,9},{2,18},{10... | collective-permute-start | bytes 147464 | tf_op jit(solution)/shard_map/ppermute | solution.py:410
  34.8 1.6 %collective-permute-done.12.refs_3_ = bf16[192,128]{1,0:T(8,128)(2,1)S(1)} collective-permute-done((bf16[192,128]{1,0:T(8,128)(2,1)S(1)}, bf16[192,128]{1,0:T(8,128)(2,1)S(1)}, u32[]{:S(2)}, u32[]{:S(2)}) %collective-permute-start.12) | collective-permute-done | bytes 49184 | tf_op jit(solution)/shard_map/ppermute | solution.py:410
  36.4 0.9 %collective-permute-done.11.refs_2_ = bf16[192,128]{1,0:T(8,128)(2,1)S(1)} collective-permute-done((bf16[192,128]{1,0:T(8,128)(2,1)S(1)}, bf16[192,128]{1,0:T(8,128)(2,1)S(1)}, u32[]{:S(2)}, u32[]{:S(2)}) %collective-permute-start.11) | collective-permute-done | bytes 49184 | tf_op jit(solution)/shard_map/ppermute | solution.py:410
  37.4 1.0 %collective-permute-done.10.refs_1_ = bf16[192,128]{1,0:T(8,128)(2,1)S(1)} collective-permute-done((bf16[192,128]{1,0:T(8,128)(2,1)S(1)}, bf16[192,128]{1,0:T(8,128)(2,1)S(1)}, u32[]{:S(2)}, u32[]{:S(2)}) %collective-permute-start.10) | collective-permute-done | bytes 49184 | tf_op jit(solution)/shard_map/ppermute | solution.py:410
  38.4 1.0 %gradient_slice.1 = (bf16[24,1024]{1,0:T(8,128)(2,1)S(1)}, bf16[24,1024]{1,0:T(8,128)(2,1)S(1)}, bf16[24,1024]{1,0:T(8,128)(2,1)S(1)}, bf16[24,1024]{1,0:T(8,128)(2,1)S(1)}) custom-call(s32[2]{0:T(128)S(1)} %pad_add_fusion.where_ref, bf16[192,128]{1,0:T(8,128)(2,1)S(1)} %constant_dynamic-update-slice_fusion.refs_0_, ...), custom_call_target="tpu_custom_call" | custom-call | tf_op jit(solution)/shard_map/gradient_slice/pallas_call | solution.py:316
  39.4 0.7 %collective-permute-start.14 = (bf16[24,1024]{1,0:T(8,128)(2,1)S(1)}, bf16[24,1024]{1,0:T(8,128)(2,1)S(1)}, u32[]{:S(2)}, u32[]{:S(2)}) collective-permute-start(bf16[24,1024]{1,0:T(8,128)(2,1)S(1)} %get-tuple-element.88), channel_id=1, source_target_pairs={{0,2},{2,0},{4,6},{6,4},{1,3},{3,1},{5,7},{7,5},{8,10},{10,8},{12,... | collective-permute-start | bytes 147464 | tf_op jit(solution)/shard_map/ppermute | solution.py:410
  40.2 2.5 %collective-permute-start.15 = (bf16[24,1024]{1,0:T(8,128)(2,1)S(1)}, bf16[24,1024]{1,0:T(8,128)(2,1)S(1)}, u32[]{:S(2)}, u32[]{:S(2)}) collective-permute-start(bf16[24,1024]{1,0:T(8,128)(2,1)S(1)} %get-tuple-element.89), channel_id=1, source_target_pairs={{0,4},{2,6},{4,0},{6,2},{1,5},{3,7},{5,1},{7,3},{8,12},{10,14},{12... | collective-permute-start | bytes 147464 | tf_op jit(solution)/shard_map/ppermute | solution.py:410
  42.6 1.2 %collective-permute-start.16 = (bf16[24,1024]{1,0:T(8,128)(2,1)S(1)}, bf16[24,1024]{1,0:T(8,128)(2,1)S(1)}, u32[]{:S(2)}, u32[]{:S(2)}) collective-permute-start(bf16[24,1024]{1,0:T(8,128)(2,1)S(1)} %get-tuple-element.90), channel_id=1, source_target_pairs={{0,6},{2,4},{4,2},{6,0},{1,7},{3,5},{5,3},{7,1},{8,14},{10,12},{12... | collective-permute-start | bytes 147464 | tf_op jit(solution)/shard_map/ppermute | solution.py:410
  43.9 2.4 %block_gradient.1 = bf16[128,4096]{1,0:T(8,128)(2,1)} custom-call(bf16[192,128]{1,0:T(8,128)(2,1)S(1)} %get-tuple-element.91.grad_ref, bf16[24,4096]{1,0:T(8,128)(2,1)S(1)} %convert_bitcast_fusion.own_ref.refs_0_, bf16[24,4096]{1,0:T(8,128)(2,1)S(1)} %collective-permute-done.1.refs_1_, bf16[24,4096]{1,0:T(8,128)(2,1)} %collective-permute-done.refs_2_, ...), custom_call_target="tpu_custom_call" | custom-call | flops 201326592 | bytes 3145728 | tf_op jit(solution)/shard_map/block_gradient/pallas_call | solution.py:257
  46.2 2.3 %collective-permute-done.16.refs_3_ = bf16[24,1024]{1,0:T(8,128)(2,1)S(1)} collective-permute-done((bf16[24,1024]{1,0:T(8,128)(2,1)S(1)}, bf16[24,1024]{1,0:T(8,128)(2,1)S(1)}, u32[]{:S(2)}, u32[]{:S(2)}) %collective-permute-start.16) | collective-permute-done | bytes 49184 | tf_op jit(solution)/shard_map/ppermute | solution.py:410
  48.6 1.5 %collective-permute-start.19 = (bf16[24,1024]{1,0:T(8,128)(2,1)S(1)}, bf16[24,1024]{1,0:T(8,128)(2,1)S(1)}, u32[]{:S(2)}, u32[]{:S(2)}) collective-permute-start(bf16[24,1024]{1,0:T(8,128)(2,1)S(1)} %stepped_slice.1.refs_0_), channel_id=1, source_target_pairs={{0,24},{8,16},{16,8},{24,0},{1,25},{9,17},{17,9},{25,1},{2,26},{10... | collective-permute-start | bytes 147464 | tf_op jit(solution)/shard_map/ppermute | solution.py:410
  50.7 1.5 %collective-permute-start.17 = (bf16[24,1024]{1,0:T(8,128)(2,1)S(1)}, bf16[24,1024]{1,0:T(8,128)(2,1)S(1)}, u32[]{:S(2)}, u32[]{:S(2)}) collective-permute-start(bf16[24,1024]{1,0:T(8,128)(2,1)S(1)} %stepped_slice.1.refs_0_), channel_id=1, source_target_pairs={{0,8},{8,0},{16,24},{24,16},{1,9},{9,1},{17,25},{25,17},{2,10},{10... | collective-permute-start | bytes 147464 | tf_op jit(solution)/shard_map/ppermute | solution.py:410
  52.1 1.5 %collective-permute-done.19.refs_3_ = bf16[24,1024]{1,0:T(8,128)(2,1)S(1)} collective-permute-done((bf16[24,1024]{1,0:T(8,128)(2,1)S(1)}, bf16[24,1024]{1,0:T(8,128)(2,1)S(1)}, u32[]{:S(2)}, u32[]{:S(2)}) %collective-permute-start.19) | collective-permute-done | bytes 49184 | tf_op jit(solution)/shard_map/ppermute | solution.py:410
  53.6 0.6 %collective-permute-done.18.refs_2_ = bf16[24,1024]{1,0:T(8,128)(2,1)S(1)} collective-permute-done((bf16[24,1024]{1,0:T(8,128)(2,1)S(1)}, bf16[24,1024]{1,0:T(8,128)(2,1)S(1)}, u32[]{:S(2)}, u32[]{:S(2)}) %collective-permute-start.18) | collective-permute-done | bytes 49184 | tf_op jit(solution)/shard_map/ppermute | solution.py:410
  54.7 1.6 %outer_step.1 = (f32[24,4096]{1,0:T(8,128)}, f32[24,4096]{1,0:T(8,128)}) custom-call(s32[2]{0:T(128)S(1)} %pad_add_fusion.where_ref, f32[24,4096]{1,0:T(8,128)S(1)} %copy-done.3, f32[24,4096]{1,0:T(8,128)S(1)} %copy-done.4, bf16[24,1024]{1,0:T(8,128)(2,1)S(1)} %stepped_slice.1.refs_0_, bf16[24,1024]{1,0:T(8,128)(2,1)S(1)} %collective-permute-done.17.refs_1_, ...), custom_call_target="tpu_custom_call" | custom-call | tf_op jit(solution)/shard_map/outer_step/pallas_call | solution.py:366
  (42 shorter events, 3.1 us)
Async XLA Ops:
  0.7 8.7 %copy-start = (bf16[128,4096]{1,0:T(8,128)(2,1)S(1)}, bf16[128,4096]{1,0:T(8,128)(2,1)}, u32[]{:S(2)}) copy-start(bf16[128,4096]{1,0:T(8,128)(2,1)} %rows_ref.5) | copy-start | bytes 3145732
  1.8 10.8 %copy-start.1 = (bf16[128,4096]{1,0:T(8,128)(2,1)S(1)}, bf16[128,4096]{1,0:T(8,128)(2,1)}, u32[]{:S(2)}) copy-start(bf16[128,4096]{1,0:T(8,128)(2,1)} %cot_ref.3) | copy-start | bytes 3145732
  1.8 12.5 %collective-permute-start.1 = (bf16[24,4096]{1,0:T(8,128)(2,1)S(1)}, bf16[24,4096]{1,0:T(8,128)(2,1)S(1)}, u32[]{:S(2)}, u32[]{:S(2)}) collective-permute-start(bf16[24,4096]{1,0:T(8,128)(2,1)S(1)} %convert_bitcast_fusion.own_ref.refs_0_), channel_id=1, source_target_pairs={{0,2},{2,0},{4,6},{6,4},{1,3},{3,1},{5,7},{7,5},{8,10},{10,8},{12,... | collective-permute-start | bytes 589832 | tf_op jit(solution)/shard_map/ppermute | solution.py:410
  4.9 11.5 %collective-permute-start = (bf16[24,4096]{1,0:T(8,128)(2,1)S(1)}, bf16[24,4096]{1,0:T(8,128)(2,1)}, u32[]{:S(2)}, u32[]{:S(2)}) collective-permute-start(bf16[24,4096]{1,0:T(8,128)(2,1)S(1)} %convert_bitcast_fusion.own_ref.refs_0_), channel_id=1, source_target_pairs={{0,6},{2,4},{4,2},{6,0},{1,7},{3,5},{5,3},{7,1},{8,14},{10,12},{12... | collective-permute-start | bytes 589832 | tf_op jit(solution)/shard_map/ppermute | solution.py:410
  9.5 3.2 %copy-start.2 = (bf16[128,4096]{1,0:T(8,128)(2,1)S(1)}, bf16[128,4096]{1,0:T(8,128)(2,1)}, u32[]{:S(2)}) copy-start(bf16[128,4096]{1,0:T(8,128)(2,1)} %val_ref.3) | copy-start | bytes 3145732
  10.1 9.5 %collective-permute-start.3 = (bf16[152,1024]{1,0:T(8,128)(2,1)S(1)}, bf16[152,1024]{1,0:T(8,128)(2,1)S(1)}, u32[]{:S(2)}, u32[]{:S(2)}) collective-permute-start(bf16[152,1024]{1,0:T(8,128)(2,1)S(1)} %get-tuple-element.57), channel_id=1, source_target_pairs={{0,24},{8,16},{16,8},{24,0},{1,25},{9,17},{17,9},{25,1},{2,26},{10... | collective-permute-start | bytes 933896 | tf_op jit(solution)/shard_map/ppermute | solution.py:410
  14.4 8.5 %collective-permute-start.4 = (bf16[48,4096]{1,0:T(8,128)(2,1)S(1)}, bf16[48,4096]{1,0:T(8,128)(2,1)S(1)}, u32[]{:S(2)}, u32[]{:S(2)}) collective-permute-start(bf16[48,4096]{1,0:T(8,128)(2,1)S(1)} %pad_maximum_fusion.1), channel_id=1, source_target_pairs={{0,1},{1,0},{2,3},{3,2},{4,5},{5,4},{6,7},{7,6},{8,9},{9,8},{10,11... | collective-permute-start | bytes 1179656 | tf_op jit(solution)/shard_map/ppermute | solution.py:410
  16.4 6.4 %collective-permute-start.2 = (bf16[24,4096]{1,0:T(8,128)(2,1)}, bf16[24,4096]{1,0:T(8,128)(2,1)S(1)}, u32[]{:S(2)}, u32[]{:S(2)}) collective-permute-start(bf16[24,4096]{1,0:T(8,128)(2,1)} %collective-permute-done.refs_2_), channel_id=1, source_target_pairs={{0,2},{2,0},{4,6},{6,4},{1,3},{3,1},{5,7},{7,5},{8,10},{10,8},{12,... | collective-permute-start | bytes 589832 | tf_op jit(solution)/shard_map/ppermute | solution.py:410
  17.0 5.8 %collective-permute-start.5 = (bf16[24,4096]{1,0:T(8,128)(2,1)}, bf16[24,4096]{1,0:T(8,128)(2,1)S(1)}, u32[]{:S(2)}, u32[]{:S(2)}) collective-permute-start(bf16[24,4096]{1,0:T(8,128)(2,1)} %collective-permute-done.refs_2_), channel_id=1, source_target_pairs={{0,1},{1,0},{2,3},{3,2},{4,5},{5,4},{6,7},{7,6},{8,9},{9,8},{10,11... | collective-permute-start | bytes 589832 | tf_op jit(solution)/shard_map/ppermute | solution.py:410
  17.0 12.8 %collective-permute-start.8 = (bf16[152,1024]{1,0:T(8,128)(2,1)S(1)}, bf16[152,1024]{1,0:T(8,128)(2,1)S(1)}, u32[]{:S(2)}, u32[]{:S(2)}) collective-permute-start(bf16[152,1024]{1,0:T(8,128)(2,1)S(1)} %get-tuple-element.55), channel_id=1, source_target_pairs={{0,8},{8,0},{16,24},{24,16},{1,9},{9,1},{17,25},{25,17},{2,10},{10... | collective-permute-start | bytes 933896 | tf_op jit(solution)/shard_map/ppermute | solution.py:410
  19.6 10.2 %collective-permute-start.9 = (bf16[152,1024]{1,0:T(8,128)(2,1)S(1)}, bf16[152,1024]{1,0:T(8,128)(2,1)S(1)}, u32[]{:S(2)}, u32[]{:S(2)}) collective-permute-start(bf16[152,1024]{1,0:T(8,128)(2,1)S(1)} %get-tuple-element.56), channel_id=1, source_target_pairs={{0,16},{8,24},{16,0},{24,8},{1,17},{9,25},{17,1},{25,9},{2,18},{10... | collective-permute-start | bytes 933896 | tf_op jit(solution)/shard_map/ppermute | solution.py:410
  22.9 1.5 %copy-start.5 = (f32[64]{0:T(128)S(1)}, f32[64]{0:T(128)}, u32[]{:S(2)}) copy-start(f32[64]{0:T(128)} %param.13) | copy-start | bytes 772
  22.9 1.5 %copy-start.6 = (f32[64]{0:T(128)S(1)}, f32[64]{0:T(128)}, u32[]{:S(2)}) copy-start(f32[64]{0:T(128)} %param.14) | copy-start | bytes 772
  22.9 1.5 %collective-permute-start.6 = (bf16[24,4096]{1,0:T(8,128)(2,1)S(1)}, bf16[24,4096]{1,0:T(8,128)(2,1)S(1)}, u32[]{:S(2)}, u32[]{:S(2)}) collective-permute-start(bf16[24,4096]{1,0:T(8,128)(2,1)S(1)} %collective-permute-done.2.rest_5_.refs_5_), channel_id=1, source_target_pairs={{0,1},{1,0},{2,3},{3,2},{4,5},{5,4},{6,7},{7,6},{8,9},{9,8},{10,11... | collective-permute-start | bytes 589832 | tf_op jit(solution)/shard_map/ppermute | solution.py:410
  29.3 1.4 %collective-permute-start.7 = (bf16[96,128]{1,0:T(8,128)(2,1)S(1)}, bf16[96,128]{1,0:T(8,128)(2,1)S(1)}, u32[]{:S(2)}, u32[]{:S(2)}) collective-permute-start(bf16[96,128]{1,0:T(8,128)(2,1)S(1)} %get-tuple-element.80), channel_id=1, source_target_pairs={{0,1},{1,0},{2,3},{3,2},{4,5},{5,4},{6,7},{7,6},{8,9},{9,8},{10,11... | collective-permute-start | bytes 73736 | tf_op jit(solution)/shard_map/ppermute | solution.py:410
  30.8 7.5 %collective-permute-start.13 = (bf16[512,1024]{1,0:T(8,128)(2,1)S(1)}, bf16[512,1024]{1,0:T(8,128)(2,1)S(1)}, u32[]{:S(2)}, u32[]{:S(2)}) collective-permute-start(bf16[512,1024]{1,0:T(8,128)(2,1)S(1)} %pad_maximum_fusion), channel_id=1, source_target_pairs={{0,1},{1,0},{2,3},{3,2},{4,5},{5,4},{6,7},{7,6},{8,9},{9,8},{10,11... | collective-permute-start | bytes 3145736 | tf_op jit(solution)/shard_map/ppermute | solution.py:410
  31.3 5.2 %collective-permute-start.12 = (bf16[192,128]{1,0:T(8,128)(2,1)S(1)}, bf16[192,128]{1,0:T(8,128)(2,1)S(1)}, u32[]{:S(2)}, u32[]{:S(2)}) collective-permute-start(bf16[192,128]{1,0:T(8,128)(2,1)S(1)} %constant_dynamic-update-slice_fusion.refs_0_), channel_id=1, source_target_pairs={{0,24},{8,16},{16,8},{24,0},{1,25},{9,17},{17,9},{25,1},{2,26},{10... | collective-permute-start | bytes 147464 | tf_op jit(solution)/shard_map/ppermute | solution.py:410
  33.3 4.1 %collective-permute-start.11 = (bf16[192,128]{1,0:T(8,128)(2,1)S(1)}, bf16[192,128]{1,0:T(8,128)(2,1)S(1)}, u32[]{:S(2)}, u32[]{:S(2)}) collective-permute-start(bf16[192,128]{1,0:T(8,128)(2,1)S(1)} %constant_dynamic-update-slice_fusion.refs_0_), channel_id=1, source_target_pairs={{0,16},{8,24},{16,0},{24,8},{1,17},{9,25},{17,1},{25,9},{2,18},{10... | collective-permute-start | bytes 147464 | tf_op jit(solution)/shard_map/ppermute | solution.py:410
  34.3 4.1 %collective-permute-start.10 = (bf16[192,128]{1,0:T(8,128)(2,1)S(1)}, bf16[192,128]{1,0:T(8,128)(2,1)S(1)}, u32[]{:S(2)}, u32[]{:S(2)}) collective-permute-start(bf16[192,128]{1,0:T(8,128)(2,1)S(1)} %constant_dynamic-update-slice_fusion.refs_0_), channel_id=1, source_target_pairs={{0,8},{8,0},{16,24},{24,16},{1,9},{9,1},{17,25},{25,17},{2,10},{10... | collective-permute-start | bytes 147464 | tf_op jit(solution)/shard_map/ppermute | solution.py:410
  39.4 6.8 %collective-permute-start.14 = (bf16[24,1024]{1,0:T(8,128)(2,1)S(1)}, bf16[24,1024]{1,0:T(8,128)(2,1)S(1)}, u32[]{:S(2)}, u32[]{:S(2)}) collective-permute-start(bf16[24,1024]{1,0:T(8,128)(2,1)S(1)} %get-tuple-element.88), channel_id=1, source_target_pairs={{0,2},{2,0},{4,6},{6,4},{1,3},{3,1},{5,7},{7,5},{8,10},{10,8},{12,... | collective-permute-start | bytes 147464 | tf_op jit(solution)/shard_map/ppermute | solution.py:410
  40.2 6.1 %collective-permute-start.15 = (bf16[24,1024]{1,0:T(8,128)(2,1)S(1)}, bf16[24,1024]{1,0:T(8,128)(2,1)S(1)}, u32[]{:S(2)}, u32[]{:S(2)}) collective-permute-start(bf16[24,1024]{1,0:T(8,128)(2,1)S(1)} %get-tuple-element.89), channel_id=1, source_target_pairs={{0,4},{2,6},{4,0},{6,2},{1,5},{3,7},{5,1},{7,3},{8,12},{10,14},{12... | collective-permute-start | bytes 147464 | tf_op jit(solution)/shard_map/ppermute | solution.py:410
  42.6 5.9 %collective-permute-start.16 = (bf16[24,1024]{1,0:T(8,128)(2,1)S(1)}, bf16[24,1024]{1,0:T(8,128)(2,1)S(1)}, u32[]{:S(2)}, u32[]{:S(2)}) collective-permute-start(bf16[24,1024]{1,0:T(8,128)(2,1)S(1)} %get-tuple-element.90), channel_id=1, source_target_pairs={{0,6},{2,4},{4,2},{6,0},{1,7},{3,5},{5,3},{7,1},{8,14},{10,12},{12... | collective-permute-start | bytes 147464 | tf_op jit(solution)/shard_map/ppermute | solution.py:410
  46.2 8.5 %copy-start.3 = (f32[24,4096]{1,0:T(8,128)S(1)}, f32[24,4096]{1,0:T(8,128)}, u32[]{:S(2)}) copy-start(f32[24,4096]{1,0:T(8,128)} %par_ref.1) | copy-start | bytes 1179652
  46.2 8.5 %copy-start.4 = (f32[24,4096]{1,0:T(8,128)S(1)}, f32[24,4096]{1,0:T(8,128)}, u32[]{:S(2)}) copy-start(f32[24,4096]{1,0:T(8,128)} %mom_ref.1) | copy-start | bytes 1179652
  48.6 5.1 %collective-permute-start.19 = (bf16[24,1024]{1,0:T(8,128)(2,1)S(1)}, bf16[24,1024]{1,0:T(8,128)(2,1)S(1)}, u32[]{:S(2)}, u32[]{:S(2)}) collective-permute-start(bf16[24,1024]{1,0:T(8,128)(2,1)S(1)} %stepped_slice.1.refs_0_), channel_id=1, source_target_pairs={{0,24},{8,16},{16,8},{24,0},{1,25},{9,17},{17,9},{25,1},{2,26},{10... | collective-permute-start | bytes 147464 | tf_op jit(solution)/shard_map/ppermute | solution.py:410
  50.1 4.1 %collective-permute-start.18 = (bf16[24,1024]{1,0:T(8,128)(2,1)S(1)}, bf16[24,1024]{1,0:T(8,128)(2,1)S(1)}, u32[]{:S(2)}, u32[]{:S(2)}) collective-permute-start(bf16[24,1024]{1,0:T(8,128)(2,1)S(1)} %stepped_slice.1.refs_0_), channel_id=1, source_target_pairs={{0,16},{8,24},{16,0},{24,8},{1,17},{9,25},{17,1},{25,9},{2,18},{10... | collective-permute-start | bytes 147464 | tf_op jit(solution)/shard_map/ppermute | solution.py:410
  50.7 4.1 %collective-permute-start.17 = (bf16[24,1024]{1,0:T(8,128)(2,1)S(1)}, bf16[24,1024]{1,0:T(8,128)(2,1)S(1)}, u32[]{:S(2)}, u32[]{:S(2)}) collective-permute-start(bf16[24,1024]{1,0:T(8,128)(2,1)S(1)} %stepped_slice.1.refs_0_), channel_id=1, source_target_pairs={{0,8},{8,0},{16,24},{24,16},{1,9},{9,1},{17,25},{25,17},{2,10},{10... | collective-permute-start | bytes 147464 | tf_op jit(solution)/shard_map/ppermute | solution.py:410

commit v5 on v4

--- a/solution.py
+++ b/solution.py
@@ -35,6 +35,21 @@
         out.append(value.astype(jnp.bfloat16))
         value = value - out[-1].astype(jnp.float32)
     return out
+
+
+def round_kernel(wide_ref, out_ref):
+    out_ref[...] = wide_ref[...].astype(out_ref.dtype)
+
+
+def rounded(wide):
+    return pl.pallas_call(
+        round_kernel,
+        in_specs=whole_vmem(1),
+        out_specs=pl.BlockSpec(memory_space=pltpu.VMEM),
+        out_shape=jax.ShapeDtypeStruct(wide.shape, jnp.bfloat16),
+        compiler_params=params(),
+        name="rounded",
+    )(wide)
 
 
 def early_kernel(cot_ref, val_ref, state_ref, cross_ref, enter_ref):
@@ -96,6 +111,10 @@
     return jnp.concatenate([r[...].astype(jnp.float32) for r in refs], axis=0).astype(jnp.bfloat16)
 
 
+def own_place(cores):
+    return lax.axis_index("rep"), lax.axis_index("line") * cores + lax.axis_index("core")
+
+
 def shard_rows(index, k, rows):
     return pl.ds(pl.multiple_of((index ^ k) * rows, 8), rows)
 
@@ -117,9 +136,10 @@
     )(rows_in, *weights)
 
 
-def ssd_kernel(order, first, where_ref, rows_ref, bias_ref, decay_ref, *rest):
+def ssd_kernel(order, first, rows_ref, bias_ref, decay_ref, *rest):
     shards = len(order)
     cross_refs, enter_refs, rest = rest[:2], rest[2:4], rest[4:]
+    _, spot = own_place(2) if shards > 1 else (0, 0)
     first_ref, rest = (rest[0], rest[1:]) if first else (None, rest)
     weight_refs, rest = rest[: shards - first], rest[shards - first :]
     grad_ref, mine_ref, other_ref, proj_ref, col_ref, out_ref = rest
@@ -132,7 +152,7 @@
     else:
         for at, k in enumerate(order):
             source, line = (first_ref, at) if at < first else (arrived, at - first)
-            proj_ref[shard_rows(where_ref[1], k, per), :] = source[line * per : (line + 1) * per]
+            proj_ref[shard_rows(spot, k, per), :] = source[line * per : (line + 1) * per]
     key_t = proj_ref[:STATE, :]
     query_t = proj_ref[STATE : 2 * STATE, :]
     bias_t = jnp.broadcast_to(bias_ref[...], (block, heads)).T
@@ -210,24 +230,23 @@
         mine_ref[...] = jnp.zeros_like(mine_ref)
         other_ref[...] = jnp.zeros_like(other_ref)
         return
-    core = where_ref[1] % 2
+    core = spot % 2
     for part, ref in ((core, mine_ref), (1 - core, other_ref)):
         of_core = [out_ref[shard_rows(f + part, 0, per), :] for f in range(0, shards, 2)]
         ref[...] = jnp.concatenate(of_core, axis=0).astype(jnp.bfloat16)
     for at, k in enumerate(order):
-        proj_ref[at * per : (at + 1) * per, :] = out_ref[shard_rows(where_ref[1], k, per), :]
+        proj_ref[at * per : (at + 1) * per, :] = out_ref[shard_rows(spot, k, per), :]
     grad_ref[...] = proj_ref[...].astype(jnp.bfloat16)
 
 
-def ssd_backward(where, rows_in, step_bias, decay_log, cross, enter, first, weights, order):
+def ssd_backward(rows_in, step_bias, decay_log, cross, enter, first, weights, order):
     block = rows_in.shape[0]
     heads = step_bias.shape[0]
     cols = len(order) * weights[0].shape[0]
     half = (cols // 2, block)
     return pl.pallas_call(
         functools.partial(ssd_kernel, order, len(order) - len(weights)),
-        in_specs=[pl.BlockSpec(memory_space=pltpu.SMEM)]
-        + whole_vmem(7 + len(first) + len(weights)),
+        in_specs=whole_vmem(7 + len(first) + len(weights)),
         out_specs=whole_vmem(3),
         out_shape=[
             jax.ShapeDtypeStruct((cols, block), jnp.bfloat16),
@@ -242,7 +261,7 @@
         compiler_params=params(),
         cost_estimate=pl.CostEstimate(flops=1, bytes_accessed=1, transcendentals=0),
         name="ssd_backward",
-    )(where, rows_in, step_bias.reshape(1, -1), decay_log.reshape(1, -1), *cross, *enter, *first, *weights)
+    )(rows_in, step_bias.reshape(1, -1), decay_log.reshape(1, -1), *cross, *enter, *first, *weights)
 
 
 def block_grad_kernel(grad_ref, *refs):
@@ -267,29 +286,30 @@
     )(grad, *weights)
 
 
-def pieces_kernel(where_ref, rows_ref, own_ref, *outs):
+def pieces_kernel(rows_ref, own_ref, *outs):
     block = rows_ref.shape[0]
+    rep, _ = own_place(2)
     width = outs[0].shape[1]
     for k, out in enumerate(outs):
-        cols = pl.ds(pl.multiple_of((where_ref[0] ^ k) * width, 128), width)
+        cols = pl.ds(pl.multiple_of((rep ^ k) * width, 128), width)
         out[:block, :] = rows_ref[:, cols]
         out[block:, :] = own_ref[:, cols]
 
 
-def column_pieces(where, rows_in, own, replicas):
+def column_pieces(rows_in, own, replicas):
     tokens, depth = rows_in.shape
     shape = (tokens + own.shape[0], depth // replicas)
     return pl.pallas_call(
         pieces_kernel,
-        in_specs=[pl.BlockSpec(memory_space=pltpu.SMEM)] + whole_vmem(2),
+        in_specs=whole_vmem(2),
         out_specs=whole_vmem(replicas),
         out_shape=[jax.ShapeDtypeStruct(shape, jnp.bfloat16)] * replicas,
         compiler_params=params(),
         name="column_pieces",
-    )(where, rows_in, own)
-
-
-def slice_kernel(replicas, where_ref, *refs):
+    )(rows_in, own)
+
+
+def slice_kernel(replicas, *refs):
     grads, pieces, refs = refs[:replicas], refs[replicas : 2 * replicas], refs[2 * replicas :]
     twin, outs, total = refs[0], refs[1:-1], refs[-1]
     tokens = twin.shape[0] // replicas
@@ -305,23 +325,23 @@
         jnp.concatenate(left, axis=1), jnp.concatenate(right, axis=0), ((1,), (0,))
     )
     per = outs[0].shape[0]
-    chip = where_ref[1] // 2
+    chip = lax.axis_index("line")
     for k, out in enumerate(outs):
         out[...] = total[shard_rows(chip, k, per), :].astype(jnp.bfloat16)
 
 
-def gradient_slice(where, grads, pieces, twin, chips):
+def gradient_slice(grads, pieces, twin, chips):
     rows = grads[0].shape[0] // (2 * chips)
     width = twin.shape[1]
     return pl.pallas_call(
         functools.partial(slice_kernel, len(pieces)),
-        in_specs=[pl.BlockSpec(memory_space=pltpu.SMEM)] + whole_vmem(1 + 2 * len(pieces)),
+        in_specs=whole_vmem(1 + 2 * len(pieces)),
         out_specs=whole_vmem(chips),
         out_shape=[jax.ShapeDtypeStruct((rows, width), jnp.bfloat16)] * chips,
         scratch_shapes=[pltpu.VMEM((rows * chips, width), jnp.float32)],
         compiler_params=params(),
         name="gradient_slice",
-    )(where, *grads, *pieces, twin)
+    )(*grads, *pieces, twin)
 
 
 def stepped_kernel(chips, *refs):
@@ -348,11 +368,11 @@
     )(*sums, *pieces)
 
 
-def outer_kernel(where_ref, par_ref, mom_ref, *refs):
+def outer_kernel(par_ref, mom_ref, *refs):
     stepped, (new_par, new_mom, all_ref) = refs[:-3], refs[-3:]
     width = stepped[0].shape[1]
     for k, part in enumerate(stepped):
-        all_ref[where_ref[0] ^ k] = part[...].astype(jnp.float32)
+        all_ref[lax.axis_index("rep") ^ k] = part[...].astype(jnp.float32)
     for r in range(len(stepped)):
         cols = slice(r * width, (r + 1) * width)
         old = par_ref[:, cols]
@@ -362,16 +382,16 @@
         new_par[:, cols] = old - outer_rate * (pseudo + momentum_decay * fresh)
 
 
-def outer_step(where, global_params, momentum, stepped):
+def outer_step(global_params, momentum, stepped):
     return pl.pallas_call(
         outer_kernel,
-        in_specs=[pl.BlockSpec(memory_space=pltpu.SMEM)] + whole_vmem(2 + len(stepped)),
+        in_specs=whole_vmem(2 + len(stepped)),
         out_specs=whole_vmem(2),
         out_shape=[jax.ShapeDtypeStruct(global_params.shape, jnp.float32)] * 2,
         scratch_shapes=[pltpu.VMEM((len(stepped),) + stepped[0].shape, jnp.float32)],
         compiler_params=params(),
         name="outer_step",
-    )(where, global_params, momentum, *stepped)
+    )(global_params, momentum, *stepped)
 
 
 def on_device(
@@ -387,13 +407,9 @@
     momentum,
 ):
     replicas, chips, cores = sizes
-    rep = lax.axis_index("rep")
-    spot = lax.axis_index("line") * cores + lax.axis_index("core")
-    where = jnp.stack([rep, spot]).astype(jnp.int32)
-    where, local_params = lax.optimization_barrier((where, local_params))
     local_rows = local_params[0]
     rows, depth = local_rows.shape
-    own = local_rows.astype(jnp.bfloat16)
+    own = rounded(local_rows)
     seq_width = ssd_input.shape[1]
     blocks = start_state.shape[0]
     block = block_input.shape[0] // blocks
@@ -432,16 +448,16 @@
                 early_products(out_grad[seq], ssd_input[seq], states[b], half, seq_width // 2)
             )
     if fast:
-        pieces = column_pieces(where, block_input, own_late, replicas)
+        pieces = column_pieces(block_input, own_late, replicas)
         far, _ = lax.optimization_barrier((far, pieces))
         pieces = [pieces[0]] + send_each(pieces[1:], "rep")
-        near, early[0] = lax.optimization_barrier((near, early[0]))
-        far, early[0] = lax.optimization_barrier((far, early[0]))
+        far, near, early = lax.optimization_barrier((far, near, early))
         middle = send(far, "line", 1)
         middle, pieces[-1] = lax.optimization_barrier((middle, pieces[-1]))
-        pair = send(jnp.concatenate([own, near], axis=0), "core", 1)
+        late_near, pieces[-1] = lax.optimization_barrier((near, pieces[-1]))
+        pair = send(jnp.concatenate([own, late_near], axis=0), "core", 1)
         weights = [own, near, far, pair, send(far, "core", 1)]
-        middle, early[1], weights = lax.optimization_barrier((middle, early[1], weights))
+        middle, weights = lax.optimization_barrier((middle, weights))
         late = [middle, send(middle, "core", 1)]
 
     begun = []
@@ -455,7 +471,6 @@
     for b in range(blocks):
         seq = slice(b * block, (b + 1) * block)
         parts = ssd_backward(
-            where,
             block_input[seq],
             step_bias,
             decay_log,
@@ -491,12 +506,12 @@
     both = jnp.concatenate([mine, other], axis=0)
     plane = [both] + send_each([both] * (replicas - 1), "rep")
     twin = send(jnp.concatenate([p[:tokens] for p in pieces], axis=0), "core", 1)
-    sums = gradient_slice(where, plane, pieces, twin, chips)
+    sums = gradient_slice(plane, pieces, twin, chips)
     sums = [sums[0]] + send_each(sums[1:], "line")
     sums, block_grad = lax.optimization_barrier((sums, block_grad))
     stepped = stepped_slice(sums, pieces)
     stepped = [stepped] + send_each([stepped] * (replicas - 1), "rep")
-    new_params, new_momentum = outer_step(where, global_params, momentum, stepped)
+    new_params, new_momentum = outer_step(global_params, momentum, stepped)
     return (block_grad, new_params, new_momentum)
 
 

time: 56.5 us -> 57.7 us (1.021)
  waiting for transfers between devices: 12.4 us -> 15.3 us
  Pallas kernels: 15.2 us -> 13 us
  other arithmetic: 1.28 us -> 0.1 us
  local copies, waits for them, and re-layouts: 2.17 us -> 3.17 us
  starting transfers between devices: 24.3 us -> 25.1 us
    ppermute x20, waiting for transfers between devices: 12.4 us -> 15.3 us  [send(): return lax.ppermute(value, axis, [(i, i ^ k) for i in range(count)])]
    pallas_call x3 -> x4, Pallas kernels: 3.23 us -> 1.64 us  [the longest x1 1.03 us: outer_step(): pl.pallas_call(outer_kernel, in_specs=whole_vmem(2 + len(stepped)), out_s...]
    convert_element_type x1 -> x0, other arithmetic: 1.11 us -> none  [on_device(): own = local_rows.astype(jnp.bfloat16)]
    unnamed x15 -> x17, local copies, waits for them, and re-layouts: 0.04 us -> 1.03 us
    ppermute x20, starting transfers between devices: 24.3 us -> 25.1 us  [send(): return lax.ppermute(value, axis, [(i, i ^ k) for i in range(count)])]
    pallas_call x1, Pallas kernels: 4.84 us -> 4.17 us  [ssd_backward(): pl.pallas_call(functools.partial(ssd_kernel, order, len(order) - len(weig...]
  transfers between devices with their start and end apart: 20 -> 20, of which waited for: 10 -> 12; matrix products, arithmetic and copies ran while one was open for 4% -> 4% of each run, Pallas kernels for 22% -> 20%
where the time goes in v5:
time: 57.7 us; the launch traced here: 57.4 us
  starting transfers between devices  25.1 us (44%)
  waiting for transfers between devices  15.3 us (27%)
  Pallas kernels  13 us (23%)
  local copies, waits for them, and re-layouts  3.17 us (5%)
  between operations  0.85 us (1%)
    ppermute x20, starting transfers between devices, send(): return lax.ppermute(value, axis, [(i, i ^ k) for i in range(count)])  25.1 us
    ppermute x20, waiting for transfers between devices, send(): return lax.ppermute(value, axis, [(i, i ^ k) for i in range(count)])  15.3 us
    pallas_call x1, Pallas kernels, ssd_backward(): pl.pallas_call(functools.partial(ssd_kernel, order, len(order) - len(weig...  4.17 us
    pallas_call x2, Pallas kernels, early_products(): pl.pallas_call(early_kernel, grid=(steps,), in_specs=[pl.BlockSpec((block...  3.35 us
    pallas_call x1, Pallas kernels, block_gradient(): pl.pallas_call(block_grad_kernel, in_specs=whole_vmem(1 + len(weights)),...  2.35 us
    another operation x1, local copies, waits for them, and re-layouts, on_device(): states = [start_state[b].reshape(seq_width, STATE) for b in range(blocks)]  2.05 us
    pallas_call x1, Pallas kernels, first_projection(): pl.pallas_call(first_kernel, in_specs=whole_vmem(1 + len(weights)), out_s...  1.39 us
  transfers between devices with their start and end apart: 20, of which 12 were waited for; matrix products, arithmetic and copies ran while one was open for 4% of the time, Pallas kernels for 20%

profile of v5, /device:TPU:0, one launch (start us, length us, event | category | flops | bytes accessed | tf_op | source)
XLA Modules:
  0.0 57.4 jit_solution(13638208254686948684)
XLA Ops:
  0.6 1.0 %copy-done.3 = f32[1,24,4096]{2,1,0:T(8,128)S(1)} copy-done((f32[1,24,4096]{2,1,0:T(8,128)S(1)}, f32[1,24,4096]{2,1,0:T(8,128)}, u32[]{:S(2)}) %copy-start.3) | copy-done | bytes 393240
  1.7 5.1 %collective-permute-start = (bf16[24,4096]{1,0:T(8,128)(2,1)S(1)}, bf16[24,4096]{1,0:T(8,128)(2,1)}, u32[]{:S(2)}, u32[]{:S(2)}) collective-permute-start(bf16[24,4096]{1,0:T(8,128)(2,1)S(1)} %rounded.1.own_ref.refs_0_), channel_id=1, source_target_pairs={{0,6},{2,4},{4,2},{6,0},{1,7},{3,5},{5,3},{7,1},{8,14},{10,12},{12... | collective-permute-start | bytes 589832 | tf_op jit(solution)/shard_map/ppermute | solution.py:426
  6.8 2.1 %reshape_squeeze.3.state_ref = bf16[4096,64]{1,0:T(8,128)(2,1)S(1)} reshape(bf16[1,64,4096]{2,1,0:T(8,128)(2,1)} %param.12) | data formatting | bytes 1048576 | tf_op jit(solution)/shard_map/reshape;squeeze | solution.py:442
  9.0 2.5 %collective-permute-start.3 = (bf16[152,1024]{1,0:T(8,128)(2,1)S(1)}, bf16[152,1024]{1,0:T(8,128)(2,1)S(1)}, u32[]{:S(2)}, u32[]{:S(2)}) collective-permute-start(bf16[152,1024]{1,0:T(8,128)(2,1)S(1)} %get-tuple-element.53), channel_id=1, source_target_pairs={{0,24},{8,16},{16,8},{24,0},{1,25},{9,17},{17,9},{25,1},{2,26},{10... | collective-permute-start | bytes 933896 | tf_op jit(solution)/shard_map/ppermute | solution.py:426
  11.5 1.7 %early_products.2 = (bf16[32,128,128]{2,1,0:T(8,128)(2,1)S(1)}, f32[128,2048]{1,0:T(8,128)S(1)}) custom-call(bf16[128,4096]{1,0:T(8,128)(2,1)S(1)} %copy-done.1, bf16[128,4096]{1,0:T(8,128)(2,1)S(1)} %copy-done.2, bf16[4096,64]{1,0:T(8,128)(2,1)S(1)} %reshape_squeeze.3.state_ref), custom_call_target="tpu_custom_call" | custom-call | flops 1 | bytes 1 | tf_op jit(solution)/shard_map/early_products/pallas_call | solution.py:86
  13.2 1.7 %early_products.3 = (bf16[32,128,128]{2,1,0:T(8,128)(2,1)S(1)}, f32[128,2048]{1,0:T(8,128)S(1)}) custom-call(bf16[128,4096]{1,0:T(8,128)(2,1)S(1)} %copy-done.1, bf16[128,4096]{1,0:T(8,128)(2,1)S(1)} %copy-done.2, bf16[4096,64]{1,0:T(8,128)(2,1)S(1)} %reshape_squeeze.3.state_ref), custom_call_target="tpu_custom_call" | custom-call | flops 1 | bytes 1 | tf_op jit(solution)/shard_map/early_products/pallas_call | solution.py:86
  14.9 1.1 %collective-permute-done.1.refs_1_ = bf16[24,4096]{1,0:T(8,128)(2,1)S(1)} collective-permute-done((bf16[24,4096]{1,0:T(8,128)(2,1)S(1)}, bf16[24,4096]{1,0:T(8,128)(2,1)S(1)}, u32[]{:S(2)}, u32[]{:S(2)}) %collective-permute-start.1) | collective-permute-done | bytes 196640 | tf_op jit(solution)/shard_map/ppermute | solution.py:426
  16.0 1.7 %collective-permute-start.2 = (bf16[24,4096]{1,0:T(8,128)(2,1)}, bf16[24,4096]{1,0:T(8,128)(2,1)S(1)}, u32[]{:S(2)}, u32[]{:S(2)}) collective-permute-start(bf16[24,4096]{1,0:T(8,128)(2,1)} %collective-permute-done.refs_2_), channel_id=1, source_target_pairs={{0,2},{2,0},{4,6},{6,4},{1,3},{3,1},{5,7},{7,5},{8,10},{10,8},{12,... | collective-permute-start | bytes 589832 | tf_op jit(solution)/shard_map/ppermute | solution.py:426
  17.7 1.1 %collective-permute-done.3.refs_7_ = bf16[152,1024]{1,0:T(8,128)(2,1)S(1)} collective-permute-done((bf16[152,1024]{1,0:T(8,128)(2,1)S(1)}, bf16[152,1024]{1,0:T(8,128)(2,1)S(1)}, u32[]{:S(2)}, u32[]{:S(2)}) %collective-permute-start.3) | collective-permute-done | bytes 311328 | tf_op jit(solution)/shard_map/ppermute | solution.py:426
  18.8 4.3 %collective-permute-done.2.rest_5_.refs_5_ = bf16[24,4096]{1,0:T(8,128)(2,1)S(1)} collective-permute-done((bf16[24,4096]{1,0:T(8,128)(2,1)}, bf16[24,4096]{1,0:T(8,128)(2,1)S(1)}, u32[]{:S(2)}, u32[]{:S(2)}) %collective-permute-start.2) | collective-permute-done | bytes 196640 | tf_op jit(solution)/shard_map/ppermute | solution.py:426
  23.2 0.5 collective-permute-start.5
  23.7 1.5 %collective-permute-start.8 = (bf16[152,1024]{1,0:T(8,128)(2,1)S(1)}, bf16[152,1024]{1,0:T(8,128)(2,1)S(1)}, u32[]{:S(2)}, u32[]{:S(2)}) collective-permute-start(bf16[152,1024]{1,0:T(8,128)(2,1)S(1)} %get-tuple-element.51), channel_id=1, source_target_pairs={{0,8},{8,0},{16,24},{24,16},{1,9},{9,1},{17,25},{25,17},{2,10},{10... | collective-permute-start | bytes 933896 | tf_op jit(solution)/shard_map/ppermute | solution.py:426
  25.2 1.5 %collective-permute-start.9 = (bf16[152,1024]{1,0:T(8,128)(2,1)S(1)}, bf16[152,1024]{1,0:T(8,128)(2,1)S(1)}, u32[]{:S(2)}, u32[]{:S(2)}) collective-permute-start(bf16[152,1024]{1,0:T(8,128)(2,1)S(1)} %get-tuple-element.52), channel_id=1, source_target_pairs={{0,16},{8,24},{16,0},{24,8},{1,17},{9,25},{17,1},{25,9},{2,18},{10... | collective-permute-start | bytes 933896 | tf_op jit(solution)/shard_map/ppermute | solution.py:426
  26.7 1.4 %first_projection.1.rest_4_ = f32[144,128]{1,0:T(8,128)S(1)} custom-call(bf16[128,4096]{1,0:T(8,128)(2,1)S(1)} %copy-done, bf16[24,4096]{1,0:T(8,128)(2,1)S(1)} %rounded.1.own_ref.refs_0_, bf16[24,4096]{1,0:T(8,128)(2,1)S(1)} %collective-permute-done.1.refs_1_, bf16[24,4096]{1,0:T(8,128)(2,1)} %collective-permute-done.refs_2_, ...), custom_call_target="tpu_custom_call" | custom-call | flops 1 | bytes 1 | tf_op jit(solution)/shard_map/first_projection/pallas_call | solution.py:128
  28.1 4.2 %ssd_backward.1 = (bf16[192,128]{1,0:T(8,128)(2,1)S(1)}, bf16[96,128]{1,0:T(8,128)(2,1)S(1)}, bf16[96,128]{1,0:T(8,128)(2,1)S(1)}) custom-call(bf16[128,4096]{1,0:T(8,128)(2,1)S(1)} %copy-done, f32[1,64]{1,0:T(1,128)S(1)} %bitcast.4, f32[1,64]{1,0:T(1,128)S(1)} %bitcast.5, bf16[32,128,128]{2,1,0:T(8,128)(2,1)S(1)} %get-tuple-element.60.rest_0_, ...), custom_call_target="tpu_custom_call" | custom-call | flops 1 | bytes 1 | tf_op jit(solution)/shard_map/ssd_backward/pallas_call | solution.py:247
  32.3 0.6 collective-permute-start.7
  33.0 1.2 %collective-permute-done.9.refs_6_ = bf16[152,1024]{1,0:T(8,128)(2,1)S(1)} collective-permute-done((bf16[152,1024]{1,0:T(8,128)(2,1)S(1)}, bf16[152,1024]{1,0:T(8,128)(2,1)S(1)}, u32[]{:S(2)}, u32[]{:S(2)}) %collective-permute-start.9) | collective-permute-done | bytes 311328 | tf_op jit(solution)/shard_map/ppermute | solution.py:426
  34.5 0.6 %collective-permute-start.10 = (bf16[192,128]{1,0:T(8,128)(2,1)S(1)}, bf16[192,128]{1,0:T(8,128)(2,1)S(1)}, u32[]{:S(2)}, u32[]{:S(2)}) collective-permute-start(bf16[192,128]{1,0:T(8,128)(2,1)S(1)} %constant_dynamic-update-slice_fusion.refs_0_), channel_id=1, source_target_pairs={{0,8},{8,0},{16,24},{24,16},{1,9},{9,1},{17,25},{25,17},{2,10},{10... | collective-permute-start | bytes 147464 | tf_op jit(solution)/shard_map/ppermute | solution.py:426
  35.1 1.5 %collective-permute-start.11 = (bf16[192,128]{1,0:T(8,128)(2,1)S(1)}, bf16[192,128]{1,0:T(8,128)(2,1)S(1)}, u32[]{:S(2)}, u32[]{:S(2)}) collective-permute-start(bf16[192,128]{1,0:T(8,128)(2,1)S(1)} %constant_dynamic-update-slice_fusion.refs_0_), channel_id=1, source_target_pairs={{0,16},{8,24},{16,0},{24,8},{1,17},{9,25},{17,1},{25,9},{2,18},{10... | collective-permute-start | bytes 147464 | tf_op jit(solution)/shard_map/ppermute | solution.py:426
  36.6 1.4 %collective-permute-start.12 = (bf16[192,128]{1,0:T(8,128)(2,1)S(1)}, bf16[192,128]{1,0:T(8,128)(2,1)S(1)}, u32[]{:S(2)}, u32[]{:S(2)}) collective-permute-start(bf16[192,128]{1,0:T(8,128)(2,1)S(1)} %constant_dynamic-update-slice_fusion.refs_0_), channel_id=1, source_target_pairs={{0,24},{8,16},{16,8},{24,0},{1,25},{9,17},{17,9},{25,1},{2,26},{10... | collective-permute-start | bytes 147464 | tf_op jit(solution)/shard_map/ppermute | solution.py:426
  38.1 0.6 %collective-permute-done.10.refs_1_ = bf16[192,128]{1,0:T(8,128)(2,1)S(1)} collective-permute-done((bf16[192,128]{1,0:T(8,128)(2,1)S(1)}, bf16[192,128]{1,0:T(8,128)(2,1)S(1)}, u32[]{:S(2)}, u32[]{:S(2)}) %collective-permute-start.10) | collective-permute-done | bytes 49184 | tf_op jit(solution)/shard_map/ppermute | solution.py:426
  39.2 2.4 %collective-permute-done.12.refs_3_ = bf16[192,128]{1,0:T(8,128)(2,1)S(1)} collective-permute-done((bf16[192,128]{1,0:T(8,128)(2,1)S(1)}, bf16[192,128]{1,0:T(8,128)(2,1)S(1)}, u32[]{:S(2)}, u32[]{:S(2)}) %collective-permute-start.12) | collective-permute-done | bytes 49184 | tf_op jit(solution)/shard_map/ppermute | solution.py:426
  42.1 0.7 %collective-permute-start.14 = (bf16[24,1024]{1,0:T(8,128)(2,1)S(1)}, bf16[24,1024]{1,0:T(8,128)(2,1)S(1)}, u32[]{:S(2)}, u32[]{:S(2)}) collective-permute-start(bf16[24,1024]{1,0:T(8,128)(2,1)S(1)} %get-tuple-element.84), channel_id=1, source_target_pairs={{0,2},{2,0},{4,6},{6,4},{1,3},{3,1},{5,7},{7,5},{8,10},{10,8},{12,... | collective-permute-start | bytes 147464 | tf_op jit(solution)/shard_map/ppermute | solution.py:426
  43.3 3.2 %collective-permute-start.16 = (bf16[24,1024]{1,0:T(8,128)(2,1)S(1)}, bf16[24,1024]{1,0:T(8,128)(2,1)S(1)}, u32[]{:S(2)}, u32[]{:S(2)}) collective-permute-start(bf16[24,1024]{1,0:T(8,128)(2,1)S(1)} %get-tuple-element.86), channel_id=1, source_target_pairs={{0,6},{2,4},{4,2},{6,0},{1,7},{3,5},{5,3},{7,1},{8,14},{10,12},{12... | collective-permute-start | bytes 147464 | tf_op jit(solution)/shard_map/ppermute | solution.py:426
  46.6 2.4 %block_gradient.1 = bf16[128,4096]{1,0:T(8,128)(2,1)} custom-call(bf16[192,128]{1,0:T(8,128)(2,1)S(1)} %get-tuple-element.87.grad_ref, bf16[24,4096]{1,0:T(8,128)(2,1)S(1)} %rounded.1.own_ref.refs_0_, bf16[24,4096]{1,0:T(8,128)(2,1)S(1)} %collective-permute-done.1.refs_1_, bf16[24,4096]{1,0:T(8,128)(2,1)} %collective-permute-done.refs_2_, ...), custom_call_target="tpu_custom_call" | custom-call | flops 201326592 | bytes 3145728 | tf_op jit(solution)/shard_map/block_gradient/pallas_call | solution.py:276
  49.3 1.6 %collective-permute-start.17 = (bf16[24,1024]{1,0:T(8,128)(2,1)S(1)}, bf16[24,1024]{1,0:T(8,128)(2,1)S(1)}, u32[]{:S(2)}, u32[]{:S(2)}) collective-permute-start(bf16[24,1024]{1,0:T(8,128)(2,1)S(1)} %stepped_slice.1.refs_0_), channel_id=1, source_target_pairs={{0,8},{8,0},{16,24},{24,16},{1,9},{9,1},{17,25},{25,17},{2,10},{10... | collective-permute-start | bytes 147464 | tf_op jit(solution)/shard_map/ppermute | solution.py:426
  50.9 0.5 collective-permute-start.18
  51.4 1.5 %collective-permute-start.19 = (bf16[24,1024]{1,0:T(8,128)(2,1)S(1)}, bf16[24,1024]{1,0:T(8,128)(2,1)S(1)}, u32[]{:S(2)}, u32[]{:S(2)}) collective-permute-start(bf16[24,1024]{1,0:T(8,128)(2,1)S(1)} %stepped_slice.1.refs_0_), channel_id=1, source_target_pairs={{0,24},{8,16},{16,8},{24,0},{1,25},{9,17},{17,9},{25,1},{2,26},{10... | collective-permute-start | bytes 147464 | tf_op jit(solution)/shard_map/ppermute | solution.py:426
  52.9 0.6 %collective-permute-done.17.refs_1_ = bf16[24,1024]{1,0:T(8,128)(2,1)S(1)} collective-permute-done((bf16[24,1024]{1,0:T(8,128)(2,1)S(1)}, bf16[24,1024]{1,0:T(8,128)(2,1)S(1)}, u32[]{:S(2)}, u32[]{:S(2)}) %collective-permute-start.17) | collective-permute-done | bytes 49184 | tf_op jit(solution)/shard_map/ppermute | solution.py:426
  53.5 1.5 %collective-permute-done.18.refs_2_ = bf16[24,1024]{1,0:T(8,128)(2,1)S(1)} collective-permute-done((bf16[24,1024]{1,0:T(8,128)(2,1)S(1)}, bf16[24,1024]{1,0:T(8,128)(2,1)S(1)}, u32[]{:S(2)}, u32[]{:S(2)}) %collective-permute-start.18) | collective-permute-done | bytes 49184 | tf_op jit(solution)/shard_map/ppermute | solution.py:426
  55.0 1.4 %collective-permute-done.19.refs_3_ = bf16[24,1024]{1,0:T(8,128)(2,1)S(1)} collective-permute-done((bf16[24,1024]{1,0:T(8,128)(2,1)S(1)}, bf16[24,1024]{1,0:T(8,128)(2,1)S(1)}, u32[]{:S(2)}, u32[]{:S(2)}) %collective-permute-start.19) | collective-permute-done | bytes 49184 | tf_op jit(solution)/shard_map/ppermute | solution.py:426
  56.4 1.0 %outer_step.1 = (f32[24,4096]{1,0:T(8,128)}, f32[24,4096]{1,0:T(8,128)}) custom-call(f32[24,4096]{1,0:T(8,128)S(1)} %copy-done.4, f32[24,4096]{1,0:T(8,128)S(1)} %copy-done.5, bf16[24,1024]{1,0:T(8,128)(2,1)S(1)} %stepped_slice.1.refs_0_, bf16[24,1024]{1,0:T(8,128)(2,1)S(1)} %collective-permute-done.17.refs_1_, ...), custom_call_target="tpu_custom_call" | custom-call | tf_op jit(solution)/shard_map/outer_step/pallas_call | solution.py:386
  (43 shorter events, 2.5 us)
Async XLA Ops:
  0.6 1.0 %copy-start.3 = (f32[1,24,4096]{2,1,0:T(8,128)S(1)}, f32[1,24,4096]{2,1,0:T(8,128)}, u32[]{:S(2)}) copy-start(f32[1,24,4096]{2,1,0:T(8,128)} %param.15) | copy-start | bytes 1179652
  1.6 7.2 %copy-start = (bf16[128,4096]{1,0:T(8,128)(2,1)S(1)}, bf16[128,4096]{1,0:T(8,128)(2,1)}, u32[]{:S(2)}) copy-start(bf16[128,4096]{1,0:T(8,128)(2,1)} %rows_ref.5) | copy-start | bytes 3145732
  1.7 9.8 %copy-start.1 = (bf16[128,4096]{1,0:T(8,128)(2,1)S(1)}, bf16[128,4096]{1,0:T(8,128)(2,1)}, u32[]{:S(2)}) copy-start(bf16[128,4096]{1,0:T(8,128)(2,1)} %cot_ref.3) | copy-start | bytes 3145732
  1.7 13.2 %collective-permute-start = (bf16[24,4096]{1,0:T(8,128)(2,1)S(1)}, bf16[24,4096]{1,0:T(8,128)(2,1)}, u32[]{:S(2)}, u32[]{:S(2)}) collective-permute-start(bf16[24,4096]{1,0:T(8,128)(2,1)S(1)} %rounded.1.own_ref.refs_0_), channel_id=1, source_target_pairs={{0,6},{2,4},{4,2},{6,0},{1,7},{3,5},{5,3},{7,1},{8,14},{10,12},{12... | collective-permute-start | bytes 589832 | tf_op jit(solution)/shard_map/ppermute | solution.py:426
  6.8 9.2 %collective-permute-start.1 = (bf16[24,4096]{1,0:T(8,128)(2,1)S(1)}, bf16[24,4096]{1,0:T(8,128)(2,1)S(1)}, u32[]{:S(2)}, u32[]{:S(2)}) collective-permute-start(bf16[24,4096]{1,0:T(8,128)(2,1)S(1)} %rounded.1.own_ref.refs_0_), channel_id=1, source_target_pairs={{0,2},{2,0},{4,6},{6,4},{1,3},{3,1},{5,7},{7,5},{8,10},{10,8},{12,... | collective-permute-start | bytes 589832 | tf_op jit(solution)/shard_map/ppermute | solution.py:426
  8.9 2.6 %copy-start.2 = (bf16[128,4096]{1,0:T(8,128)(2,1)S(1)}, bf16[128,4096]{1,0:T(8,128)(2,1)}, u32[]{:S(2)}) copy-start(bf16[128,4096]{1,0:T(8,128)(2,1)} %val_ref.3) | copy-start | bytes 3145732
  9.0 9.8 %collective-permute-start.3 = (bf16[152,1024]{1,0:T(8,128)(2,1)S(1)}, bf16[152,1024]{1,0:T(8,128)(2,1)S(1)}, u32[]{:S(2)}, u32[]{:S(2)}) collective-permute-start(bf16[152,1024]{1,0:T(8,128)(2,1)S(1)} %get-tuple-element.53), channel_id=1, source_target_pairs={{0,24},{8,16},{16,8},{24,0},{1,25},{9,17},{17,9},{25,1},{2,26},{10... | collective-permute-start | bytes 933896 | tf_op jit(solution)/shard_map/ppermute | solution.py:426
  16.0 7.0 %collective-permute-start.2 = (bf16[24,4096]{1,0:T(8,128)(2,1)}, bf16[24,4096]{1,0:T(8,128)(2,1)S(1)}, u32[]{:S(2)}, u32[]{:S(2)}) collective-permute-start(bf16[24,4096]{1,0:T(8,128)(2,1)} %collective-permute-done.refs_2_), channel_id=1, source_target_pairs={{0,2},{2,0},{4,6},{6,4},{1,3},{3,1},{5,7},{7,5},{8,10},{10,8},{12,... | collective-permute-start | bytes 589832 | tf_op jit(solution)/shard_map/ppermute | solution.py:426
  23.1 5.1 %copy-start.6 = (f32[64]{0:T(128)S(1)}, f32[64]{0:T(128)}, u32[]{:S(2)}) copy-start(f32[64]{0:T(128)} %param.13) | copy-start | bytes 772
  23.1 5.1 %copy-start.7 = (f32[64]{0:T(128)S(1)}, f32[64]{0:T(128)}, u32[]{:S(2)}) copy-start(f32[64]{0:T(128)} %param.14) | copy-start | bytes 772
  23.1 3.6 %collective-permute-start.4 = (bf16[48,4096]{1,0:T(8,128)(2,1)S(1)}, bf16[48,4096]{1,0:T(8,128)(2,1)S(1)}, u32[]{:S(2)}, u32[]{:S(2)}) collective-permute-start(bf16[48,4096]{1,0:T(8,128)(2,1)S(1)} %pad_maximum_fusion.1), channel_id=1, source_target_pairs={{0,1},{1,0},{2,3},{3,2},{4,5},{5,4},{6,7},{7,6},{8,9},{9,8},{10,11... | collective-permute-start | bytes 1179656 | tf_op jit(solution)/shard_map/ppermute | solution.py:426
  23.2 3.5 %collective-permute-start.5 = (bf16[24,4096]{1,0:T(8,128)(2,1)}, bf16[24,4096]{1,0:T(8,128)(2,1)S(1)}, u32[]{:S(2)}, u32[]{:S(2)}) collective-permute-start(bf16[24,4096]{1,0:T(8,128)(2,1)} %collective-permute-done.refs_2_), channel_id=1, source_target_pairs={{0,1},{1,0},{2,3},{3,2},{4,5},{5,4},{6,7},{7,6},{8,9},{9,8},{10,11... | collective-permute-start | bytes 589832 | tf_op jit(solution)/shard_map/ppermute | solution.py:426
  23.7 9.3 %collective-permute-start.8 = (bf16[152,1024]{1,0:T(8,128)(2,1)S(1)}, bf16[152,1024]{1,0:T(8,128)(2,1)S(1)}, u32[]{:S(2)}, u32[]{:S(2)}) collective-permute-start(bf16[152,1024]{1,0:T(8,128)(2,1)S(1)} %get-tuple-element.51), channel_id=1, source_target_pairs={{0,8},{8,0},{16,24},{24,16},{1,9},{9,1},{17,25},{25,17},{2,10},{10... | collective-permute-start | bytes 933896 | tf_op jit(solution)/shard_map/ppermute | solution.py:426
  25.2 9.1 %collective-permute-start.9 = (bf16[152,1024]{1,0:T(8,128)(2,1)S(1)}, bf16[152,1024]{1,0:T(8,128)(2,1)S(1)}, u32[]{:S(2)}, u32[]{:S(2)}) collective-permute-start(bf16[152,1024]{1,0:T(8,128)(2,1)S(1)} %get-tuple-element.52), channel_id=1, source_target_pairs={{0,16},{8,24},{16,0},{24,8},{1,17},{9,25},{17,1},{25,9},{2,18},{10... | collective-permute-start | bytes 933896 | tf_op jit(solution)/shard_map/ppermute | solution.py:426
  26.7 1.4 %collective-permute-start.6 = (bf16[24,4096]{1,0:T(8,128)(2,1)S(1)}, bf16[24,4096]{1,0:T(8,128)(2,1)S(1)}, u32[]{:S(2)}, u32[]{:S(2)}) collective-permute-start(bf16[24,4096]{1,0:T(8,128)(2,1)S(1)} %collective-permute-done.2.rest_5_.refs_5_), channel_id=1, source_target_pairs={{0,1},{1,0},{2,3},{3,2},{4,5},{5,4},{6,7},{7,6},{8,9},{9,8},{10,11... | collective-permute-start | bytes 589832 | tf_op jit(solution)/shard_map/ppermute | solution.py:426
  32.3 1.9 %collective-permute-start.7 = (bf16[96,128]{1,0:T(8,128)(2,1)S(1)}, bf16[96,128]{1,0:T(8,128)(2,1)S(1)}, u32[]{:S(2)}, u32[]{:S(2)}) collective-permute-start(bf16[96,128]{1,0:T(8,128)(2,1)S(1)} %get-tuple-element.76), channel_id=1, source_target_pairs={{0,1},{1,0},{2,3},{3,2},{4,5},{5,4},{6,7},{7,6},{8,9},{9,8},{10,11... | collective-permute-start | bytes 73736 | tf_op jit(solution)/shard_map/ppermute | solution.py:426
  34.4 7.2 %collective-permute-start.13 = (bf16[512,1024]{1,0:T(8,128)(2,1)S(1)}, bf16[512,1024]{1,0:T(8,128)(2,1)S(1)}, u32[]{:S(2)}, u32[]{:S(2)}) collective-permute-start(bf16[512,1024]{1,0:T(8,128)(2,1)S(1)} %pad_maximum_fusion), channel_id=1, source_target_pairs={{0,1},{1,0},{2,3},{3,2},{4,5},{5,4},{6,7},{7,6},{8,9},{9,8},{10,11... | collective-permute-start | bytes 3145736 | tf_op jit(solution)/shard_map/ppermute | solution.py:426
  34.5 4.2 %collective-permute-start.10 = (bf16[192,128]{1,0:T(8,128)(2,1)S(1)}, bf16[192,128]{1,0:T(8,128)(2,1)S(1)}, u32[]{:S(2)}, u32[]{:S(2)}) collective-permute-start(bf16[192,128]{1,0:T(8,128)(2,1)S(1)} %constant_dynamic-update-slice_fusion.refs_0_), channel_id=1, source_target_pairs={{0,8},{8,0},{16,24},{24,16},{1,9},{9,1},{17,25},{25,17},{2,10},{10... | collective-permute-start | bytes 147464 | tf_op jit(solution)/shard_map/ppermute | solution.py:426
  35.1 4.1 %collective-permute-start.11 = (bf16[192,128]{1,0:T(8,128)(2,1)S(1)}, bf16[192,128]{1,0:T(8,128)(2,1)S(1)}, u32[]{:S(2)}, u32[]{:S(2)}) collective-permute-start(bf16[192,128]{1,0:T(8,128)(2,1)S(1)} %constant_dynamic-update-slice_fusion.refs_0_), channel_id=1, source_target_pairs={{0,16},{8,24},{16,0},{24,8},{1,17},{9,25},{17,1},{25,9},{2,18},{10... | collective-permute-start | bytes 147464 | tf_op jit(solution)/shard_map/ppermute | solution.py:426
  36.6 5.0 %collective-permute-start.12 = (bf16[192,128]{1,0:T(8,128)(2,1)S(1)}, bf16[192,128]{1,0:T(8,128)(2,1)S(1)}, u32[]{:S(2)}, u32[]{:S(2)}) collective-permute-start(bf16[192,128]{1,0:T(8,128)(2,1)S(1)} %constant_dynamic-update-slice_fusion.refs_0_), channel_id=1, source_target_pairs={{0,24},{8,16},{16,8},{24,0},{1,25},{9,17},{17,9},{25,1},{2,26},{10... | collective-permute-start | bytes 147464 | tf_op jit(solution)/shard_map/ppermute | solution.py:426
  42.1 6.8 %collective-permute-start.14 = (bf16[24,1024]{1,0:T(8,128)(2,1)S(1)}, bf16[24,1024]{1,0:T(8,128)(2,1)S(1)}, u32[]{:S(2)}, u32[]{:S(2)}) collective-permute-start(bf16[24,1024]{1,0:T(8,128)(2,1)S(1)} %get-tuple-element.84), channel_id=1, source_target_pairs={{0,2},{2,0},{4,6},{6,4},{1,3},{3,1},{5,7},{7,5},{8,10},{10,8},{12,... | collective-permute-start | bytes 147464 | tf_op jit(solution)/shard_map/ppermute | solution.py:426
  42.9 6.1 %collective-permute-start.15 = (bf16[24,1024]{1,0:T(8,128)(2,1)S(1)}, bf16[24,1024]{1,0:T(8,128)(2,1)S(1)}, u32[]{:S(2)}, u32[]{:S(2)}) collective-permute-start(bf16[24,1024]{1,0:T(8,128)(2,1)S(1)} %get-tuple-element.85), channel_id=1, source_target_pairs={{0,4},{2,6},{4,0},{6,2},{1,5},{3,7},{5,1},{7,3},{8,12},{10,14},{12... | collective-permute-start | bytes 147464 | tf_op jit(solution)/shard_map/ppermute | solution.py:426
  43.3 5.9 %collective-permute-start.16 = (bf16[24,1024]{1,0:T(8,128)(2,1)S(1)}, bf16[24,1024]{1,0:T(8,128)(2,1)S(1)}, u32[]{:S(2)}, u32[]{:S(2)}) collective-permute-start(bf16[24,1024]{1,0:T(8,128)(2,1)S(1)} %get-tuple-element.86), channel_id=1, source_target_pairs={{0,6},{2,4},{4,2},{6,0},{1,7},{3,5},{5,3},{7,1},{8,14},{10,12},{12... | collective-permute-start | bytes 147464 | tf_op jit(solution)/shard_map/ppermute | solution.py:426
  48.9 7.5 %copy-start.4 = (f32[24,4096]{1,0:T(8,128)S(1)}, f32[24,4096]{1,0:T(8,128)}, u32[]{:S(2)}) copy-start(f32[24,4096]{1,0:T(8,128)} %par_ref.1) | copy-start | bytes 1179652
  48.9 7.5 %copy-start.5 = (f32[24,4096]{1,0:T(8,128)S(1)}, f32[24,4096]{1,0:T(8,128)}, u32[]{:S(2)}) copy-start(f32[24,4096]{1,0:T(8,128)} %mom_ref.1) | copy-start | bytes 1179652
  49.3 4.2 %collective-permute-start.17 = (bf16[24,1024]{1,0:T(8,128)(2,1)S(1)}, bf16[24,1024]{1,0:T(8,128)(2,1)S(1)}, u32[]{:S(2)}, u32[]{:S(2)}) collective-permute-start(bf16[24,1024]{1,0:T(8,128)(2,1)S(1)} %stepped_slice.1.refs_0_), channel_id=1, source_target_pairs={{0,8},{8,0},{16,24},{24,16},{1,9},{9,1},{17,25},{25,17},{2,10},{10... | collective-permute-start | bytes 147464 | tf_op jit(solution)/shard_map/ppermute | solution.py:426
  50.9 4.1 %collective-permute-start.18 = (bf16[24,1024]{1,0:T(8,128)(2,1)S(1)}, bf16[24,1024]{1,0:T(8,128)(2,1)S(1)}, u32[]{:S(2)}, u32[]{:S(2)}) collective-permute-start(bf16[24,1024]{1,0:T(8,128)(2,1)S(1)} %stepped_slice.1.refs_0_), channel_id=1, source_target_pairs={{0,16},{8,24},{16,0},{24,8},{1,17},{9,25},{17,1},{25,9},{2,18},{10... | collective-permute-start | bytes 147464 | tf_op jit(solution)/shard_map/ppermute | solution.py:426
  51.4 5.0 %collective-permute-start.19 = (bf16[24,1024]{1,0:T(8,128)(2,1)S(1)}, bf16[24,1024]{1,0:T(8,128)(2,1)S(1)}, u32[]{:S(2)}, u32[]{:S(2)}) collective-permute-start(bf16[24,1024]{1,0:T(8,128)(2,1)S(1)} %stepped_slice.1.refs_0_), channel_id=1, source_target_pairs={{0,24},{8,16},{16,8},{24,0},{1,25},{9,17},{17,9},{25,1},{2,26},{10... | collective-permute-start | bytes 147464 | tf_op jit(solution)/shard_map/ppermute | solution.py:426
